TPU v7x, 128 devices: a whole 4x4x4 slice. The times are simulated.
128 devices in a mesh: seq: 32 (over x_hi, z, y), head: 4 (over x_lo, core).
Axes of the slice: x: 4 (x_hi: 2, x_lo: 2; x = x_hi * 2 + x_lo), y: 4, z: 4, core: 2. Of those that a mesh axis runs over, the one named last changes fastest.
Arguments:
- queries: bfloat16 [65536, 4096], P('seq', 'head'), may hold values from -112 to 112
- key_rows: bfloat16 [65536, 4096], P('seq', 'head'), may hold values from -5 to 5
- value_rows: bfloat16 [65536, 4096], P('seq', 'head'), may hold values from -5 to 5
Outputs:
- attended: bfloat16 [65536, 4096], P(('seq', 'head'))
All inputs are finite; a program needn't handle non-finite values.
Results may differ from a plain program's by a relative error of at most 0.0055.
Values may be sent and summed in bfloat16 or wider, within the bound.
No kernel may reach another device: no remote copies, remote signals or barrier semaphores. Data moves between devices by JAX's collectives and lax.ppermute only.
A program may use at most 256 MiB of HBM per device.

v0:
```python
import math

import jax
import jax.numpy as jnp
from jax import lax
from jax.sharding import PartitionSpec as P

HD = 128
BLK = 256
P1 = 8
P2 = 64
R1 = 12


def passed_along(block, axis, distance):
    devices = range(lax.axis_size(axis))
    route = [(i - distance, i) for i in devices if i - distance in devices]
    return lax.ppermute(block, axis, route)


def pooled_mean(rows_in, factor):
    return jnp.mean(
        rows_in.astype(jnp.float32).reshape(-1, factor, rows_in.shape[1]), axis=1
    ).astype(jnp.bfloat16)


def absorb(running, query_tile, key_part, val_part, allowed, bias):
    maxima, totals, weighted = running
    score_scale = 1.0 / math.sqrt(query_tile.shape[2])
    logits = (
        jnp.einsum("qhd,khd->hqk", query_tile, key_part, preferred_element_type=jnp.float32)
        * score_scale
        + bias
    )
    logits = jnp.where(allowed[None], logits, -jnp.inf)
    newest = jnp.maximum(maxima, jnp.max(logits, axis=2))
    weights = jnp.exp(logits - newest[:, :, None])
    factor = jnp.exp(maxima - newest)
    totals = totals * factor + jnp.sum(weights, axis=2)
    product = jnp.einsum(
        "hqk,khd->qhd", weights.astype(jnp.bfloat16), val_part, preferred_element_type=jnp.float32
    )
    weighted = weighted * factor.T[:, :, None] + product
    return (newest, totals, weighted)


def shards(queries, key_rows, value_rows):
    tok_rows, feat_width = queries.shape
    head_count = feat_width // HD
    offset = lax.axis_index("seq") * tok_rows
    tile_size = min(tok_rows, 512)
    tile_count = tok_rows // tile_size
    reach_ranges = (R1 * BLK + tok_rows - 1) // tok_rows
    key_one = pooled_mean(key_rows, P1)
    val_one = pooled_mean(value_rows, P1)
    key_two = pooled_mean(key_rows, P2)
    val_two = pooled_mean(value_rows, P2)
    prev_keys, prev_vals = passed_along(
        (key_rows[tok_rows - BLK :], value_rows[tok_rows - BLK :]), "seq", 1
    )
    distant = []
    for hops in range(reach_ranges, 0, -1):
        distant.append(passed_along((key_one, val_one), "seq", hops))
    near_keys = jnp.concatenate([prev_keys, key_rows])
    near_vals = jnp.concatenate([prev_vals, value_rows])
    mid_keys = jnp.concatenate([pair[0] for pair in distant] + [key_one]).reshape(
        -1, head_count, HD
    )
    mid_vals = jnp.concatenate([pair[1] for pair in distant] + [val_one]).reshape(
        -1, head_count, HD
    )
    mid_first = offset // P1 - reach_ranges * tok_rows // P1
    mid_groups = mid_first + jnp.arange(mid_keys.shape[0], dtype=jnp.int32)
    mid_block = mid_groups * P1 // BLK

    def row_positions(start, count):
        return offset + start + jnp.arange(count, dtype=jnp.int32)

    def near_state(query_tile, start):
        count = query_tile.shape[0]
        query_pos = row_positions(start, count)
        query_block = query_pos // BLK
        running = (
            jnp.full((head_count, count), -jnp.inf, jnp.float32),
            jnp.zeros((head_count, count), jnp.float32),
            jnp.zeros((count, head_count, HD), jnp.float32),
        )
        near_k = lax.dynamic_slice_in_dim(near_keys, start, count + BLK, 0).reshape(
            -1, head_count, HD
        )
        near_v = lax.dynamic_slice_in_dim(near_vals, start, count + BLK, 0).reshape(
            -1, head_count, HD
        )
        near_pos = offset - BLK + start + jnp.arange(count + BLK, dtype=jnp.int32)
        near_ok = (
            (near_pos[None, :] <= query_pos[:, None])
            & (near_pos[None, :] >= 0)
            & (near_pos[None, :] // BLK >= query_block[:, None] - 1)
        )
        running = absorb(running, query_tile, near_k, near_v, near_ok, 0.0)
        mid_ok = (
            (mid_groups[None, :] >= 0)
            & (mid_block[None, :] >= query_block[:, None] - R1)
            & (mid_block[None, :] <= query_block[:, None] - 2)
        )
        return absorb(running, query_tile, mid_keys, mid_vals, mid_ok, math.log(P1))

    def far_state(running, query_tile, start, key_part, val_part):
        query_block = row_positions(start, query_tile.shape[0]) // BLK
        group_idx = jnp.arange(key_part.shape[0], dtype=jnp.int32)
        allowed = (group_idx * P2 // BLK)[None, :] < query_block[:, None] - R1
        return absorb(running, query_tile, key_part, val_part, allowed, math.log(P2))

    query_tiles = queries.reshape(tile_count, tile_size, head_count, HD)
    tile_starts = jnp.arange(tile_count, dtype=jnp.int32) * tile_size
    states = lax.map(lambda packet: near_state(packet[0], packet[1]), (query_tiles, tile_starts))
    all_keys, all_vals = (
        lax.all_gather(key_two, "seq", axis=0, tiled=True),
        lax.all_gather(val_two, "seq", axis=0, tiled=True),
    )
    far_k = all_keys.reshape(-1, head_count, HD)
    far_v = all_vals.reshape(-1, head_count, HD)
    states = lax.map(
        lambda packet: far_state(
            (packet[0], packet[1], packet[2]), packet[3], packet[4], far_k, far_v
        ),
        (states[0], states[1], states[2], query_tiles, tile_starts),
    )
    maxima, totals, weighted = states
    combined = (
        (weighted / jnp.swapaxes(totals, 1, 2)[:, :, :, None])
        .astype(jnp.bfloat16)
        .reshape(tok_rows, feat_width)
    )
    return lax.all_to_all(combined, "head", split_axis=0, concat_axis=1, tiled=True)


def solution(mesh):
    return jax.shard_map(
        shards,
        mesh=mesh,
        in_specs=(P("seq", "head"), P("seq", "head"), P("seq", "head")),
        out_specs=P(("seq", "head"), None),
        check_vma=False,
    )
```

profile of v0, /device:TPU:5, one launch (start us, length us, event | category | flops | bytes accessed | tf_op | source)
XLA Modules:
  0.0 424.3 jit_solution(14135688017410194678)
XLA Ops:
  10.5 5.6 %bitcast_reduce_fusion.3 = f32[256,1024]{1,0:T(8,128)S(1)} fusion(bf16[2048,1024]{1,0:T(8,128)(2,1)} %param.8), kind=kLoop, calls=%fused_computation.137 | loop fusion | flops 3932160 | bytes 5242880 | tf_op jit(solution)/shard_map/reduce_sum | solution.py:22
  29.9 4.8 %collective-permute-start.4 = (bf16[256,1024]{1,0:T(8,128)(2,1)S(1)}, bf16[256,1024]{1,0:T(8,128)(2,1)}, u32[]{:S(2)}, u32[]{:S(2)}) collective-permute-start(bf16[256,1024]{1,0:T(8,128)(2,1)S(1)} %multiply_convert_fusion), channel_id=1, source_target_pairs={{0,8},{4,12},{8,16},{12,20},{16,24},{20,28},{24,32},{28,36},{32,40... | collective-permute-start | bytes 1572872 | tf_op jit(solution)/shard_map/ppermute | solution.py:18
  34.8 6.5 %copy.27 = bf16[2048,1024]{0,1:T(8,128)(2,1)} copy(bf16[2048,1024]{1,0:T(8,128)(2,1)} %param.8) | data formatting | bytes 8388608 | tf_op args[1]
  50.2 6.6 %copy.30 = bf16[2048,1024]{0,1:T(8,128)(2,1)} copy(bf16[2048,1024]{1,0:T(8,128)(2,1)} %param.9) | data formatting | bytes 8388608 | tf_op args[2]
  77.8 15.2 %collective-permute-done = bf16[256,1024]{0,1:T(8,128)(2,1)} collective-permute-done((bf16[256,1024]{0,1:T(8,128)(2,1)}, bf16[256,1024]{0,1:T(8,128)(2,1)}, u32[]{:S(2)}, u32[]{:S(2)}) %collective-permute-start) | collective-permute-done | bytes 524320 | tf_op jit(solution)/shard_map/ppermute | solution.py:18
  97.7 6.5 %collective-permute-done.3 = bf16[256,1024]{0,1:T(8,128)(2,1)} collective-permute-done((bf16[256,1024]{0,1:T(8,128)(2,1)}, bf16[256,1024]{0,1:T(8,128)(2,1)}, u32[]{:S(2)}, u32[]{:S(2)}) %collective-permute-start.3) | collective-permute-done | bytes 524320 | tf_op jit(solution)/shard_map/ppermute | solution.py:18
  112.3 124.3 %while.35 = (s32[]{:T(128)}, f32[4,8,512]{2,1,0:T(8,128)S(1)}, f32[4,8,512]{2,1,0:T(8,128)S(1)}, f32[4,512,8,128]{1,3,2,0:T(8,128)}, s32[4]{0:T(128)S(1)}, /*ind...) while((s32[]{:T(128)}, f32[4,8,512]{2,1,0:T(8,128)S(1)}, ...), condition=%wide.region_7.8_spmd.clone.clone, body=%wide.region_2.7_spmd.clone.clone.sunk | while | flops 3304666368 | bytes 116806952 | solution.py:116
  137.0 6.4 %bitcast_dynamic-update-slice_fusion.2 = f32[4,512,8,128]{1,3,2,0:T(8,128)} fusion(f32[4,512,8,128]{1,3,2,0:T(8,128)} %get-tuple-element.794, s32[]{:T(128)S(6)} %copy.68, f32[8,128,512]{2,1,0:T(8,128)S(1)} %fusion.134, bf16[768,8,128]{2,0,1:T(8,128)(2,1)S(1)} %get-tuple-element.818, f32[8,512,768]{2,1,0:T(8,128)S(1)} %get-tuple-element.761, ...), kind=kOutput, calls=%fused_computation.64.clone.1 | convolution fusion | flops 822607872 | bytes 18792452 | tf_op jit(solution)/shard_map/while/body/eval_jaxpr/hqk,khd->qhd/dot_general | solution.py:40
  168.1 6.5 %bitcast_dynamic-update-slice_fusion.2 = f32[4,512,8,128]{1,3,2,0:T(8,128)} fusion(f32[4,512,8,128]{1,3,2,0:T(8,128)} %get-tuple-element.794, s32[]{:T(128)S(6)} %copy.68, f32[8,128,512]{2,1,0:T(8,128)S(1)} %fusion.134, bf16[768,8,128]{2,0,1:T(8,128)(2,1)S(1)} %get-tuple-element.818, f32[8,512,768]{2,1,0:T(8,128)S(1)} %get-tuple-element.761, ...), kind=kOutput, calls=%fused_computation.64.clone.1 | convolution fusion | flops 822607872 | bytes 18792452 | tf_op jit(solution)/shard_map/while/body/eval_jaxpr/hqk,khd->qhd/dot_general | solution.py:40
  199.2 6.5 %bitcast_dynamic-update-slice_fusion.2 = f32[4,512,8,128]{1,3,2,0:T(8,128)} fusion(f32[4,512,8,128]{1,3,2,0:T(8,128)} %get-tuple-element.794, s32[]{:T(128)S(6)} %copy.68, f32[8,128,512]{2,1,0:T(8,128)S(1)} %fusion.134, bf16[768,8,128]{2,0,1:T(8,128)(2,1)S(1)} %get-tuple-element.818, f32[8,512,768]{2,1,0:T(8,128)S(1)} %get-tuple-element.761, ...), kind=kOutput, calls=%fused_computation.64.clone.1 | convolution fusion | flops 822607872 | bytes 18792452 | tf_op jit(solution)/shard_map/while/body/eval_jaxpr/hqk,khd->qhd/dot_general | solution.py:40
  230.1 6.5 %bitcast_dynamic-update-slice_fusion.2 = f32[4,512,8,128]{1,3,2,0:T(8,128)} fusion(f32[4,512,8,128]{1,3,2,0:T(8,128)} %get-tuple-element.794, s32[]{:T(128)S(6)} %copy.68, f32[8,128,512]{2,1,0:T(8,128)S(1)} %fusion.134, bf16[768,8,128]{2,0,1:T(8,128)(2,1)S(1)} %get-tuple-element.818, f32[8,512,768]{2,1,0:T(8,128)S(1)} %get-tuple-element.761, ...), kind=kOutput, calls=%fused_computation.64.clone.1 | convolution fusion | flops 822607872 | bytes 18792452 | tf_op jit(solution)/shard_map/while/body/eval_jaxpr/hqk,khd->qhd/dot_general | solution.py:40
  251.7 102.2 %while.34 = (s32[]{:T(128)}, f32[4,8,512]{2,1,0:T(8,128)S(1)}, f32[4,512,8,128]{1,3,2,0:T(8,128)}, f32[4,8,512]{2,1,0:T(8,128)S(1)}, f32[4,8,512]{2,1,0:T(8,128)...) while((s32[]{:T(128)}, f32[4,8,512]{2,1,0:T(8,128)S(1)}, ...), condition=%wide.region_13.14_spmd, body=%wide.region_10.13_spmd.sunk | while | flops 2207818240 | bytes 95662312 | solution.py:123
  257.1 5.5 %fusion.116 = (f32[8,512]{1,0:T(8,128)S(1)}, f32[8,512,1024]{2,1,0:T(8,128)S(1)}) fusion(pred[512,1024]{1,0:T(8,128)(4,1)S(1)} %broadcast_compare_fusion.2, bf16[1024,8,128]{2,0,1:T(8,128)(2,1)} %get-tuple-element.855, bf16[4,512,8,128]{3,1,2,0:T(8,128)(2,1)} %get-tuple-element.854, s32[]{:T(128)S(6)} %copy.79), kind=kOutput, calls=%fused_computation.6.clone.1 | convolution fusion | flops 1090514944 | bytes 20463620 | tf_op jit(solution)/shard_map/while/body/eval_jaxpr/qhd,khd->hqk/dot_general | solution.py:31
  262.6 6.3 %fusion.120 = f32[1,512,8,128]{3,1,2,0:T(8,128)} fusion(f32[1,512,8,128]{3,1,2,0:T(8,128)S(1)} %copy-done, bf16[1024,8,128]{2,0,1:T(8,128)(2,1)S(1)} %copy-done.4, f32[8,512,1024]{2,1,0:T(8,128)S(1)} %get-tuple-element.742, f32[8,512]{1,0:T(8,128)S(1)} %get-tuple-element.744, pred[512,1024]{1,0:T(8,128)(4,1)S(1)} %broadcast_compare_fusion.2, ...), kind=kOutput, calls=%fused_computation.10.clone.1 | convolution fusion | flops 1095761920 | bytes 23625728 | tf_op jit(solution)/shard_map/while/body/eval_jaxpr/hqk,khd->qhd/dot_general | solution.py:40
  269.0 4.7 %fusion.118 = f32[8,512]{1,0:T(8,128)S(1)} fusion(f32[8,512,1024]{2,1,0:T(8,128)S(1)} %get-tuple-element.742, f32[8,512]{1,0:T(8,128)S(1)} %get-tuple-element.744, pred[512,1024]{1,0:T(8,128)(4,1)S(1)} %broadcast_compare_fusion.2), kind=kLoop, calls=%fused_computation.5.clone.1 | loop fusion | flops 20967424 | bytes 17334272 | tf_op jit(solution)/shard_map/while/body/eval_jaxpr/reduce_sum | solution.py:39
  282.6 5.5 %fusion.116 = (f32[8,512]{1,0:T(8,128)S(1)}, f32[8,512,1024]{2,1,0:T(8,128)S(1)}) fusion(pred[512,1024]{1,0:T(8,128)(4,1)S(1)} %broadcast_compare_fusion.2, bf16[1024,8,128]{2,0,1:T(8,128)(2,1)} %get-tuple-element.855, bf16[4,512,8,128]{3,1,2,0:T(8,128)(2,1)} %get-tuple-element.854, s32[]{:T(128)S(6)} %copy.79), kind=kOutput, calls=%fused_computation.6.clone.1 | convolution fusion | flops 1090514944 | bytes 20463620 | tf_op jit(solution)/shard_map/while/body/eval_jaxpr/qhd,khd->hqk/dot_general | solution.py:31
  288.2 6.3 %fusion.120 = f32[1,512,8,128]{3,1,2,0:T(8,128)} fusion(f32[1,512,8,128]{3,1,2,0:T(8,128)S(1)} %copy-done, bf16[1024,8,128]{2,0,1:T(8,128)(2,1)S(1)} %copy-done.4, f32[8,512,1024]{2,1,0:T(8,128)S(1)} %get-tuple-element.742, f32[8,512]{1,0:T(8,128)S(1)} %get-tuple-element.744, pred[512,1024]{1,0:T(8,128)(4,1)S(1)} %broadcast_compare_fusion.2, ...), kind=kOutput, calls=%fused_computation.10.clone.1 | convolution fusion | flops 1095761920 | bytes 23625728 | tf_op jit(solution)/shard_map/while/body/eval_jaxpr/hqk,khd->qhd/dot_general | solution.py:40
  294.5 4.7 %fusion.118 = f32[8,512]{1,0:T(8,128)S(1)} fusion(f32[8,512,1024]{2,1,0:T(8,128)S(1)} %get-tuple-element.742, f32[8,512]{1,0:T(8,128)S(1)} %get-tuple-element.744, pred[512,1024]{1,0:T(8,128)(4,1)S(1)} %broadcast_compare_fusion.2), kind=kLoop, calls=%fused_computation.5.clone.1 | loop fusion | flops 20967424 | bytes 17334272 | tf_op jit(solution)/shard_map/while/body/eval_jaxpr/reduce_sum | solution.py:39
  308.2 5.5 %fusion.116 = (f32[8,512]{1,0:T(8,128)S(1)}, f32[8,512,1024]{2,1,0:T(8,128)S(1)}) fusion(pred[512,1024]{1,0:T(8,128)(4,1)S(1)} %broadcast_compare_fusion.2, bf16[1024,8,128]{2,0,1:T(8,128)(2,1)} %get-tuple-element.855, bf16[4,512,8,128]{3,1,2,0:T(8,128)(2,1)} %get-tuple-element.854, s32[]{:T(128)S(6)} %copy.79), kind=kOutput, calls=%fused_computation.6.clone.1 | convolution fusion | flops 1090514944 | bytes 20463620 | tf_op jit(solution)/shard_map/while/body/eval_jaxpr/qhd,khd->hqk/dot_general | solution.py:31
  313.7 6.3 %fusion.120 = f32[1,512,8,128]{3,1,2,0:T(8,128)} fusion(f32[1,512,8,128]{3,1,2,0:T(8,128)S(1)} %copy-done, bf16[1024,8,128]{2,0,1:T(8,128)(2,1)S(1)} %copy-done.4, f32[8,512,1024]{2,1,0:T(8,128)S(1)} %get-tuple-element.742, f32[8,512]{1,0:T(8,128)S(1)} %get-tuple-element.744, pred[512,1024]{1,0:T(8,128)(4,1)S(1)} %broadcast_compare_fusion.2, ...), kind=kOutput, calls=%fused_computation.10.clone.1 | convolution fusion | flops 1095761920 | bytes 23625728 | tf_op jit(solution)/shard_map/while/body/eval_jaxpr/hqk,khd->qhd/dot_general | solution.py:40
  333.7 5.5 %fusion.116 = (f32[8,512]{1,0:T(8,128)S(1)}, f32[8,512,1024]{2,1,0:T(8,128)S(1)}) fusion(pred[512,1024]{1,0:T(8,128)(4,1)S(1)} %broadcast_compare_fusion.2, bf16[1024,8,128]{2,0,1:T(8,128)(2,1)} %get-tuple-element.855, bf16[4,512,8,128]{3,1,2,0:T(8,128)(2,1)} %get-tuple-element.854, s32[]{:T(128)S(6)} %copy.79), kind=kOutput, calls=%fused_computation.6.clone.1 | convolution fusion | flops 1090514944 | bytes 20463620 | tf_op jit(solution)/shard_map/while/body/eval_jaxpr/qhd,khd->hqk/dot_general | solution.py:31
  339.2 6.3 %fusion.120 = f32[1,512,8,128]{3,1,2,0:T(8,128)} fusion(f32[1,512,8,128]{3,1,2,0:T(8,128)S(1)} %copy-done, bf16[1024,8,128]{2,0,1:T(8,128)(2,1)S(1)} %copy-done.4, f32[8,512,1024]{2,1,0:T(8,128)S(1)} %get-tuple-element.742, f32[8,512]{1,0:T(8,128)S(1)} %get-tuple-element.744, pred[512,1024]{1,0:T(8,128)(4,1)S(1)} %broadcast_compare_fusion.2, ...), kind=kOutput, calls=%fused_computation.10.clone.1 | convolution fusion | flops 1095761920 | bytes 23625728 | tf_op jit(solution)/shard_map/while/body/eval_jaxpr/hqk,khd->qhd/dot_general | solution.py:40
  358.6 52.2 %all_to_all.19 = bf16[4,512,1024]{1,2,0:T(8,128)(2,1)} all-to-all(bf16[4,512,1024]{1,2,0:T(8,128)(2,1)S(1)} %bitcast.181), channel_id=1, replica_groups=mesh['seq'=32,'head'=4] {'head'}, dimensions={0} | all-to-all | bytes 8388608 | tf_op jit(solution)/shard_map/all_to_all | solution.py:135
  410.7 6.3 %copy.44 = bf16[512,4096]{1,0:T(8,128)(2,1)} copy(bf16[512,4096]{0,1:T(8,128)(2,1)} %bitcast.182) | data formatting | bytes 8388608 | tf_op jit(solution)/shard_map/all_to_all | solution.py:135
  (191 shorter events, 208.1 us)
Async XLA Ops:
  6.5 230.0 %all-gather.3.cloned.1.call-start = ((), (), s32[]{:S(2)}) async-start(), calls=%async_computation.1 | async-start | bytes 2162688 | tf_op jit(solution)/shard_map/all_gather | solution.py:118
  10.5 231.4 %all-gather.5.cloned.1.call-start = ((), (), s32[]{:S(2)}) async-start(), calls=%async_computation.2 | async-start | bytes 2162688 | tf_op jit(solution)/shard_map/all_gather | solution.py:119
  10.5 13.5 %copy-start.1 = (bf16[2048,1024]{1,0:T(8,128)(2,1)S(1)}, bf16[2048,1024]{1,0:T(8,128)(2,1)}, u32[]{:S(2)}) copy-start(bf16[2048,1024]{1,0:T(8,128)(2,1)} %param.9) | copy-start | bytes 12582916
  16.3 48.6 %collective-permute-start.2 = (bf16[256,1024]{1,0:T(8,128)(2,1)S(1)}, bf16[256,1024]{1,0:T(8,128)(2,1)S(1)}, u32[]{:S(2)}, u32[]{:S(2)}) collective-permute-start(bf16[256,1024]{1,0:T(8,128)(2,1)S(1)} %multiply_convert_fusion.1), channel_id=1, source_target_pairs={{0,4},{4,8},{8,12},{12,16},{16,20},{20,24},{24,28},{28,32},{32,36}... | collective-permute-start | bytes 1572872 | tf_op jit(solution)/shard_map/ppermute | solution.py:18
  19.5 47.3 %collective-permute-start.1 = (bf16[256,1024]{1,0:T(8,128)(2,1)S(1)}, bf16[256,1024]{1,0:T(8,128)(2,1)}, u32[]{:S(2)}, u32[]{:S(2)}) collective-permute-start(bf16[256,1024]{1,0:T(8,128)(2,1)S(1)} %multiply_convert_fusion.1), channel_id=1, source_target_pairs={{0,8},{4,12},{8,16},{12,20},{16,24},{20,28},{24,32},{28,36},{32,40... | collective-permute-start | bytes 1572872 | tf_op jit(solution)/shard_map/ppermute | solution.py:18
  27.3 15.8 %copy-start.5 = (bf16[256,1024]{1,0:T(8,128)(2,1)}, bf16[256,1024]{1,0:T(8,128)(2,1)S(1)}, u32[]{:S(2)}) copy-start(bf16[256,1024]{1,0:T(8,128)(2,1)S(1)} %multiply_convert_fusion) | copy-start | bytes 1572868
  27.3 43.2 %collective-permute-start.5 = (bf16[256,1024]{1,0:T(8,128)(2,1)S(1)}, bf16[256,1024]{1,0:T(8,128)(2,1)}, u32[]{:S(2)}, u32[]{:S(2)}) collective-permute-start(bf16[256,1024]{1,0:T(8,128)(2,1)S(1)} %multiply_convert_fusion), channel_id=1, source_target_pairs={{0,4},{4,8},{8,12},{12,16},{16,20},{20,24},{24,28},{28,32},{32,36}... | collective-permute-start | bytes 1572872 | tf_op jit(solution)/shard_map/ppermute | solution.py:18
  29.9 40.5 %collective-permute-start.4 = (bf16[256,1024]{1,0:T(8,128)(2,1)S(1)}, bf16[256,1024]{1,0:T(8,128)(2,1)}, u32[]{:S(2)}, u32[]{:S(2)}) collective-permute-start(bf16[256,1024]{1,0:T(8,128)(2,1)S(1)} %multiply_convert_fusion), channel_id=1, source_target_pairs={{0,8},{4,12},{8,16},{12,20},{16,24},{20,28},{24,32},{28,36},{32,40... | collective-permute-start | bytes 1572872 | tf_op jit(solution)/shard_map/ppermute | solution.py:18
  43.2 49.8 %collective-permute-start = (bf16[256,1024]{0,1:T(8,128)(2,1)}, bf16[256,1024]{0,1:T(8,128)(2,1)}, u32[]{:S(2)}, u32[]{:S(2)}) collective-permute-start(bf16[256,1024]{0,1:T(8,128)(2,1)} %slice.8), channel_id=1, source_target_pairs={{0,4},{4,8},{8,12},{12,16},{16,20},{20,24},{24,28},{28,32},{32,36}... | collective-permute-start | bytes 1572872 | tf_op jit(solution)/shard_map/ppermute | solution.py:18
  64.8 39.4 %collective-permute-start.3 = (bf16[256,1024]{0,1:T(8,128)(2,1)}, bf16[256,1024]{0,1:T(8,128)(2,1)}, u32[]{:S(2)}, u32[]{:S(2)}) collective-permute-start(bf16[256,1024]{0,1:T(8,128)(2,1)} %slice.9), channel_id=1, source_target_pairs={{0,4},{4,8},{8,12},{12,16},{16,20},{20,24},{24,28},{28,32},{32,36}... | collective-permute-start | bytes 1572872 | tf_op jit(solution)/shard_map/ppermute | solution.py:18
  77.8 26.4 %copy-start.3 = (bf16[2048,1024]{0,1:T(8,128)(2,1)S(1)}, bf16[2048,1024]{0,1:T(8,128)(2,1)}, u32[]{:S(2)}) copy-start(bf16[2048,1024]{0,1:T(8,128)(2,1)} %copy.30) | copy-start | bytes 12582916
  107.8 4.4 %copy-start.6 = (bf16[768,8,128]{2,0,1:T(8,128)(2,1)S(1)}, bf16[768,8,128]{2,0,1:T(8,128)(2,1)}, u32[]{:S(2)}) copy-start(bf16[768,8,128]{2,0,1:T(8,128)(2,1)} %copy.34) | copy-start | bytes 4718596
  116.2 5.0 %copy-start.2 = (bf16[4,512,8,128]{3,1,2,0:T(8,128)(2,1)S(1)}, bf16[4,512,8,128]{3,1,2,0:T(8,128)(2,1)}, u32[]{:S(2)}) copy-start(bf16[4,512,8,128]{3,1,2,0:T(8,128)(2,1)} %get-tuple-element.814) | copy-start | bytes 12582916 | tf_op jit(solution)/shard_map/while
  147.3 5.0 %copy-start.2 = (bf16[4,512,8,128]{3,1,2,0:T(8,128)(2,1)S(1)}, bf16[4,512,8,128]{3,1,2,0:T(8,128)(2,1)}, u32[]{:S(2)}) copy-start(bf16[4,512,8,128]{3,1,2,0:T(8,128)(2,1)} %get-tuple-element.814) | copy-start | bytes 12582916 | tf_op jit(solution)/shard_map/while
  178.4 5.0 %copy-start.2 = (bf16[4,512,8,128]{3,1,2,0:T(8,128)(2,1)S(1)}, bf16[4,512,8,128]{3,1,2,0:T(8,128)(2,1)}, u32[]{:S(2)}) copy-start(bf16[4,512,8,128]{3,1,2,0:T(8,128)(2,1)} %get-tuple-element.814) | copy-start | bytes 12582916 | tf_op jit(solution)/shard_map/while
  209.4 4.8 %copy-start.2 = (bf16[4,512,8,128]{3,1,2,0:T(8,128)(2,1)S(1)}, bf16[4,512,8,128]{3,1,2,0:T(8,128)(2,1)}, u32[]{:S(2)}) copy-start(bf16[4,512,8,128]{3,1,2,0:T(8,128)(2,1)} %get-tuple-element.814) | copy-start | bytes 12582916 | tf_op jit(solution)/shard_map/while
  257.1 5.5 %copy-start = (f32[1,512,8,128]{3,1,2,0:T(8,128)S(1)}, f32[1,512,8,128]{3,1,2,0:T(8,128)}, u32[]{:S(2)}) copy-start(f32[1,512,8,128]{3,1,2,0:T(8,128)} %copy.57) | copy-start | bytes 6291460 | tf_op jit(solution)/shard_map/while
  257.1 5.5 %copy-start.4 = (bf16[1024,8,128]{2,0,1:T(8,128)(2,1)S(1)}, bf16[1024,8,128]{2,0,1:T(8,128)(2,1)}, u32[]{:S(2)}) copy-start(bf16[1024,8,128]{2,0,1:T(8,128)(2,1)} %get-tuple-element.857) | copy-start | bytes 6291460 | tf_op jit(solution)/shard_map/while
  282.6 5.5 %copy-start = (f32[1,512,8,128]{3,1,2,0:T(8,128)S(1)}, f32[1,512,8,128]{3,1,2,0:T(8,128)}, u32[]{:S(2)}) copy-start(f32[1,512,8,128]{3,1,2,0:T(8,128)} %copy.57) | copy-start | bytes 6291460 | tf_op jit(solution)/shard_map/while
  282.6 5.5 %copy-start.4 = (bf16[1024,8,128]{2,0,1:T(8,128)(2,1)S(1)}, bf16[1024,8,128]{2,0,1:T(8,128)(2,1)}, u32[]{:S(2)}) copy-start(bf16[1024,8,128]{2,0,1:T(8,128)(2,1)} %get-tuple-element.857) | copy-start | bytes 6291460 | tf_op jit(solution)/shard_map/while
  308.2 5.5 %copy-start = (f32[1,512,8,128]{3,1,2,0:T(8,128)S(1)}, f32[1,512,8,128]{3,1,2,0:T(8,128)}, u32[]{:S(2)}) copy-start(f32[1,512,8,128]{3,1,2,0:T(8,128)} %copy.57) | copy-start | bytes 6291460 | tf_op jit(solution)/shard_map/while
  308.2 5.5 %copy-start.4 = (bf16[1024,8,128]{2,0,1:T(8,128)(2,1)S(1)}, bf16[1024,8,128]{2,0,1:T(8,128)(2,1)}, u32[]{:S(2)}) copy-start(bf16[1024,8,128]{2,0,1:T(8,128)(2,1)} %get-tuple-element.857) | copy-start | bytes 6291460 | tf_op jit(solution)/shard_map/while
  333.7 5.5 %copy-start = (f32[1,512,8,128]{3,1,2,0:T(8,128)S(1)}, f32[1,512,8,128]{3,1,2,0:T(8,128)}, u32[]{:S(2)}) copy-start(f32[1,512,8,128]{3,1,2,0:T(8,128)} %copy.57) | copy-start | bytes 6291460 | tf_op jit(solution)/shard_map/while
  333.7 5.5 %copy-start.4 = (bf16[1024,8,128]{2,0,1:T(8,128)(2,1)S(1)}, bf16[1024,8,128]{2,0,1:T(8,128)(2,1)}, u32[]{:S(2)}) copy-start(bf16[1024,8,128]{2,0,1:T(8,128)(2,1)} %get-tuple-element.857) | copy-start | bytes 6291460 | tf_op jit(solution)/shard_map/while
Sparse Core Ops, SparseCore 0:
  10.6 127.0 all-gather.2
  140.7 68.9 all-gather.4
where the time goes:
time: 433 us; the launch traced here: 424 us
  matrix products  109 us (25%)
  local copies, waits for them, and re-layouts  104 us (24%)
  other arithmetic  84.1 us (19%)
  blocking collectives  52.2 us (12%)
  waiting for transfers between devices  24.3 us (6%)
  starting transfers between devices  20.3 us (5%)
  loops' own time  16 us (4%)
  between operations  14.1 us (3%)
    dot_general x12, matrix products, absorb(): jnp.einsum('hqk,khd->qhd', weights.astype(jnp.bfloat16), val_part, prefer...  65.8 us
    all_to_all x1, blocking collectives, shards(): lax.all_to_all(combined, 'head', split_axis=0, concat_axis=1, tiled=True)  52.2 us
    reduce_sum x12, other arithmetic, absorb(): totals = totals * factor + jnp.sum(weights, axis=2)  45.8 us
    dot_general x12, matrix products, absorb(): jnp.einsum('qhd,khd->hqk', query_tile, key_part, preferred_element_type=j...  43.4 us
    ppermute x6, waiting for transfers between devices, passed_along(): return lax.ppermute(block, axis, route)  24.2 us
    unnamed x14, local copies, waits for them, and re-layouts  22.8 us
    ppermute x6, starting transfers between devices, passed_along(): return lax.ppermute(block, axis, route)  20.2 us
    reduce_sum x4, other arithmetic, pooled_mean(): jnp.mean(rows_in.astype(jnp.float32).reshape(-1, factor, rows_in.shape[1]...  15.4 us
  transfers between devices with their start and end apart: 8, of which 3 were waited for; matrix products, arithmetic and copies ran while one was open for 41% of the time, Pallas kernels for 0%

commit v1 on v0

v1 whole, which is shorter than its diff:
```python
import math

import jax
import jax.numpy as jnp
from jax import lax
from jax.experimental import pallas as pl
from jax.experimental.pallas import tpu as pltpu
from jax.sharding import PartitionSpec as P

HD = 128
BLK = 256
P1 = 8
P2 = 64
R1 = 12
SEQ = 32
TOK = 2048
NEG = -1e30
MIDB = BLK // P1
FARD = TOK // P2
FARS = SEQ * FARD
MIDS = 18 * MIDB
EXP_SCALE = math.log2(math.e) / math.sqrt(HD)
CHUNKS = 2
WIDTH = 1024 // CHUNKS
VMEM_LIMIT = 56 * 1024 * 1024


def seq_route(move):
    route = []
    for s in range(SEQ):
        x, z, y = s // 16, (s // 4) % 4, s % 4
        x, z, y = move(x, z, y)
        route.append((s, x * 16 + (z % 4) * 4 + y % 4))
    return route


X_ROUTE = seq_route(lambda x, z, y: (1 - x, z, y))
Y_ROUTES = [seq_route(lambda x, z, y, d=d: (x, z, y + d)) for d in (1, 3, 2)]
Z_ROUTES = [seq_route(lambda x, z, y, d=d: (x, z + d, y)) for d in (1, 3, 2)]
OFFSETS = (0, 3, 1, 2)


def shift_route(distance):
    return [(i - distance, i) for i in range(distance, SEQ)]


def pool_kernel(k_ref, v_ref, b1_ref, b2_ref, f_ref):
    rows = lax.broadcasted_iota(jnp.int32, (40, BLK), 0)
    cols = lax.broadcasted_iota(jnp.int32, (40, BLK), 1)
    mid = jnp.where(cols // P1 == rows, 1.0 / P1, 0.0)
    far = jnp.where(cols // P2 == rows - 32, 1.0 / P2, 0.0)
    mean = jnp.where(rows < 32, mid, far).astype(jnp.bfloat16)
    for i, ref in enumerate((k_ref, v_ref)):
        b1_ref[i * 256 : i * 256 + 256, :] = ref[TOK - BLK :, :]
        fars = []
        for b in range(TOK // BLK):
            pooled = jnp.dot(
                mean, ref[b * BLK : (b + 1) * BLK, :], preferred_element_type=jnp.float32
            )
            mids = pooled[:32].astype(jnp.bfloat16)
            at = 512 + (b // 4) * 256 + i * 128 + (b % 4) * 32
            b1_ref[at : at + 32, :] = mids
            if b >= 4:
                at = i * 128 + (b % 4) * 32
                b2_ref[at : at + 32, :] = mids
            fars.append(pooled[32:36])
        f_ref[i * 32 : i * 32 + 32, :] = jnp.concatenate(fars, axis=0).astype(jnp.bfloat16)


def pool(chunk, key_rows, value_rows):
    step = 256
    first = chunk * WIDTH // step
    return pl.pallas_call(
        pool_kernel,
        grid=(WIDTH // step,),
        in_specs=[pl.BlockSpec((TOK, step), lambda i: (0, first + i))] * 2,
        out_specs=[
            pl.BlockSpec((1024, step), lambda i: (0, i)),
            pl.BlockSpec((256, step), lambda i: (0, i)),
            pl.BlockSpec((64, step), lambda i: (0, i)),
        ],
        out_shape=[
            jax.ShapeDtypeStruct((1024, WIDTH), jnp.bfloat16),
            jax.ShapeDtypeStruct((256, WIDTH), jnp.bfloat16),
            jax.ShapeDtypeStruct((64, WIDTH), jnp.bfloat16),
        ],
        compiler_params=pltpu.CompilerParams(vmem_limit_bytes=VMEM_LIMIT),
        cost_estimate=pl.CostEstimate(
            flops=2 * 2 * TOK * WIDTH * 40, bytes_accessed=2 * TOK * WIDTH * 3, transcendentals=0
        ),
        name="pool",
    )(key_rows, value_rows)


def dot_nt(a, b):
    return lax.dot_general(a, b, (((1,), (1,)), ((), ())), preferred_element_type=jnp.float32)


def attend_kernel(
    info_ref, q_ref, k_ref, v_ref, own_ref, r1_ref, r2_ref, h0_ref, h1_ref, h2_ref, h3_ref,
    oa_ref, ob_ref, kn, vn, km, vm, kf, vf, ke, ve, sa, sb,
):
    s = info_ref[0]
    half = info_ref[1]
    flip = info_ref[2]
    x, z, y = s // 16, (s // 4) % 4, s % 4
    bf = jnp.bfloat16

    @pl.when(pl.program_id(0) == 0)
    def _():
        vn[:, HD:] = jnp.ones((1280, HD), bf)
        vm[:, HD:] = jnp.full((MIDS, HD), P1, bf)
        ve[:, HD:] = jnp.full((32, HD), P2, bf)

    @pl.when(half == 0)
    def _():
        kn[:256, :] = r1_ref[0:256, :]
        vn[:256, :HD] = r1_ref[256:512, :]
        kn[256:, :] = k_ref[:1024, :]
        vn[256:, :HD] = v_ref[:1024, :]

    @pl.when(half == 1)
    def _():
        kn[...] = k_ref[768:, :]
        vn[:, :HD] = v_ref[768:, :]

    eight = jnp.full((128, HD), P1, bf)
    km[0:128, :] = r2_ref[0:128, :]
    vm[0:128, :HD] = r2_ref[128:256, :] * eight
    km[128:256, :] = r1_ref[512:640, :]
    vm[128:256, :HD] = r1_ref[640:768, :] * eight
    km[256:384, :] = r1_ref[768:896, :]
    vm[256:384, :HD] = r1_ref[896:1024, :] * eight
    km[384:512, :] = own_ref[512:640, :]
    vm[384:512, :HD] = own_ref[640:768, :] * eight
    km[512:576, :] = own_ref[768:832, :]
    vm[512:576, :HD] = own_ref[896:960, :] * eight[:64]

    scale = jnp.full((32, HD), P2, bf)
    for zi, h_ref in enumerate((h0_ref, h1_ref, h2_ref, h3_ref)):
        for yi in range(4):
            for xi in range(2):
                src = (x ^ xi) * 16 + ((z + OFFSETS[zi]) % 4) * 4 + (y + OFFSETS[yi]) % 4
                to = pl.multiple_of(src * 32, 32)
                at = yi * 128 + xi * 64
                kf[pl.ds(to, 32), :] = h_ref[at : at + 32, :]
                vf[pl.ds(to, 32), :HD] = h_ref[at + 32 : at + 64, :] * scale
    vf[:, HD:] = jnp.full((FARS, HD), P2, bf)
    edge = 2 * s - 3
    for i in range(2):
        at = pl.multiple_of(jnp.maximum(edge + i, 0) * 16, 16)
        ke[i * 16 : i * 16 + 16, :] = kf[pl.ds(at, 16), :]
        ve[i * 16 : i * 16 + 16, :HD] = vf[pl.ds(at, 16), :HD]
    filler = jnp.broadcast_to(kf[0:1, :], (16, HD))

    def fill(u, carry):
        at = pl.multiple_of(u * 16, 16)
        kf[pl.ds(at, 16), :] = filler
        vf[pl.ds(at, 16), :] = jnp.zeros((16, 2 * HD), bf)
        return carry

    lax.fori_loop(jnp.maximum(edge, 0), FARS // 16, fill, 0)

    def block_of(n):
        local = 2 * ((n // 2) ^ flip) + n % 2
        return local, half * 4 + local

    def scores(n, s_ref, with_far):
        local, j = block_of(n)
        q = q_ref[pl.ds(pl.multiple_of(local * BLK, BLK), BLK), :]
        start = pl.multiple_of(local * BLK, BLK)
        sn = dot_nt(q, kn[pl.ds(start, BLK), :])
        sn = sn + jnp.where((s == 0) & (j == 0), NEG, 0.0)
        s_ref[:, 0:256] = sn
        top = jnp.maximum(sn[:, :128], sn[:, 128:])
        rows = lax.broadcasted_iota(jnp.int32, (BLK, BLK), 0)
        cols = lax.broadcasted_iota(jnp.int32, (BLK, BLK), 1)
        sd = dot_nt(q, kn[pl.ds(start + BLK, BLK), :])
        sd = jnp.where(cols <= rows, sd, NEG)
        s_ref[:, 256:512] = sd
        top = jnp.maximum(top, jnp.maximum(sd[:, :128], sd[:, 128:]))
        mids = jnp.concatenate(
            [km[pl.ds(pl.multiple_of(j * MIDB, MIDB), 352), :], ke[...]], axis=0
        )
        col = lax.broadcasted_iota(jnp.int32, (1, 384), 1)
        low = MIDB * (R1 - 8 * s - j)
        e = col - 352
        ok = jnp.where(e < 0, col - low, jnp.minimum(e - (48 - 32 * s), 4 * j - 1 - e)) >= 0
        sm = dot_nt(q, mids) + jnp.where(ok, 0.0, NEG)
        s_ref[:, 512:896] = sm
        for i in range(3):
            top = jnp.maximum(top, sm[:, i * 128 : i * 128 + 128])
        if with_far:
            for i in range(4):
                sf = dot_nt(q, kf[i * 256 : i * 256 + 256, :])
                s_ref[:, 896 + i * 256 : 1152 + i * 256] = sf
                top = jnp.maximum(top, jnp.maximum(sf[:, :128], sf[:, 128:]))
        return jnp.max(top, axis=1, keepdims=True)

    def finish(n, s_ref, top, o_ref, with_far):
        local, j = block_of(n)
        start = pl.multiple_of(local * BLK, BLK)

        def weights(a, b):
            return jnp.exp2((s_ref[:, a:b] - top) * EXP_SCALE).astype(bf)

        acc = jnp.dot(
            weights(0, 512), vn[pl.ds(start, 512), :], preferred_element_type=jnp.float32
        )
        mids = jnp.concatenate(
            [vm[pl.ds(pl.multiple_of(j * MIDB, MIDB), 352), :], ve[...]], axis=0
        )
        acc = acc + jnp.dot(weights(512, 896), mids, preferred_element_type=jnp.float32)
        if with_far:
            for i in range(4):
                acc = acc + jnp.dot(
                    weights(896 + i * 256, 1152 + i * 256),
                    vf[i * 256 : i * 256 + 256, :],
                    preferred_element_type=jnp.float32,
                )
        at = (n % 2) * BLK
        o_ref[at : at + BLK, :] = (acc[:, :HD] / acc[:, HD:]).astype(bf)

    def blocks(with_far):
        slots = (sa, sb)
        top = scores(0, sa, with_far)
        for n in range(4):
            later = scores(n + 1, slots[(n + 1) % 2], with_far) if n < 3 else None
            finish(n, slots[n % 2], top, (oa_ref, ob_ref)[n // 2], with_far)
            top = later

    @pl.when(edge > 0)
    def _():
        blocks(True)

    @pl.when(edge <= 0)
    def _():
        blocks(False)


def attend(chunk, info, queries, key_rows, value_rows, own, r1, r2, fars):
    heads = WIDTH // HD
    first = chunk * heads
    whole = lambda rows: pl.BlockSpec((rows, HD), lambda h, info: (0, h))
    return pl.pallas_call(
        attend_kernel,
        grid_spec=pltpu.PrefetchScalarGridSpec(
            num_scalar_prefetch=1,
            grid=(heads,),
            in_specs=[
                pl.BlockSpec((1024, HD), lambda h, info: (info[1], first + h)),
                pl.BlockSpec((TOK, HD), lambda h, info: (0, first + h)),
                pl.BlockSpec((TOK, HD), lambda h, info: (0, first + h)),
                whole(1024),
                whole(1024),
                whole(256),
                whole(512),
                whole(512),
                whole(512),
                whole(512),
            ],
            out_specs=[whole(512), whole(512)],
            scratch_shapes=[
                pltpu.VMEM((1280, HD), jnp.bfloat16),
                pltpu.VMEM((1280, 2 * HD), jnp.bfloat16),
                pltpu.VMEM((MIDS, HD), jnp.bfloat16),
                pltpu.VMEM((MIDS, 2 * HD), jnp.bfloat16),
                pltpu.VMEM((FARS, HD), jnp.bfloat16),
                pltpu.VMEM((FARS, 2 * HD), jnp.bfloat16),
                pltpu.VMEM((32, HD), jnp.bfloat16),
                pltpu.VMEM((32, 2 * HD), jnp.bfloat16),
                pltpu.VMEM((BLK, 1920), jnp.float32),
                pltpu.VMEM((BLK, 1920), jnp.float32),
            ],
        ),
        out_shape=[jax.ShapeDtypeStruct((512, WIDTH), jnp.bfloat16)] * 2,
        compiler_params=pltpu.CompilerParams(vmem_limit_bytes=VMEM_LIMIT),
        cost_estimate=pl.CostEstimate(
            flops=heads * 4 * BLK * 1920 * HD * 8,
            bytes_accessed=heads * HD * 2 * 10000,
            transcendentals=heads * 4 * BLK * 1920,
        ),
        name="attend",
    )(info, queries, key_rows, value_rows, own, r1, r2, *fars)


def place_kernel(me_ref, *refs):
    pieces, out_ref = refs[:-1], refs[-1]
    me = me_ref[0]
    for i, piece in enumerate(pieces):
        chunk, k = i // 4, i % 4
        at = pl.multiple_of((me ^ k) * 1024 + chunk * WIDTH, WIDTH)
        out_ref[:, pl.ds(at, WIDTH)] = piece[...]


def place(me, pieces):
    step = 64
    return pl.pallas_call(
        place_kernel,
        grid_spec=pltpu.PrefetchScalarGridSpec(
            num_scalar_prefetch=1,
            grid=(512 // step,),
            in_specs=[pl.BlockSpec((step, WIDTH), lambda i, me: (i, 0))] * len(pieces),
            out_specs=pl.BlockSpec((step, 4096), lambda i, me: (i, 0)),
        ),
        out_shape=jax.ShapeDtypeStruct((512, 4096), jnp.bfloat16),
        cost_estimate=pl.CostEstimate(flops=0, bytes_accessed=8 * 1024 * 1024, transcendentals=0),
        name="place",
    )(me, *pieces)


def swap_heads(piece, k):
    return lax.ppermute(piece, "head", [(i, i ^ k) for i in range(4)])


def shards(queries, key_rows, value_rows):
    s = lax.axis_index("seq").astype(jnp.int32)
    me = lax.axis_index("head").astype(jnp.int32)
    pair, flip = me // 2, me % 2
    over = lambda value, route: lax.ppermute(value, "seq", route)
    ready = []
    for c in range(CHUNKS):
        b1, b2, f0 = pool(c, key_rows, value_rows)
        f1 = over(f0, X_ROUTE)
        r1 = over(b1, shift_route(1))
        g0 = jnp.concatenate([f0, f1])
        gs = [over(g0, route) for route in Y_ROUTES]
        r2 = over(b2, shift_route(2))
        h0 = jnp.concatenate([g0] + gs)
        hs = [over(h0, route) for route in Z_ROUTES]
        ready.append((b1, r1, r2, [h0] + hs))
    pieces = {}
    for c in range(CHUNKS):
        parts = (queries, key_rows, value_rows) + ready[c]
        out2, out3 = attend(c, jnp.stack([s, 1 - pair, flip]), *parts)
        pieces[c, 2], pieces[c, 3] = swap_heads(out2, 2), swap_heads(out3, 3)
        out0, out1 = attend(c, jnp.stack([s, pair, flip]), *parts)
        pieces[c, 0], pieces[c, 1] = out0, swap_heads(out1, 1)
    return place(
        me.reshape(1), [pieces[c, k] for c in range(CHUNKS) for k in range(4)]
    )


def solution(mesh):
    return jax.shard_map(
        shards,
        mesh=mesh,
        in_specs=(P("seq", "head"), P("seq", "head"), P("seq", "head")),
        out_specs=P(("seq", "head"), None),
        check_vma=False,
    )
```

time: 433 us -> 194 us (0.45); the launches traced: 424 us -> 194 us
  matrix products: 109 us -> 0 us
  local copies, waits for them, and re-layouts: 104 us -> 4.36 us
  other arithmetic: 84.1 us -> 0.67 us
  Pallas kernels: 0 us -> 74.7 us
  waiting for transfers between devices: 24.3 us -> 80.1 us
  blocking collectives: 52.2 us -> 0 us
  loops' own time: 16 us -> 0 us
  between operations: 14.1 us -> 0.38 us
  starting transfers between devices: 20.3 us -> 33.4 us
    dot_general x24 -> x0, matrix products: 109 us -> none  [the longest x12 65.8 us: absorb(): jnp.einsum('hqk,khd->qhd', weights.astype(jnp.bfloat16), val_part, prefer...]
    pallas_call x0 -> x7, Pallas kernels: none -> 74.7 us  [the longest x4 61.1 us: attend(): pl.pallas_call(attend_kernel, grid_spec=pltpu.PrefetchScalarGridSpec(num_...]
    reduce_sum x16 -> x0, other arithmetic: 61.1 us -> none  [the longest x12 45.8 us: absorb(): totals = totals * factor + jnp.sum(weights, axis=2)]
    ppermute x6 -> x24, waiting for transfers between devices: 24.2 us -> 80.1 us  [the longest x18 71.8 us: shards(): over = lambda value, route: lax.ppermute(value, 'seq', route)]
    all_to_all x1 -> x0, blocking collectives: 52.2 us -> none  [shards(): lax.all_to_all(combined, 'head', split_axis=0, concat_axis=1, tiled=True)]
    dynamic_slice x20 -> x0, local copies, waits for them, and re-layouts: 35.3 us -> none  [the longest x4 15.3 us: near_state(): lax.dynamic_slice_in_dim(near_vals, start, count + BLK, 0)]
    unnamed x14 -> x46, local copies, waits for them, and re-layouts: 22.8 us -> 4.32 us
    another operation x2 -> x0, loops' own time: 16 us -> none  [the longest x1 13.2 us: shards(): lax.map(lambda packet: near_state(packet[0], packet[1]), (query_tiles, ti...]
  transfers between devices with their start and end apart: 8 -> 24, of which waited for: 3 -> 6; matrix products, arithmetic and copies ran while one was open for 41% -> 1% of each run, Pallas kernels for 0% -> 33%
where the time goes in v1:
time: 194 us
  waiting for transfers between devices  80.1 us (41%)
  Pallas kernels  74.7 us (39%)
  starting transfers between devices  33.4 us (17%)
  local copies, waits for them, and re-layouts  4.36 us (2%)
    ppermute x18, waiting for transfers between devices, shards(): over = lambda value, route: lax.ppermute(value, 'seq', route)  71.8 us
    pallas_call x4, Pallas kernels, attend(): pl.pallas_call(attend_kernel, grid_spec=pltpu.PrefetchScalarGridSpec(num_...  61.1 us
    ppermute x18, starting transfers between devices, shards(): over = lambda value, route: lax.ppermute(value, 'seq', route)  26.6 us
    ppermute x6, waiting for transfers between devices, swap_heads(): return lax.ppermute(piece, 'head', [(i, i ^ k) for i in range(4)])  8.27 us
    pallas_call x2, Pallas kernels, pool(): pl.pallas_call(pool_kernel, grid=(WIDTH // step,), in_specs=[pl.BlockSpec...  7.12 us
    ppermute x6, starting transfers between devices, swap_heads(): return lax.ppermute(piece, 'head', [(i, i ^ k) for i in range(4)])  6.85 us
    pallas_call x1, Pallas kernels, place(): pl.pallas_call(place_kernel, grid_spec=pltpu.PrefetchScalarGridSpec(num_s...  6.47 us
    unnamed x46, local copies, waits for them, and re-layouts  4.32 us
  transfers between devices with their start and end apart: 24, of which 6 were waited for; matrix products, arithmetic and copies ran while one was open for 1% of the time, Pallas kernels for 33%

profile of v1, /device:TPU:5, one launch (start us, length us, event | category | flops | bytes accessed | tf_op | source)
XLA Modules:
  0.0 193.6 jit_solution(8816834318313433267)
XLA Ops:
  0.0 3.6 %pool.3 = (bf16[1024,512]{1,0:T(8,128)(2,1)}, bf16[256,512]{1,0:T(8,128)(2,1)}, bf16[64,512]{1,0:T(8,128)(2,1)}) custom-call(bf16[2048,1024]{1,0:T(8,128)(2,1)} %k_ref.11, bf16[2048,1024]{1,0:T(8,128)(2,1)} %v_ref.11), custom_call_target="tpu_custom_call" | custom-call | flops 167772160 | bytes 6291456 | tf_op jit(solution)/shard_map/pool/pallas_call | solution.py:73
  3.6 3.5 %collective-permute-start.12 = (bf16[1024,512]{1,0:T(8,128)(2,1)}, bf16[1024,512]{1,0:T(8,128)(2,1)S(1)}, u32[]{:S(2)}, u32[]{:S(2)}) collective-permute-start(bf16[1024,512]{1,0:T(8,128)(2,1)} %get-tuple-element.26.own_ref), channel_id=1, source_target_pairs={{0,4},{4,8},{8,12},{12,16},{16,20},{20,24},{24,28},{28,32},{32,36}... | collective-permute-start | bytes 3145736 | tf_op jit(solution)/shard_map/ppermute | solution.py:320
  7.1 3.6 %pool.2 = (bf16[1024,512]{1,0:T(8,128)(2,1)}, bf16[256,512]{1,0:T(8,128)(2,1)}, bf16[64,512]{1,0:T(8,128)(2,1)}) custom-call(bf16[2048,1024]{1,0:T(8,128)(2,1)} %k_ref.11, bf16[2048,1024]{1,0:T(8,128)(2,1)} %v_ref.11), custom_call_target="tpu_custom_call" | custom-call | flops 167772160 | bytes 6291456 | tf_op jit(solution)/shard_map/pool/pallas_call | solution.py:73
  10.7 2.8 %collective-permute-start.2 = (bf16[64,512]{1,0:T(8,128)(2,1)}, bf16[64,512]{1,0:T(8,128)(2,1)S(1)}, u32[]{:S(2)}, u32[]{:S(2)}) collective-permute-start(bf16[64,512]{1,0:T(8,128)(2,1)} %get-tuple-element.21), channel_id=1, source_target_pairs={{0,64},{4,68},{8,72},{12,76},{16,80},{20,84},{24,88},{28,92},{32,9... | collective-permute-start | bytes 196616 | tf_op jit(solution)/shard_map/ppermute | solution.py:320
  13.5 1.3 collective-permute-start.15
  15.7 1.5 collective-permute-start.16
  17.2 1.3 collective-permute-start.17
  19.3 15.9 %collective-permute-done.15 = bf16[128,512]{1,0:T(8,128)(2,1)S(1)} collective-permute-done((bf16[128,512]{1,0:T(8,128)(2,1)S(1)}, bf16[128,512]{1,0:T(8,128)(2,1)S(1)}, u32[]{:S(2)}, u32[]{:S(2)}) %collective-permute-start.15) | collective-permute-done | bytes 131104 | tf_op jit(solution)/shard_map/ppermute | solution.py:320
  35.3 2.5 %collective-permute-done.17 = bf16[128,512]{1,0:T(8,128)(2,1)S(1)} collective-permute-done((bf16[128,512]{1,0:T(8,128)(2,1)S(1)}, bf16[128,512]{1,0:T(8,128)(2,1)S(1)}, u32[]{:S(2)}, u32[]{:S(2)}) %collective-permute-start.17) | collective-permute-done | bytes 131104 | tf_op jit(solution)/shard_map/ppermute | solution.py:320
  37.8 1.4 collective-permute-start.18
  39.2 4.9 %collective-permute-start.19 = (bf16[512,512]{1,0:T(8,128)(2,1)S(1)}, bf16[512,512]{1,0:T(8,128)(2,1)}, u32[]{:S(2)}, u32[]{:S(2)}) collective-permute-start(bf16[512,512]{1,0:T(8,128)(2,1)S(1)} %constant_dynamic-update-slice_fusion.9.h0_ref), channel_id=1, source_target_pairs={{0,48},{4,52},{8,56},{12,60},{16,0},{20,4},{24,8},{28,12},{32,16},... | collective-permute-start | bytes 1572872 | tf_op jit(solution)/shard_map/ppermute | solution.py:320
  46.0 4.7 %collective-permute-done.5 = bf16[128,512]{1,0:T(8,128)(2,1)S(1)} collective-permute-done((bf16[128,512]{1,0:T(8,128)(2,1)S(1)}, bf16[128,512]{1,0:T(8,128)(2,1)S(1)}, u32[]{:S(2)}, u32[]{:S(2)}) %collective-permute-start.5) | collective-permute-done | bytes 131104 | tf_op jit(solution)/shard_map/ppermute | solution.py:320
  50.6 2.2 %collective-permute-start.13 = (bf16[256,512]{1,0:T(8,128)(2,1)S(1)}, bf16[256,512]{1,0:T(8,128)(2,1)S(1)}, u32[]{:S(2)}, u32[]{:S(2)}) collective-permute-start(bf16[256,512]{1,0:T(8,128)(2,1)S(1)} %copy-done.17), channel_id=1, source_target_pairs={{0,8},{4,12},{8,16},{12,20},{16,24},{20,28},{24,32},{28,36},{32,40... | collective-permute-start | bytes 786440 | tf_op jit(solution)/shard_map/ppermute | solution.py:320
  52.9 11.2 %collective-permute-done.13.r2_ref = bf16[256,512]{1,0:T(8,128)(2,1)S(1)} collective-permute-done((bf16[256,512]{1,0:T(8,128)(2,1)S(1)}, bf16[256,512]{1,0:T(8,128)(2,1)S(1)}, u32[]{:S(2)}, u32[]{:S(2)}) %collective-permute-start.13) | collective-permute-done | bytes 262176 | tf_op jit(solution)/shard_map/ppermute | solution.py:320
  64.1 3.3 %collective-permute-start = (bf16[1024,512]{1,0:T(8,128)(2,1)}, bf16[1024,512]{1,0:T(8,128)(2,1)S(1)}, u32[]{:S(2)}, u32[]{:S(2)}) collective-permute-start(bf16[1024,512]{1,0:T(8,128)(2,1)} %get-tuple-element.19.own_ref), channel_id=1, source_target_pairs={{0,4},{4,8},{8,12},{12,16},{16,20},{20,24},{24,28},{28,32},{32,36}... | collective-permute-start | bytes 3145736 | tf_op jit(solution)/shard_map/ppermute | solution.py:320
  67.5 1.9 collective-permute-start.1
  69.5 37.5 %collective-permute-done.20.h3_ref = bf16[512,512]{1,0:T(8,128)(2,1)} collective-permute-done((bf16[512,512]{1,0:T(8,128)(2,1)S(1)}, bf16[512,512]{1,0:T(8,128)(2,1)}, u32[]{:S(2)}, u32[]{:S(2)}) %collective-permute-start.20) | collective-permute-done | bytes 524320 | tf_op jit(solution)/shard_map/ppermute | solution.py:320
  108.0 15.2 %attend.7 = (bf16[512,512]{1,0:T(8,128)(2,1)}, bf16[512,512]{1,0:T(8,128)(2,1)}) custom-call(s32[3]{0:T(128)} %get-tuple-element.42.info_ref, bf16[2048,1024]{1,0:T(8,128)(2,1)} %q_ref.7, bf16[2048,1024]{1,0:T(8,128)(2,1)} %k_ref.11, bf16[2048,1024]{1,0:T(8,128)(2,1)} %v_ref.11, bf16[1024,512]{1,0:T(8,128)(2,1)} %get-tuple-element.26.own_ref, ...), custom_call_target="tpu_custom_call" | custom-call | flops 8053063680 | bytes 10240000 | tf_op jit(solution)/shard_map/attend/pallas_call | solution.py:245
  123.3 15.4 %attend.6 = (bf16[512,512]{1,0:T(8,128)(2,1)}, bf16[512,512]{1,0:T(8,128)(2,1)}) custom-call(s32[3]{0:T(128)} %get-tuple-element.41.info_ref, bf16[2048,1024]{1,0:T(8,128)(2,1)} %q_ref.7, bf16[2048,1024]{1,0:T(8,128)(2,1)} %k_ref.11, bf16[2048,1024]{1,0:T(8,128)(2,1)} %v_ref.11, bf16[1024,512]{1,0:T(8,128)(2,1)} %get-tuple-element.26.own_ref, ...), custom_call_target="tpu_custom_call" | custom-call | flops 8053063680 | bytes 10240000 | tf_op jit(solution)/shard_map/attend/pallas_call | solution.py:245
  138.8 4.3 %collective-permute-start.23 = (bf16[512,512]{1,0:T(8,128)(2,1)S(1)}, bf16[512,512]{1,0:T(8,128)(2,1)S(1)}, u32[]{:S(2)}, u32[]{:S(2)}) collective-permute-start(bf16[512,512]{1,0:T(8,128)(2,1)S(1)} %copy-done.14), channel_id=1, source_target_pairs={{0,3},{1,2},{2,1},{3,0},{4,7},{5,6},{6,5},{7,4},{8,11},{9,10},{10,... | collective-permute-start | bytes 1572872 | tf_op jit(solution)/shard_map/ppermute | solution.py:313
  145.4 15.2 %attend.5 = (bf16[512,512]{1,0:T(8,128)(2,1)}, bf16[512,512]{1,0:T(8,128)(2,1)}) custom-call(s32[3]{0:T(128)} %get-tuple-element.42.info_ref, bf16[2048,1024]{1,0:T(8,128)(2,1)} %q_ref.7, bf16[2048,1024]{1,0:T(8,128)(2,1)} %k_ref.11, bf16[2048,1024]{1,0:T(8,128)(2,1)} %v_ref.11, bf16[1024,512]{1,0:T(8,128)(2,1)} %get-tuple-element.19.own_ref, ...), custom_call_target="tpu_custom_call" | custom-call | flops 8053063680 | bytes 10240000 | tf_op jit(solution)/shard_map/attend/pallas_call | solution.py:245
  162.3 15.2 %attend.4 = (bf16[512,512]{1,0:T(8,128)(2,1)}, bf16[512,512]{1,0:T(8,128)(2,1)}) custom-call(s32[3]{0:T(128)} %get-tuple-element.41.info_ref, bf16[2048,1024]{1,0:T(8,128)(2,1)} %q_ref.7, bf16[2048,1024]{1,0:T(8,128)(2,1)} %k_ref.11, bf16[2048,1024]{1,0:T(8,128)(2,1)} %v_ref.11, bf16[1024,512]{1,0:T(8,128)(2,1)} %get-tuple-element.19.own_ref, ...), custom_call_target="tpu_custom_call" | custom-call | flops 8053063680 | bytes 10240000 | tf_op jit(solution)/shard_map/attend/pallas_call | solution.py:245
  177.9 8.3 %collective-permute-done.11.refs_3_ = bf16[512,512]{1,0:T(8,128)(2,1)S(1)} collective-permute-done((bf16[512,512]{1,0:T(8,128)(2,1)}, bf16[512,512]{1,0:T(8,128)(2,1)S(1)}, u32[]{:S(2)}, u32[]{:S(2)}) %collective-permute-start.11) | collective-permute-done | bytes 524320 | tf_op jit(solution)/shard_map/ppermute | solution.py:313
  187.1 6.5 %place.1 = bf16[512,4096]{1,0:T(8,128)(2,1)} custom-call(s32[1]{0:T(128)} %bitcast.me_ref, bf16[512,512]{1,0:T(8,128)(2,1)} %get-tuple-element.22.refs_0_, bf16[512,512]{1,0:T(8,128)(2,1)} %copy-done.5, bf16[512,512]{1,0:T(8,128)(2,1)} %copy-done.3, bf16[512,512]{1,0:T(8,128)(2,1)} %copy-done.4, bf16[512,512]{1,0:T(8,128)(2,1)} %get-tuple-element.29.refs_4_, ...), custom_call_target="tpu_custom_call" | custom-call | bytes 8388608 | tf_op jit(solution)/shard_map/place/pallas_call | solution.py:298
  (82 shorter events, 10.0 us)
Async XLA Ops:
  3.6 9.9 %collective-permute-start.14 = (bf16[64,512]{1,0:T(8,128)(2,1)}, bf16[64,512]{1,0:T(8,128)(2,1)S(1)}, u32[]{:S(2)}, u32[]{:S(2)}) collective-permute-start(bf16[64,512]{1,0:T(8,128)(2,1)} %get-tuple-element.28), channel_id=1, source_target_pairs={{0,64},{4,68},{8,72},{12,76},{16,80},{20,84},{24,88},{28,92},{32,9... | collective-permute-start | bytes 196616 | tf_op jit(solution)/shard_map/ppermute | solution.py:320
  3.6 103.5 %collective-permute-start.12 = (bf16[1024,512]{1,0:T(8,128)(2,1)}, bf16[1024,512]{1,0:T(8,128)(2,1)S(1)}, u32[]{:S(2)}, u32[]{:S(2)}) collective-permute-start(bf16[1024,512]{1,0:T(8,128)(2,1)} %get-tuple-element.26.own_ref), channel_id=1, source_target_pairs={{0,4},{4,8},{8,12},{12,16},{16,20},{20,24},{24,28},{28,32},{32,36}... | collective-permute-start | bytes 3145736 | tf_op jit(solution)/shard_map/ppermute | solution.py:320
  10.7 7.9 %collective-permute-start.2 = (bf16[64,512]{1,0:T(8,128)(2,1)}, bf16[64,512]{1,0:T(8,128)(2,1)S(1)}, u32[]{:S(2)}, u32[]{:S(2)}) collective-permute-start(bf16[64,512]{1,0:T(8,128)(2,1)} %get-tuple-element.21), channel_id=1, source_target_pairs={{0,64},{4,68},{8,72},{12,76},{16,80},{20,84},{24,88},{28,92},{32,9... | collective-permute-start | bytes 196616 | tf_op jit(solution)/shard_map/ppermute | solution.py:320
  13.5 21.7 %collective-permute-start.15 = (bf16[128,512]{1,0:T(8,128)(2,1)S(1)}, bf16[128,512]{1,0:T(8,128)(2,1)S(1)}, u32[]{:S(2)}, u32[]{:S(2)}) collective-permute-start(bf16[128,512]{1,0:T(8,128)(2,1)S(1)} %get-tuple-element.33), channel_id=1, source_target_pairs={{0,4},{4,8},{8,12},{12,0},{16,20},{20,24},{24,28},{28,16},{32,36},... | collective-permute-start | bytes 393224 | tf_op jit(solution)/shard_map/ppermute | solution.py:320
  15.7 19.6 %collective-permute-start.16 = (bf16[128,512]{1,0:T(8,128)(2,1)S(1)}, bf16[128,512]{1,0:T(8,128)(2,1)S(1)}, u32[]{:S(2)}, u32[]{:S(2)}) collective-permute-start(bf16[128,512]{1,0:T(8,128)(2,1)S(1)} %get-tuple-element.33), channel_id=1, source_target_pairs={{0,12},{4,0},{8,4},{12,8},{16,28},{20,16},{24,20},{28,24},{32,44},... | collective-permute-start | bytes 393224 | tf_op jit(solution)/shard_map/ppermute | solution.py:320
  17.2 20.6 %collective-permute-start.17 = (bf16[128,512]{1,0:T(8,128)(2,1)S(1)}, bf16[128,512]{1,0:T(8,128)(2,1)S(1)}, u32[]{:S(2)}, u32[]{:S(2)}) collective-permute-start(bf16[128,512]{1,0:T(8,128)(2,1)S(1)} %get-tuple-element.33), channel_id=1, source_target_pairs={{0,8},{4,12},{8,0},{12,4},{16,24},{20,28},{24,16},{28,20},{32,40},... | collective-permute-start | bytes 393224 | tf_op jit(solution)/shard_map/ppermute | solution.py:320
  18.6 25.6 %collective-permute-start.3 = (bf16[128,512]{1,0:T(8,128)(2,1)S(1)}, bf16[128,512]{1,0:T(8,128)(2,1)S(1)}, u32[]{:S(2)}, u32[]{:S(2)}) collective-permute-start(bf16[128,512]{1,0:T(8,128)(2,1)S(1)} %get-tuple-element.37), channel_id=1, source_target_pairs={{0,4},{4,8},{8,12},{12,0},{16,20},{20,24},{24,28},{28,16},{32,36},... | collective-permute-start | bytes 393224 | tf_op jit(solution)/shard_map/ppermute | solution.py:320
  35.2 10.1 %collective-permute-start.4 = (bf16[128,512]{1,0:T(8,128)(2,1)S(1)}, bf16[128,512]{1,0:T(8,128)(2,1)S(1)}, u32[]{:S(2)}, u32[]{:S(2)}) collective-permute-start(bf16[128,512]{1,0:T(8,128)(2,1)S(1)} %get-tuple-element.37), channel_id=1, source_target_pairs={{0,12},{4,0},{8,4},{12,8},{16,28},{20,16},{24,20},{28,24},{32,44},... | collective-permute-start | bytes 393224 | tf_op jit(solution)/shard_map/ppermute | solution.py:320
  37.8 29.6 %collective-permute-start.18 = (bf16[512,512]{1,0:T(8,128)(2,1)S(1)}, bf16[512,512]{1,0:T(8,128)(2,1)S(1)}, u32[]{:S(2)}, u32[]{:S(2)}) collective-permute-start(bf16[512,512]{1,0:T(8,128)(2,1)S(1)} %constant_dynamic-update-slice_fusion.9.h0_ref), channel_id=1, source_target_pairs={{0,16},{4,20},{8,24},{12,28},{16,32},{20,36},{24,40},{28,44},{32,4... | collective-permute-start | bytes 1572872 | tf_op jit(solution)/shard_map/ppermute | solution.py:320
  39.2 30.2 %collective-permute-start.19 = (bf16[512,512]{1,0:T(8,128)(2,1)S(1)}, bf16[512,512]{1,0:T(8,128)(2,1)}, u32[]{:S(2)}, u32[]{:S(2)}) collective-permute-start(bf16[512,512]{1,0:T(8,128)(2,1)S(1)} %constant_dynamic-update-slice_fusion.9.h0_ref), channel_id=1, source_target_pairs={{0,48},{4,52},{8,56},{12,60},{16,0},{20,4},{24,8},{28,12},{32,16},... | collective-permute-start | bytes 1572872 | tf_op jit(solution)/shard_map/ppermute | solution.py:320
  44.2 62.9 %collective-permute-start.20 = (bf16[512,512]{1,0:T(8,128)(2,1)S(1)}, bf16[512,512]{1,0:T(8,128)(2,1)}, u32[]{:S(2)}, u32[]{:S(2)}) collective-permute-start(bf16[512,512]{1,0:T(8,128)(2,1)S(1)} %constant_dynamic-update-slice_fusion.9.h0_ref), channel_id=1, source_target_pairs={{0,32},{4,36},{8,40},{12,44},{16,48},{20,52},{24,56},{28,60},{32,0... | collective-permute-start | bytes 1572872 | tf_op jit(solution)/shard_map/ppermute | solution.py:320
  45.3 5.3 %collective-permute-start.5 = (bf16[128,512]{1,0:T(8,128)(2,1)S(1)}, bf16[128,512]{1,0:T(8,128)(2,1)S(1)}, u32[]{:S(2)}, u32[]{:S(2)}) collective-permute-start(bf16[128,512]{1,0:T(8,128)(2,1)S(1)} %get-tuple-element.37), channel_id=1, source_target_pairs={{0,8},{4,12},{8,0},{12,4},{16,24},{20,28},{24,16},{28,20},{32,40},... | collective-permute-start | bytes 393224 | tf_op jit(solution)/shard_map/ppermute | solution.py:320
  50.6 13.5 %collective-permute-start.13 = (bf16[256,512]{1,0:T(8,128)(2,1)S(1)}, bf16[256,512]{1,0:T(8,128)(2,1)S(1)}, u32[]{:S(2)}, u32[]{:S(2)}) collective-permute-start(bf16[256,512]{1,0:T(8,128)(2,1)S(1)} %copy-done.17), channel_id=1, source_target_pairs={{0,8},{4,12},{8,16},{12,20},{16,24},{20,28},{24,32},{28,36},{32,40... | collective-permute-start | bytes 786440 | tf_op jit(solution)/shard_map/ppermute | solution.py:320
  64.1 79.5 %collective-permute-start = (bf16[1024,512]{1,0:T(8,128)(2,1)}, bf16[1024,512]{1,0:T(8,128)(2,1)S(1)}, u32[]{:S(2)}, u32[]{:S(2)}) collective-permute-start(bf16[1024,512]{1,0:T(8,128)(2,1)} %get-tuple-element.19.own_ref), channel_id=1, source_target_pairs={{0,4},{4,8},{8,12},{12,16},{16,20},{20,24},{24,28},{28,32},{32,36}... | collective-permute-start | bytes 3145736 | tf_op jit(solution)/shard_map/ppermute | solution.py:320
  67.5 71.2 %collective-permute-start.1 = (bf16[256,512]{1,0:T(8,128)(2,1)}, bf16[256,512]{1,0:T(8,128)(2,1)S(1)}, u32[]{:S(2)}, u32[]{:S(2)}) collective-permute-start(bf16[256,512]{1,0:T(8,128)(2,1)} %get-tuple-element.20), channel_id=1, source_target_pairs={{0,8},{4,12},{8,16},{12,20},{16,24},{20,28},{24,32},{28,36},{32,40... | collective-permute-start | bytes 786440 | tf_op jit(solution)/shard_map/ppermute | solution.py:320
  69.4 69.4 %collective-permute-start.6 = (bf16[512,512]{1,0:T(8,128)(2,1)S(1)}, bf16[512,512]{1,0:T(8,128)(2,1)S(1)}, u32[]{:S(2)}, u32[]{:S(2)}) collective-permute-start(bf16[512,512]{1,0:T(8,128)(2,1)S(1)} %constant_dynamic-update-slice_fusion.2.h0_ref), channel_id=1, source_target_pairs={{0,16},{4,20},{8,24},{12,28},{16,32},{20,36},{24,40},{28,44},{32,4... | collective-permute-start | bytes 1572872 | tf_op jit(solution)/shard_map/ppermute | solution.py:320
  107.0 36.0 %collective-permute-start.7 = (bf16[512,512]{1,0:T(8,128)(2,1)S(1)}, bf16[512,512]{1,0:T(8,128)(2,1)S(1)}, u32[]{:S(2)}, u32[]{:S(2)}) collective-permute-start(bf16[512,512]{1,0:T(8,128)(2,1)S(1)} %constant_dynamic-update-slice_fusion.2.h0_ref), channel_id=1, source_target_pairs={{0,48},{4,52},{8,56},{12,60},{16,0},{20,4},{24,8},{28,12},{32,16},... | collective-permute-start | bytes 1572872 | tf_op jit(solution)/shard_map/ppermute | solution.py:320
  107.0 36.5 %collective-permute-start.8 = (bf16[512,512]{1,0:T(8,128)(2,1)S(1)}, bf16[512,512]{1,0:T(8,128)(2,1)S(1)}, u32[]{:S(2)}, u32[]{:S(2)}) collective-permute-start(bf16[512,512]{1,0:T(8,128)(2,1)S(1)} %constant_dynamic-update-slice_fusion.2.h0_ref), channel_id=1, source_target_pairs={{0,32},{4,36},{8,40},{12,44},{16,48},{20,52},{24,56},{28,60},{32,0... | collective-permute-start | bytes 1572872 | tf_op jit(solution)/shard_map/ppermute | solution.py:320
  138.7 38.8 %collective-permute-start.22 = (bf16[512,512]{1,0:T(8,128)(2,1)S(1)}, bf16[512,512]{1,0:T(8,128)(2,1)S(1)}, u32[]{:S(2)}, u32[]{:S(2)}) collective-permute-start(bf16[512,512]{1,0:T(8,128)(2,1)S(1)} %copy-done.16), channel_id=1, source_target_pairs={{0,2},{1,3},{2,0},{3,1},{4,6},{5,7},{6,4},{7,5},{8,10},{9,11},{10,... | collective-permute-start | bytes 1572872 | tf_op jit(solution)/shard_map/ppermute | solution.py:313
  138.8 39.0 %collective-permute-start.23 = (bf16[512,512]{1,0:T(8,128)(2,1)S(1)}, bf16[512,512]{1,0:T(8,128)(2,1)S(1)}, u32[]{:S(2)}, u32[]{:S(2)}) collective-permute-start(bf16[512,512]{1,0:T(8,128)(2,1)S(1)} %copy-done.14), channel_id=1, source_target_pairs={{0,3},{1,2},{2,1},{3,0},{4,7},{5,6},{6,5},{7,4},{8,11},{9,10},{10,... | collective-permute-start | bytes 1572872 | tf_op jit(solution)/shard_map/ppermute | solution.py:313
  143.1 34.8 %collective-permute-start.21 = (bf16[512,512]{1,0:T(8,128)(2,1)}, bf16[512,512]{1,0:T(8,128)(2,1)S(1)}, u32[]{:S(2)}, u32[]{:S(2)}) collective-permute-start(bf16[512,512]{1,0:T(8,128)(2,1)} %get-tuple-element.30), channel_id=1, source_target_pairs={{0,1},{1,0},{2,3},{3,2},{4,5},{5,4},{6,7},{7,6},{8,9},{9,8},{10,11... | collective-permute-start | bytes 1572872 | tf_op jit(solution)/shard_map/ppermute | solution.py:313
  160.6 17.3 %collective-permute-start.10 = (bf16[512,512]{1,0:T(8,128)(2,1)}, bf16[512,512]{1,0:T(8,128)(2,1)S(1)}, u32[]{:S(2)}, u32[]{:S(2)}) collective-permute-start(bf16[512,512]{1,0:T(8,128)(2,1)} %get-tuple-element.24), channel_id=1, source_target_pairs={{0,2},{1,3},{2,0},{3,1},{4,6},{5,7},{6,4},{7,5},{8,10},{9,11},{10,... | collective-permute-start | bytes 1572872 | tf_op jit(solution)/shard_map/ppermute | solution.py:313
  161.9 24.3 %collective-permute-start.11 = (bf16[512,512]{1,0:T(8,128)(2,1)}, bf16[512,512]{1,0:T(8,128)(2,1)S(1)}, u32[]{:S(2)}, u32[]{:S(2)}) collective-permute-start(bf16[512,512]{1,0:T(8,128)(2,1)} %get-tuple-element.25), channel_id=1, source_target_pairs={{0,3},{1,2},{2,1},{3,0},{4,7},{5,6},{6,5},{7,4},{8,11},{9,10},{10,... | collective-permute-start | bytes 1572872 | tf_op jit(solution)/shard_map/ppermute | solution.py:313
  177.6 8.6 %collective-permute-start.9 = (bf16[512,512]{1,0:T(8,128)(2,1)}, bf16[512,512]{1,0:T(8,128)(2,1)S(1)}, u32[]{:S(2)}, u32[]{:S(2)}) collective-permute-start(bf16[512,512]{1,0:T(8,128)(2,1)} %get-tuple-element.23), channel_id=1, source_target_pairs={{0,1},{1,0},{2,3},{3,2},{4,5},{5,4},{6,7},{7,6},{8,9},{9,8},{10,11... | collective-permute-start | bytes 1572872 | tf_op jit(solution)/shard_map/ppermute | solution.py:313
  (20 other events, 359.5 us)

commit v2 on v0

v2 whole, which is shorter than its diff:
```python
import math

import jax
import jax.numpy as jnp
from jax import lax
from jax.experimental import pallas as pl
from jax.experimental.pallas import tpu as pltpu
from jax.sharding import PartitionSpec as P

HD = 128
BLK = 256
P1 = 8
P2 = 64
R1 = 12
SEQ = 32
TOK = 2048
HEADS = 8
NEG = -1e30
MIDB = BLK // P1
FARD = TOK // P2
FARS = SEQ * FARD
MIDS = 19 * MIDB
KEYS = 512 + 384 + FARS
EXP_SCALE = math.log2(math.e) / math.sqrt(HD)
CHUNKS = (5, 3)
VMEM_LIMIT = 56 * 1024 * 1024
BF = jnp.bfloat16
WORK = 4 * 4 * BLK * KEYS * HD * 8


def seq_route(move):
    route = []
    for s in range(SEQ):
        x, z, y = move(s // 16, (s // 4) % 4, s % 4)
        route.append((s, x * 16 + (z % 4) * 4 + y % 4))
    return route


Y_UP = seq_route(lambda x, z, y: (x, z, y + 1))
Y_DOWN = seq_route(lambda x, z, y: (x, z, y - 1))
X_ROUTE = seq_route(lambda x, z, y: (1 - x, z, y))
Z_UP = seq_route(lambda x, z, y: (x, z + 1, y))
Z_DOWN = seq_route(lambda x, z, y: (x, z - 1, y))
FROM = (0, 1, 3, 2)


def shift_route(distance):
    return [(i - distance, i) for i in range(distance, SEQ)]


ALONG_Y = [(i, i + 1) for i in range(SEQ) if i % 4 < 3]
UP_Z = [(i, i + 4) for i in range(3, SEQ - 4, 4)]
ROUND_Y = [(i, i - 3) for i in range(7, SEQ, 4)]


def pool_kernel(k_ref, v_ref, send_k_ref, send_v_ref, mid2_ref, far_ref):
    rows = lax.broadcasted_iota(jnp.int32, (48, BLK), 0)
    cols = lax.broadcasted_iota(jnp.int32, (48, BLK), 1)
    mid = jnp.where(cols // P1 == rows, 1.0, 0.0)
    far = jnp.where(cols // P2 == rows - 32, 1.0, 0.0)
    heads = k_ref.shape[1] // HD
    for i, (ref, send_ref) in enumerate(((k_ref, send_k_ref), (v_ref, send_v_ref))):
        group = (mid / P1, far / P2) if i == 0 else (mid, far)
        take = jnp.where(rows < 32, group[0], group[1]).astype(BF)
        fars = []
        for b in range(TOK // BLK):
            pooled = jnp.dot(
                take, ref[b * BLK : (b + 1) * BLK, :], preferred_element_type=jnp.float32
            )
            mids = pooled[:32].astype(BF)
            for h in range(heads):
                piece = mids[:, h * HD : (h + 1) * HD]
                send_ref[h, BLK + b * MIDB : BLK + (b + 1) * MIDB, :] = piece
                if b >= 4:
                    mid2_ref[h, i, (b - 4) * MIDB : (b - 3) * MIDB, :] = piece
            fars.append(pooled[32:36])
        fars = jnp.concatenate(fars, axis=0).astype(BF)
        for h in range(heads):
            send_ref[h, :BLK, :] = ref[TOK - BLK :, h * HD : (h + 1) * HD]
            far_ref[h, i] = fars[:, h * HD : (h + 1) * HD]


def pool(first, heads, key_rows, value_rows):
    step = 2
    return pl.pallas_call(
        pool_kernel,
        grid=(heads // step,),
        in_specs=[pl.BlockSpec((TOK, step * HD), lambda i: (0, first // step + i))] * 2,
        out_specs=[
            pl.BlockSpec((step, 2 * BLK, HD), lambda i: (i, 0, 0)),
            pl.BlockSpec((step, 2 * BLK, HD), lambda i: (i, 0, 0)),
            pl.BlockSpec((step, 2, 128, HD), lambda i: (i, 0, 0, 0)),
            pl.BlockSpec((step, 2, FARD, HD), lambda i: (i, 0, 0, 0)),
        ],
        out_shape=[
            jax.ShapeDtypeStruct((heads, 2 * BLK, HD), BF),
            jax.ShapeDtypeStruct((heads, 2 * BLK, HD), BF),
            jax.ShapeDtypeStruct((heads, 2, 128, HD), BF),
            jax.ShapeDtypeStruct((heads, 2, FARD, HD), BF),
        ],
        compiler_params=pltpu.CompilerParams(vmem_limit_bytes=VMEM_LIMIT),
        cost_estimate=pl.CostEstimate(
            flops=2 * 2 * TOK * heads * HD * 48,
            bytes_accessed=2 * TOK * heads * HD * 3,
            transcendentals=0,
        ),
        name="pool",
    )(key_rows, value_rows)


def dot_nt(a, b):
    return lax.dot_general(a, b, (((1,), (1,)), ((), ())), preferred_element_type=jnp.float32)


def dot_ones(weights, values, one):
    wide = jnp.concatenate([values, jnp.full(values.shape, one, BF)], axis=1)
    return jnp.dot(weights, wide, preferred_element_type=jnp.float32)


def attend_kernel(
    info_ref, q_ref, k_ref, v_ref, kp_ref, vp_ref, far_ok_ref, own_k_ref, own_v_ref, back_k_ref, back_v_ref, back2_ref,
    h0_ref, h1_ref, h2_ref, h3_ref, oa_ref, ob_ref, kn, vn, km, vm, sa, sb,
):
    s = info_ref[0]
    half = info_ref[1]
    flip = info_ref[2]

    far_refs = (h0_ref, h1_ref, h2_ref, h3_ref)
    from_other = jnp.full((BLK, HD), half, jnp.int32) == 0
    kn[:BLK, :] = jnp.where(from_other, back_k_ref[0, :BLK], kp_ref[...])
    vn[:BLK, :] = jnp.where(from_other, back_v_ref[0, :BLK], vp_ref[...])
    kn[BLK:, :] = k_ref[...]
    vn[BLK:, :] = v_ref[...]
    for i, (to, back_ref, own_ref) in enumerate(
        ((km, back_k_ref, own_k_ref), (vm, back_v_ref, own_v_ref))
    ):
        to[0:128, :] = back2_ref[0, i]
        to[128:384, :] = back_ref[0, BLK:]
        to[384:608, :] = own_ref[0, BLK : BLK + 224]

    def block_of(n):
        return 2 * ((n // 2) ^ flip) + n % 2

    def scores(n, s_ref):
        local = block_of(n)
        j = half * 4 + local
        start = pl.multiple_of(local * BLK, BLK)
        q = q_ref[pl.ds(start, BLK), :]
        sn = dot_nt(q, kn[pl.ds(start, BLK), :])
        sn = sn + jnp.where((s == 0) & (j == 0), NEG, 0.0)
        s_ref[:, 0:256] = sn
        top = jnp.maximum(sn[:, :128], sn[:, 128:])
        rows = lax.broadcasted_iota(jnp.int32, (BLK, BLK), 0)
        cols = lax.broadcasted_iota(jnp.int32, (BLK, BLK), 1)
        sd = dot_nt(q, kn[pl.ds(start + BLK, BLK), :])
        sd = jnp.where(cols <= rows, sd, NEG)
        s_ref[:, 256:512] = sd
        top = jnp.maximum(top, jnp.maximum(sd[:, :128], sd[:, 128:]))
        col = lax.broadcasted_iota(jnp.int32, (1, 384), 1)
        ok = jnp.minimum(col - MIDB * (R1 - 8 * s - j), (R1 - 1) * MIDB - 1 - col) >= 0
        sm = dot_nt(q, km[pl.ds(pl.multiple_of(j * MIDB, MIDB), 384), :])
        sm = sm + jnp.where(ok, 0.0, NEG)
        s_ref[:, 512:896] = sm
        for i in range(3):
            top = jnp.maximum(top, sm[:, i * 128 : i * 128 + 128])
        for i in range(4):
            sf = dot_nt(q, far_refs[i][0, 0]) + far_ok_ref[pl.ds(j, 1), i * 256 : i * 256 + 256]
            s_ref[:, 896 + i * 256 : 1152 + i * 256] = sf
            top = jnp.maximum(top, jnp.maximum(sf[:, :128], sf[:, 128:]))
        return jnp.max(top, axis=1, keepdims=True)

    def finish(n, s_ref, top, o_ref):
        local = block_of(n)
        j = half * 4 + local
        start = pl.multiple_of(local * BLK, BLK)

        def weights(a, b):
            return jnp.exp2((s_ref[:, a:b] - top) * EXP_SCALE).astype(BF)

        acc = dot_ones(weights(0, 512), vn[pl.ds(start, 512), :], 1)
        mids = vm[pl.ds(pl.multiple_of(j * MIDB, MIDB), 384), :]
        acc = acc + dot_ones(weights(512, 896), mids, P1)
        for i in range(4):
            acc = acc + dot_ones(weights(896 + i * 256, 1152 + i * 256), far_refs[i][0, 1], P2)
        at = (n % 2) * BLK
        o_ref[at : at + BLK, :] = (acc[:, :HD] / acc[:, HD:]).astype(BF)

    slots = (sa, sb)
    top = scores(0, sa)
    for n in range(4):
        later = scores(n + 1, slots[(n + 1) % 2]) if n < 3 else None
        finish(n, slots[n % 2], top, (oa_ref, ob_ref)[n // 2])
        top = later


def attend(work, first, heads, info, queries, key_rows, value_rows, far_ok, own_k, own_v, back_k, back_v, back2, *fars):
    def rows(count, row):
        return pl.BlockSpec((count, HD), lambda h, info: (row(info), first + h))

    half = rows(1024, lambda info: info[1])
    before = rows(BLK, lambda info: 3 * info[1])
    head = lambda count: pl.BlockSpec((1, 2, count, HD), lambda h, info: (h, 0, 0, 0))
    out = pl.BlockSpec((512, HD), lambda h, info: (0, h))
    return pl.pallas_call(
        attend_kernel,
        grid_spec=pltpu.PrefetchScalarGridSpec(
            num_scalar_prefetch=1,
            grid=(heads,),
            in_specs=[half, half, half, before, before]
            + [pl.BlockSpec((8, FARS), lambda h, info: (0, 0))]
            + [pl.BlockSpec((1, 2 * BLK, HD), lambda h, info: (first + h, 0, 0))] * 2
            + [pl.BlockSpec((1, 2 * BLK, HD), lambda h, info: (h, 0, 0))] * 2
            + [pl.BlockSpec((1, 2, 128, HD), lambda h, info: (first + h, 0, 0, 0))]
            + [head(256)] * 4,
            out_specs=[out, out],
            scratch_shapes=[
                pltpu.VMEM((1280, HD), BF),
                pltpu.VMEM((1280, HD), BF),
                pltpu.VMEM((MIDS, HD), BF),
                pltpu.VMEM((MIDS, HD), BF),
                pltpu.VMEM((BLK, KEYS), jnp.float32),
                pltpu.VMEM((BLK, KEYS), jnp.float32),
            ],
        ),
        out_shape=[jax.ShapeDtypeStruct((512, heads * HD), BF)] * 2,
        compiler_params=pltpu.CompilerParams(vmem_limit_bytes=VMEM_LIMIT),
        cost_estimate=pl.CostEstimate(
            flops=work,
            bytes_accessed=4096,
            transcendentals=0,
        ),
        name="attend",
    )(info, queries, key_rows, value_rows, key_rows, value_rows, far_ok, own_k, own_v, back_k, back_v, back2, *fars)


def place_kernel(columns, me_ref, *refs):
    count = len(columns)
    pieces, out_ref, held, in_sems, out_sems = refs[:count], *refs[count:]
    me = me_ref[0]
    loads, stores = [], []
    for i in range(count):
        loads.append(pltpu.make_async_copy(pieces[i], held[i], in_sems.at[i]))
        loads[i].start()
    for i, (k, at) in enumerate(columns):
        to = pl.multiple_of((me ^ k) * 1024 + at, HD)
        width = pieces[i].shape[1]
        stores.append(
            pltpu.make_async_copy(held[i], out_ref.at[:, pl.ds(to, width)], out_sems.at[i])
        )
        loads[i].wait()
        stores[i].start()
    for store in stores:
        store.wait()


def place(me, pieces, columns):
    count = len(pieces)
    return pl.pallas_call(
        lambda *refs: place_kernel(columns, *refs),
        in_specs=[pl.BlockSpec(memory_space=pltpu.SMEM)]
        + [pl.BlockSpec(memory_space=pl.ANY)] * count,
        out_specs=pl.BlockSpec(memory_space=pl.ANY),
        out_shape=jax.ShapeDtypeStruct((512, 4096), BF),
        scratch_shapes=[
            [pltpu.VMEM(piece.shape, BF) for piece in pieces],
            pltpu.SemaphoreType.DMA((count,)),
            pltpu.SemaphoreType.DMA((count,)),
        ],
        compiler_params=pltpu.CompilerParams(vmem_limit_bytes=VMEM_LIMIT),
        cost_estimate=pl.CostEstimate(
            flops=0, bytes_accessed=count * 1024 * 1024, transcendentals=0
        ),
        name="place",
    )(me, *pieces)


def swap_heads(piece, k):
    return lax.ppermute(piece, "head", [(i, i ^ k) for i in range(4)])


def far_bias(s):
    x, z, y = s // 16, (s // 4) % 4, s % 4
    of = jnp.array(FROM, jnp.int32)
    zs = ((z + of) % 4).reshape(4, 1, 1, 1)
    ys = ((y + of) % 4).reshape(1, 4, 1, 1)
    xs = (x ^ jnp.arange(2, dtype=jnp.int32)).reshape(1, 1, 2, 1)
    group = (xs * 16 + zs * 4 + ys) * FARD + jnp.arange(FARD, dtype=jnp.int32)
    limit = (8 * s + jnp.arange(8, dtype=jnp.int32) - R1) * (BLK // P2)
    return jnp.where(group.reshape(1, FARS) < limit[:, None], 0.0, NEG)


def shards(queries, key_rows, value_rows):
    s = lax.axis_index("seq").astype(jnp.int32)
    me = lax.axis_index("head").astype(jnp.int32)
    pair, flip = me // 2, me % 2
    over = lambda value, route: lax.ppermute(value, "seq", route)
    firsts = [sum(CHUNKS[:c]) for c in range(len(CHUNKS))]
    own_k, own_v, last, f0 = pool(0, HEADS, key_rows, value_rows)
    g0 = jnp.concatenate([f0, over(f0, X_ROUTE)], axis=2)
    g0, own_v = lax.optimization_barrier((g0, own_v))
    cut = lambda value, c: value[firsts[c] : firsts[c] + CHUNKS[c]]
    above = [over(cut(own_v, c), UP_Z) for c in range(2)]
    g1, g3 = over(g0, Y_DOWN), over(g0, Y_UP)
    gs = [g0, g1, g3, over(g1, Y_DOWN)]
    gs, above[0], own_k, own_v, last = lax.optimization_barrier(
        (gs, above[0], own_k, own_v, last)
    )
    own = (own_k, own_v)
    far_ok = far_bias(s)

    def first_stage(c, own_k, own_v, gs):
        h0 = jnp.concatenate([cut(g, c) for g in gs], axis=2)
        h1, h3 = over(h0, Z_DOWN), over(h0, Z_UP)
        back_k = over(cut(own_k, c), shift_route(1))
        along = over(cut(own_v, c), ALONG_Y)
        return h0, h1, h3, back_k, along

    def second_stage(above, h0, h1, h3, back_k, along):
        h2 = over(h1, Z_DOWN)
        back_v = jnp.where(s % 4 == 0, over(above, ROUND_Y), along)
        return (far_ok, *own, back_k, back_v, back2, h0, h1, h3, h2)

    pieces = {}

    def run(c, half, parts):
        which, names = ((1 - pair, (2, 3)), (pair, (0, 1)))[half]
        info = jnp.stack([s, which, flip])
        work = WORK if c else 1
        outs = attend(work, firsts[c], CHUNKS[c], info, queries, key_rows, value_rows, *parts)
        for k, out in zip(names, outs):
            pieces[c, k] = swap_heads(out, k) if k else out
        return outs[0]

    stage = first_stage(0, own_k, own_v, gs)
    back2 = over(last, shift_route(2))
    sent, h1 = lax.optimization_barrier(((own_k, own_v, gs), stage[1]))
    parts = second_stage(above[0], stage[0], h1, *stage[2:])
    stage = first_stage(1, *sent)
    done = run(0, 0, parts)
    parts_b = second_stage(above[1], *stage)
    far_ok, done = lax.optimization_barrier((parts[0], done))
    done = run(0, 1, (far_ok, *parts[1:]))
    far_ok, done, pieces[0, 2] = lax.optimization_barrier((parts_b[0], done, pieces[0, 2]))
    done = run(1, 0, (far_ok, *parts_b[1:]))
    far_ok, done, pieces[0, 3] = lax.optimization_barrier((far_ok, done, pieces[0, 3]))
    run(1, 1, (far_ok, *parts_b[1:]))
    order = sorted(pieces, key=lambda at: (at[0], at[1]))
    return place(
        me.reshape(1), [pieces[at] for at in order], [(k, firsts[c] * HD) for c, k in order]
    )


def solution(mesh):
    return jax.shard_map(
        shards,
        mesh=mesh,
        in_specs=(P("seq", "head"), P("seq", "head"), P("seq", "head")),
        out_specs=P(("seq", "head"), None),
        check_vma=False,
    )
```

time: 433 us -> 189 us (0.44)
  the two profiles are of different devices: /device:TPU:5 before, /device:TPU:29 now
where the time goes in v2:
time: 189 us; the launch traced here: 188 us
  Pallas kernels  66.5 us (35%)
  starting transfers between devices  54.2 us (29%)
  waiting for transfers between devices  47.2 us (25%)
  local copies, waits for them, and re-layouts  14.3 us (8%)
  other arithmetic  5.41 us (3%)
    pallas_call x4, Pallas kernels, attend(): pl.pallas_call(attend_kernel, grid_spec=pltpu.PrefetchScalarGridSpec(num_...  56.9 us
    ppermute x19, starting transfers between devices, shards(): over = lambda value, route: lax.ppermute(value, 'seq', route)  46.5 us
    ppermute x19, waiting for transfers between devices, shards(): over = lambda value, route: lax.ppermute(value, 'seq', route)  34.9 us
    ppermute x6, waiting for transfers between devices, swap_heads(): return lax.ppermute(piece, 'head', [(i, i ^ k) for i in range(4)])  12.2 us
    slice x15, local copies, waits for them, and re-layouts, shards(): cut = lambda value, c: value[firsts[c]:firsts[c] + CHUNKS[c]]  8.64 us
    ppermute x6, starting transfers between devices, swap_heads(): return lax.ppermute(piece, 'head', [(i, i ^ k) for i in range(4)])  7.7 us
    pallas_call x1, Pallas kernels, pool(): pl.pallas_call(pool_kernel, grid=(heads // step,), in_specs=[pl.BlockSpec...  6.13 us
    unnamed x52, local copies, waits for them, and re-layouts  5.54 us
  transfers between devices with their start and end apart: 25, of which 11 were waited for; matrix products, arithmetic and copies ran while one was open for 6% of the time, Pallas kernels for 30%

profile of v2, /device:TPU:29, one launch (start us, length us, event | category | flops | bytes accessed | tf_op | source)
XLA Modules:
  0.0 188.2 jit_solution(3023741545524053507)
XLA Ops:
  0.0 6.1 %pool.1 = (bf16[8,512,128]{2,1,0:T(8,128)(2,1)}, bf16[8,512,128]{2,1,0:T(8,128)(2,1)}, bf16[8,2,128,128]{3,2,1,0:T(8,128)(2,1)}, bf16[8,2,32,128]{3,2,1,0:T(8,128)(2,1)}) custom-call(bf16[2048,1024]{1,0:T(8,128)(2,1)} %kp_ref.7, bf16[2048,1024]{1,0:T(8,128)(2,1)} %vp_ref.7), custom_call_target="tpu_custom_call" | custom-call | flops 402653184 | bytes 12582912 | tf_op jit(solution)/shard_map/pool/pallas_call | solution.py:85
  6.4 5.9 %collective-permute-done = bf16[8,2,32,128]{3,2,1,0:T(8,128)(2,1)S(1)} collective-permute-done((bf16[8,2,32,128]{3,2,1,0:T(8,128)(2,1)}, bf16[8,2,32,128]{3,2,1,0:T(8,128)(2,1)S(1)}, u32[]{:S(2)}, u32[]{:S(2)}) %collective-permute-start) | collective-permute-done | bytes 131104 | tf_op jit(solution)/shard_map/ppermute | solution.py:296
  14.5 3.5 %collective-permute-start.4 = (bf16[5,512,128]{2,1,0:T(8,128)(2,1)S(1)}, bf16[5,512,128]{2,1,0:T(8,128)(2,1)S(1)}, u32[]{:S(2)}, u32[]{:S(2)}) collective-permute-start(bf16[5,512,128]{2,1,0:T(8,128)(2,1)S(1)} %slice.42), channel_id=1, source_target_pairs={{12,28},{28,44},{44,60},{60,76},{76,92},{92,108},{108,124},{13,29}... | collective-permute-start | bytes 1966088 | tf_op jit(solution)/shard_map/ppermute | solution.py:296
  18.1 2.6 %collective-permute-start.2 = (bf16[8,2,64,128]{3,2,1,0:T(8,128)(2,1)S(1)}, bf16[8,2,64,128]{3,2,1,0:T(8,128)(2,1)S(1)}, u32[]{:S(2)}, u32[]{:S(2)}) collective-permute-start(bf16[8,2,64,128]{3,2,1,0:T(8,128)(2,1)S(1)} %pad_maximum_fusion.2), channel_id=1, source_target_pairs={{0,4},{4,8},{8,12},{12,0},{16,20},{20,24},{24,28},{28,16},{32,36},... | collective-permute-start | bytes 786440 | tf_op jit(solution)/shard_map/ppermute | solution.py:296
  20.7 4.5 %collective-permute-done.1 = bf16[8,2,64,128]{3,2,1,0:T(8,128)(2,1)S(1)} collective-permute-done((bf16[8,2,64,128]{3,2,1,0:T(8,128)(2,1)S(1)}, bf16[8,2,64,128]{3,2,1,0:T(8,128)(2,1)S(1)}, u32[]{:S(2)}, u32[]{:S(2)}) %collective-permute-start.1) | collective-permute-done | bytes 262176 | tf_op jit(solution)/shard_map/ppermute | solution.py:296
  25.3 6.6 %collective-permute-done.3 = bf16[8,2,64,128]{3,2,1,0:T(8,128)(2,1)S(1)} collective-permute-done((bf16[8,2,64,128]{3,2,1,0:T(8,128)(2,1)S(1)}, bf16[8,2,64,128]{3,2,1,0:T(8,128)(2,1)S(1)}, u32[]{:S(2)}, u32[]{:S(2)}) %collective-permute-start.3) | collective-permute-done | bytes 262176 | tf_op jit(solution)/shard_map/ppermute | solution.py:296
  32.0 2.7 %collective-permute-done.4 = bf16[5,512,128]{2,1,0:T(8,128)(2,1)S(1)} collective-permute-done((bf16[5,512,128]{2,1,0:T(8,128)(2,1)S(1)}, bf16[5,512,128]{2,1,0:T(8,128)(2,1)S(1)}, u32[]{:S(2)}, u32[]{:S(2)}) %collective-permute-start.4) | collective-permute-done | bytes 655392 | tf_op jit(solution)/shard_map/ppermute | solution.py:296
  37.7 2.2 %collective-permute-start.15 = (bf16[3,512,128]{2,1,0:T(8,128)(2,1)}, bf16[3,512,128]{2,1,0:T(8,128)(2,1)}, u32[]{:S(2)}, u32[]{:S(2)}) collective-permute-start(bf16[3,512,128]{2,1,0:T(8,128)(2,1)} %slice.50), channel_id=1, source_target_pairs={{12,28},{28,44},{44,60},{60,76},{76,92},{92,108},{108,124},{13,29}... | collective-permute-start | bytes 1179656 | tf_op jit(solution)/shard_map/ppermute | solution.py:296
  42.7 2.1 %collective-permute-start.6 = (bf16[5,512,128]{2,1,0:T(8,128)(2,1)}, bf16[5,512,128]{2,1,0:T(8,128)(2,1)}, u32[]{:S(2)}, u32[]{:S(2)}) collective-permute-start(bf16[5,512,128]{2,1,0:T(8,128)(2,1)} %copy-done.19), channel_id=1, source_target_pairs={{28,16},{44,32},{60,48},{76,64},{92,80},{108,96},{124,112},{29,17}... | collective-permute-start | bytes 1966088 | tf_op jit(solution)/shard_map/ppermute | solution.py:296
  49.6 2.1 %collective-permute-done.15 = bf16[3,512,128]{2,1,0:T(8,128)(2,1)} collective-permute-done((bf16[3,512,128]{2,1,0:T(8,128)(2,1)}, bf16[3,512,128]{2,1,0:T(8,128)(2,1)}, u32[]{:S(2)}, u32[]{:S(2)}) %collective-permute-start.15) | collective-permute-done | bytes 393248 | tf_op jit(solution)/shard_map/ppermute | solution.py:296
  51.7 2.9 %collective-permute-start.5 = (bf16[5,512,128]{2,1,0:T(8,128)(2,1)}, bf16[5,512,128]{2,1,0:T(8,128)(2,1)S(1)}, u32[]{:S(2)}, u32[]{:S(2)}) collective-permute-start(bf16[5,512,128]{2,1,0:T(8,128)(2,1)} %slice.43), channel_id=1, source_target_pairs={{0,4},{4,8},{8,12},{12,16},{16,20},{20,24},{24,28},{28,32},{32,36}... | collective-permute-start | bytes 1966088 | tf_op jit(solution)/shard_map/ppermute | solution.py:296
  58.2 7.2 %collective-permute-done.6 = bf16[5,512,128]{2,1,0:T(8,128)(2,1)} collective-permute-done((bf16[5,512,128]{2,1,0:T(8,128)(2,1)}, bf16[5,512,128]{2,1,0:T(8,128)(2,1)}, u32[]{:S(2)}, u32[]{:S(2)}) %collective-permute-start.6) | collective-permute-done | bytes 655392 | tf_op jit(solution)/shard_map/ppermute | solution.py:296
  65.4 5.3 %collective-permute-start.16 = (bf16[3,512,128]{2,1,0:T(8,128)(2,1)}, bf16[3,512,128]{2,1,0:T(8,128)(2,1)S(1)}, u32[]{:S(2)}, u32[]{:S(2)}) collective-permute-start(bf16[3,512,128]{2,1,0:T(8,128)(2,1)} %collective-permute-done.15), channel_id=1, source_target_pairs={{28,16},{44,32},{60,48},{76,64},{92,80},{108,96},{124,112},{29,17}... | collective-permute-start | bytes 1179656 | tf_op jit(solution)/shard_map/ppermute | solution.py:296
  70.7 18.2 %collective-permute-start.18 = (bf16[3,2,256,128]{3,2,1,0:T(8,128)(2,1)S(1)}, bf16[3,2,256,128]{3,2,1,0:T(8,128)(2,1)S(1)}, u32[]{:S(2)}, u32[]{:S(2)}) collective-permute-start(bf16[3,2,256,128]{3,2,1,0:T(8,128)(2,1)S(1)} %pad_maximum_fusion.1.h0_ref), channel_id=1, source_target_pairs={{0,48},{4,52},{8,56},{12,60},{16,0},{20,4},{24,8},{28,12},{32,16},... | collective-permute-start | bytes 1179656 | tf_op jit(solution)/shard_map/ppermute | solution.py:296
  88.9 2.0 %broadcast_select_fusion.back_v_ref = bf16[5,512,128]{2,1,0:T(8,128)(2,1)} fusion(bf16[5,512,128]{2,1,0:T(8,128)(2,1)} %collective-permute-done.6, bf16[5,512,128]{2,1,0:T(8,128)(2,1)} %collective-permute-done.7, pred[]{:T(512)S(6)} %eq.13), kind=kLoop, calls=%fused_computation.1 | loop fusion | flops 327680 | bytes 1966081 | tf_op jit(solution)/shard_map/jit(_where)/select_n | solution.py:320
  92.2 17.0 %attend.4 = (bf16[512,640]{1,0:T(8,128)(2,1)}, bf16[512,640]{1,0:T(8,128)(2,1)}) custom-call(s32[3]{0:T(128)} %get-tuple-element.76.info_ref, bf16[2048,1024]{1,0:T(8,128)(2,1)} %q_ref.7, bf16[2048,1024]{1,0:T(8,128)(2,1)} %kp_ref.7, bf16[2048,1024]{1,0:T(8,128)(2,1)} %vp_ref.7, bf16[2048,1024]{1,0:T(8,128)(2,1)} %kp_ref.7, bf16[2048,1024]{1,0:T(8,128)(2,1)} %vp_ref.7, ...), custom_call_target="tpu_custom_call" | custom-call | flops 1 | bytes 4096 | tf_op jit(solution)/shard_map/attend/pallas_call | solution.py:204
  115.6 2.3 %collective-permute-start.20 = (bf16[3,2,256,128]{3,2,1,0:T(8,128)(2,1)S(1)}, bf16[3,2,256,128]{3,2,1,0:T(8,128)(2,1)S(1)}, u32[]{:S(2)}, u32[]{:S(2)}) collective-permute-start(bf16[3,2,256,128]{3,2,1,0:T(8,128)(2,1)S(1)} %collective-permute-done.18.h1_ref), channel_id=1, source_target_pairs={{0,48},{4,52},{8,56},{12,60},{16,0},{20,4},{24,8},{28,12},{32,16},... | collective-permute-start | bytes 1179656 | tf_op jit(solution)/shard_map/ppermute | solution.py:296
  117.9 4.5 %collective-permute-done.17 = bf16[3,512,128]{2,1,0:T(8,128)(2,1)S(1)} collective-permute-done((bf16[3,512,128]{2,1,0:T(8,128)(2,1)S(1)}, bf16[3,512,128]{2,1,0:T(8,128)(2,1)S(1)}, u32[]{:S(2)}, u32[]{:S(2)}) %collective-permute-start.17) | collective-permute-done | bytes 393248 | tf_op jit(solution)/shard_map/ppermute | solution.py:296
  123.2 17.2 %attend.5 = (bf16[512,640]{1,0:T(8,128)(2,1)}, bf16[512,640]{1,0:T(8,128)(2,1)}) custom-call(s32[3]{0:T(128)} %get-tuple-element.75.info_ref, bf16[2048,1024]{1,0:T(8,128)(2,1)} %q_ref.7, bf16[2048,1024]{1,0:T(8,128)(2,1)} %kp_ref.7, bf16[2048,1024]{1,0:T(8,128)(2,1)} %vp_ref.7, bf16[2048,1024]{1,0:T(8,128)(2,1)} %kp_ref.7, bf16[2048,1024]{1,0:T(8,128)(2,1)} %vp_ref.7, ...), custom_call_target="tpu_custom_call" | custom-call | flops 1 | bytes 4096 | tf_op jit(solution)/shard_map/attend/pallas_call | solution.py:204
  140.4 4.2 %collective-permute-start.12 = (bf16[512,640]{1,0:T(8,128)(2,1)}, bf16[512,640]{1,0:T(8,128)(2,1)S(1)}, u32[]{:S(2)}, u32[]{:S(2)}) collective-permute-start(bf16[512,640]{1,0:T(8,128)(2,1)} %get-tuple-element.57), channel_id=1, source_target_pairs={{0,1},{1,0},{2,3},{3,2},{4,5},{5,4},{6,7},{7,6},{8,9},{9,8},{10,11... | collective-permute-start | bytes 1966088 | tf_op jit(solution)/shard_map/ppermute | solution.py:278
  146.9 11.4 %attend.6 = (bf16[512,384]{1,0:T(8,128)(2,1)}, bf16[512,384]{1,0:T(8,128)(2,1)}) custom-call(s32[3]{0:T(128)} %get-tuple-element.76.info_ref, bf16[2048,1024]{1,0:T(8,128)(2,1)} %q_ref.7, bf16[2048,1024]{1,0:T(8,128)(2,1)} %kp_ref.7, bf16[2048,1024]{1,0:T(8,128)(2,1)} %vp_ref.7, bf16[2048,1024]{1,0:T(8,128)(2,1)} %kp_ref.7, bf16[2048,1024]{1,0:T(8,128)(2,1)} %vp_ref.7, ...), custom_call_target="tpu_custom_call" | custom-call | flops 8053063680 | bytes 4096 | tf_op jit(solution)/shard_map/attend/pallas_call | solution.py:204
  161.1 11.4 %attend.7 = (bf16[512,384]{1,0:T(8,128)(2,1)}, bf16[512,384]{1,0:T(8,128)(2,1)}) custom-call(s32[3]{0:T(128)} %get-tuple-element.75.info_ref, bf16[2048,1024]{1,0:T(8,128)(2,1)} %q_ref.7, bf16[2048,1024]{1,0:T(8,128)(2,1)} %kp_ref.7, bf16[2048,1024]{1,0:T(8,128)(2,1)} %vp_ref.7, bf16[2048,1024]{1,0:T(8,128)(2,1)} %kp_ref.7, bf16[2048,1024]{1,0:T(8,128)(2,1)} %vp_ref.7, ...), custom_call_target="tpu_custom_call" | custom-call | flops 8053063680 | bytes 4096 | tf_op jit(solution)/shard_map/attend/pallas_call | solution.py:204
  174.6 9.3 %collective-permute-done.24.refs_8_ = bf16[512,384]{1,0:T(8,128)(2,1)S(1)} collective-permute-done((bf16[512,384]{1,0:T(8,128)(2,1)S(1)}, bf16[512,384]{1,0:T(8,128)(2,1)S(1)}, u32[]{:S(2)}, u32[]{:S(2)}) %collective-permute-start.24) | collective-permute-done | bytes 393248 | tf_op jit(solution)/shard_map/ppermute | solution.py:278
  184.6 3.4 %place.1 = bf16[512,4096]{1,0:T(8,128)(2,1)} custom-call(s32[1]{0:T(128)} %bitcast.refs_0_, bf16[512,640]{1,0:T(8,128)(2,1)} %get-tuple-element.56.refs_1_, bf16[512,640]{1,0:T(8,128)(2,1)} %copy-done.9, bf16[512,640]{1,0:T(8,128)(2,1)} %copy-done.8, bf16[512,640]{1,0:T(8,128)(2,1)} %copy-done.10, bf16[512,384]{1,0:T(8,128)(2,1)} %get-tuple-element.70.refs_5_, ...), custom_call_target="tpu_custom_call" | custom-call | bytes 8388608 | tf_op jit(solution)/shard_map/place/pallas_call | solution.py:258
  (113 shorter events, 32.9 us)
Async XLA Ops:
  6.1 6.1 %collective-permute-start = (bf16[8,2,32,128]{3,2,1,0:T(8,128)(2,1)}, bf16[8,2,32,128]{3,2,1,0:T(8,128)(2,1)S(1)}, u32[]{:S(2)}, u32[]{:S(2)}) collective-permute-start(bf16[8,2,32,128]{3,2,1,0:T(8,128)(2,1)} %get-tuple-element.39), channel_id=1, source_target_pairs={{0,64},{4,68},{8,72},{12,76},{16,80},{20,84},{24,88},{28,92},{32,9... | collective-permute-start | bytes 393224 | tf_op jit(solution)/shard_map/ppermute | solution.py:296
  14.5 20.2 %collective-permute-start.4 = (bf16[5,512,128]{2,1,0:T(8,128)(2,1)S(1)}, bf16[5,512,128]{2,1,0:T(8,128)(2,1)S(1)}, u32[]{:S(2)}, u32[]{:S(2)}) collective-permute-start(bf16[5,512,128]{2,1,0:T(8,128)(2,1)S(1)} %slice.42), channel_id=1, source_target_pairs={{12,28},{28,44},{44,60},{60,76},{76,92},{92,108},{108,124},{13,29}... | collective-permute-start | bytes 1966088 | tf_op jit(solution)/shard_map/ppermute | solution.py:296
  18.0 7.2 %collective-permute-start.1 = (bf16[8,2,64,128]{3,2,1,0:T(8,128)(2,1)S(1)}, bf16[8,2,64,128]{3,2,1,0:T(8,128)(2,1)S(1)}, u32[]{:S(2)}, u32[]{:S(2)}) collective-permute-start(bf16[8,2,64,128]{3,2,1,0:T(8,128)(2,1)S(1)} %pad_maximum_fusion.2), channel_id=1, source_target_pairs={{0,12},{4,0},{8,4},{12,8},{16,28},{20,16},{24,20},{28,24},{32,44},... | collective-permute-start | bytes 786440 | tf_op jit(solution)/shard_map/ppermute | solution.py:296
  18.1 7.2 %collective-permute-start.2 = (bf16[8,2,64,128]{3,2,1,0:T(8,128)(2,1)S(1)}, bf16[8,2,64,128]{3,2,1,0:T(8,128)(2,1)S(1)}, u32[]{:S(2)}, u32[]{:S(2)}) collective-permute-start(bf16[8,2,64,128]{3,2,1,0:T(8,128)(2,1)S(1)} %pad_maximum_fusion.2), channel_id=1, source_target_pairs={{0,4},{4,8},{8,12},{12,0},{16,20},{20,24},{24,28},{28,16},{32,36},... | collective-permute-start | bytes 786440 | tf_op jit(solution)/shard_map/ppermute | solution.py:296
  25.2 6.7 %collective-permute-start.3 = (bf16[8,2,64,128]{3,2,1,0:T(8,128)(2,1)S(1)}, bf16[8,2,64,128]{3,2,1,0:T(8,128)(2,1)S(1)}, u32[]{:S(2)}, u32[]{:S(2)}) collective-permute-start(bf16[8,2,64,128]{3,2,1,0:T(8,128)(2,1)S(1)} %collective-permute-done.1), channel_id=1, source_target_pairs={{0,12},{4,0},{8,4},{12,8},{16,28},{20,16},{24,20},{28,24},{32,44},... | collective-permute-start | bytes 786440 | tf_op jit(solution)/shard_map/ppermute | solution.py:296
  35.7 13.9 %collective-permute-start.9 = (bf16[5,2,256,128]{3,2,1,0:T(8,128)(2,1)S(1)}, bf16[5,2,256,128]{3,2,1,0:T(8,128)(2,1)S(1)}, u32[]{:S(2)}, u32[]{:S(2)}) collective-permute-start(bf16[5,2,256,128]{3,2,1,0:T(8,128)(2,1)S(1)} %pad_maximum_fusion.h0_ref), channel_id=1, source_target_pairs={{0,48},{4,52},{8,56},{12,60},{16,0},{20,4},{24,8},{28,12},{32,16},... | collective-permute-start | bytes 1966088 | tf_op jit(solution)/shard_map/ppermute | solution.py:296
  37.7 14.0 %collective-permute-start.15 = (bf16[3,512,128]{2,1,0:T(8,128)(2,1)}, bf16[3,512,128]{2,1,0:T(8,128)(2,1)}, u32[]{:S(2)}, u32[]{:S(2)}) collective-permute-start(bf16[3,512,128]{2,1,0:T(8,128)(2,1)} %slice.50), channel_id=1, source_target_pairs={{12,28},{28,44},{44,60},{60,76},{76,92},{92,108},{108,124},{13,29}... | collective-permute-start | bytes 1179656 | tf_op jit(solution)/shard_map/ppermute | solution.py:296
  40.0 14.6 %collective-permute-start.8 = (bf16[8,2,128,128]{3,2,1,0:T(8,128)(2,1)}, bf16[8,2,128,128]{3,2,1,0:T(8,128)(2,1)}, u32[]{:S(2)}, u32[]{:S(2)}) collective-permute-start(bf16[8,2,128,128]{3,2,1,0:T(8,128)(2,1)} %get-tuple-element.48), channel_id=1, source_target_pairs={{0,8},{4,12},{8,16},{12,20},{16,24},{20,28},{24,32},{28,36},{32,40... | collective-permute-start | bytes 1572872 | tf_op jit(solution)/shard_map/ppermute | solution.py:296
  42.7 22.7 %collective-permute-start.6 = (bf16[5,512,128]{2,1,0:T(8,128)(2,1)}, bf16[5,512,128]{2,1,0:T(8,128)(2,1)}, u32[]{:S(2)}, u32[]{:S(2)}) collective-permute-start(bf16[5,512,128]{2,1,0:T(8,128)(2,1)} %copy-done.19), channel_id=1, source_target_pairs={{28,16},{44,32},{60,48},{76,64},{92,80},{108,96},{124,112},{29,17}... | collective-permute-start | bytes 1966088 | tf_op jit(solution)/shard_map/ppermute | solution.py:296
  45.7 25.0 %collective-permute-start.7 = (bf16[5,512,128]{2,1,0:T(8,128)(2,1)}, bf16[5,512,128]{2,1,0:T(8,128)(2,1)}, u32[]{:S(2)}, u32[]{:S(2)}) collective-permute-start(bf16[5,512,128]{2,1,0:T(8,128)(2,1)} %slice.44), channel_id=1, source_target_pairs={{0,4},{4,8},{8,12},{16,20},{20,24},{24,28},{32,36},{36,40},{40,44}... | collective-permute-start | bytes 1966088 | tf_op jit(solution)/shard_map/ppermute | solution.py:296
  49.6 41.4 %collective-permute-start.10 = (bf16[5,2,256,128]{3,2,1,0:T(8,128)(2,1)S(1)}, bf16[5,2,256,128]{3,2,1,0:T(8,128)(2,1)S(1)}, u32[]{:S(2)}, u32[]{:S(2)}) collective-permute-start(bf16[5,2,256,128]{3,2,1,0:T(8,128)(2,1)S(1)} %pad_maximum_fusion.h0_ref), channel_id=1, source_target_pairs={{0,16},{4,20},{8,24},{12,28},{16,32},{20,36},{24,40},{28,44},{32,4... | collective-permute-start | bytes 1966088 | tf_op jit(solution)/shard_map/ppermute | solution.py:296
  51.7 39.3 %collective-permute-start.5 = (bf16[5,512,128]{2,1,0:T(8,128)(2,1)}, bf16[5,512,128]{2,1,0:T(8,128)(2,1)S(1)}, u32[]{:S(2)}, u32[]{:S(2)}) collective-permute-start(bf16[5,512,128]{2,1,0:T(8,128)(2,1)} %slice.43), channel_id=1, source_target_pairs={{0,4},{4,8},{8,12},{12,16},{16,20},{20,24},{24,28},{28,32},{32,36}... | collective-permute-start | bytes 1966088 | tf_op jit(solution)/shard_map/ppermute | solution.py:296
  54.6 36.4 %collective-permute-start.11 = (bf16[5,2,256,128]{3,2,1,0:T(8,128)(2,1)S(1)}, bf16[5,2,256,128]{3,2,1,0:T(8,128)(2,1)S(1)}, u32[]{:S(2)}, u32[]{:S(2)}) collective-permute-start(bf16[5,2,256,128]{3,2,1,0:T(8,128)(2,1)S(1)} %collective-permute-done.9.h1_ref), channel_id=1, source_target_pairs={{0,48},{4,52},{8,56},{12,60},{16,0},{20,4},{24,8},{28,12},{32,16},... | collective-permute-start | bytes 1966088 | tf_op jit(solution)/shard_map/ppermute | solution.py:296
  65.4 48.3 %collective-permute-start.16 = (bf16[3,512,128]{2,1,0:T(8,128)(2,1)}, bf16[3,512,128]{2,1,0:T(8,128)(2,1)S(1)}, u32[]{:S(2)}, u32[]{:S(2)}) collective-permute-start(bf16[3,512,128]{2,1,0:T(8,128)(2,1)} %collective-permute-done.15), channel_id=1, source_target_pairs={{28,16},{44,32},{60,48},{76,64},{92,80},{108,96},{124,112},{29,17}... | collective-permute-start | bytes 1179656 | tf_op jit(solution)/shard_map/ppermute | solution.py:296
  70.7 44.9 %collective-permute-start.18 = (bf16[3,2,256,128]{3,2,1,0:T(8,128)(2,1)S(1)}, bf16[3,2,256,128]{3,2,1,0:T(8,128)(2,1)S(1)}, u32[]{:S(2)}, u32[]{:S(2)}) collective-permute-start(bf16[3,2,256,128]{3,2,1,0:T(8,128)(2,1)S(1)} %pad_maximum_fusion.1.h0_ref), channel_id=1, source_target_pairs={{0,48},{4,52},{8,56},{12,60},{16,0},{20,4},{24,8},{28,12},{32,16},... | collective-permute-start | bytes 1179656 | tf_op jit(solution)/shard_map/ppermute | solution.py:296
  109.2 35.4 %collective-permute-start.13 = (bf16[512,640]{1,0:T(8,128)(2,1)}, bf16[512,640]{1,0:T(8,128)(2,1)S(1)}, u32[]{:S(2)}, u32[]{:S(2)}) collective-permute-start(bf16[512,640]{1,0:T(8,128)(2,1)} %get-tuple-element.54), channel_id=1, source_target_pairs={{0,2},{1,3},{2,0},{3,1},{4,6},{5,7},{6,4},{7,5},{8,10},{9,11},{10,... | collective-permute-start | bytes 1966088 | tf_op jit(solution)/shard_map/ppermute | solution.py:278
  111.3 11.2 %collective-permute-start.17 = (bf16[3,512,128]{2,1,0:T(8,128)(2,1)S(1)}, bf16[3,512,128]{2,1,0:T(8,128)(2,1)S(1)}, u32[]{:S(2)}, u32[]{:S(2)}) collective-permute-start(bf16[3,512,128]{2,1,0:T(8,128)(2,1)S(1)} %slice.51), channel_id=1, source_target_pairs={{0,4},{4,8},{8,12},{16,20},{20,24},{24,28},{32,36},{36,40},{40,44}... | collective-permute-start | bytes 1179656 | tf_op jit(solution)/shard_map/ppermute | solution.py:296
  112.6 32.6 %collective-permute-start.19 = (bf16[3,2,256,128]{3,2,1,0:T(8,128)(2,1)S(1)}, bf16[3,2,256,128]{3,2,1,0:T(8,128)(2,1)S(1)}, u32[]{:S(2)}, u32[]{:S(2)}) collective-permute-start(bf16[3,2,256,128]{3,2,1,0:T(8,128)(2,1)S(1)} %pad_maximum_fusion.1.h0_ref), channel_id=1, source_target_pairs={{0,16},{4,20},{8,24},{12,28},{16,32},{20,36},{24,40},{28,44},{32,4... | collective-permute-start | bytes 1179656 | tf_op jit(solution)/shard_map/ppermute | solution.py:296
  113.7 31.5 %collective-permute-start.14 = (bf16[3,512,128]{2,1,0:T(8,128)(2,1)S(1)}, bf16[3,512,128]{2,1,0:T(8,128)(2,1)S(1)}, u32[]{:S(2)}, u32[]{:S(2)}) collective-permute-start(bf16[3,512,128]{2,1,0:T(8,128)(2,1)S(1)} %slice.49), channel_id=1, source_target_pairs={{0,4},{4,8},{8,12},{12,16},{16,20},{20,24},{24,28},{28,32},{32,36}... | collective-permute-start | bytes 1179656 | tf_op jit(solution)/shard_map/ppermute | solution.py:296
  115.6 29.6 %collective-permute-start.20 = (bf16[3,2,256,128]{3,2,1,0:T(8,128)(2,1)S(1)}, bf16[3,2,256,128]{3,2,1,0:T(8,128)(2,1)S(1)}, u32[]{:S(2)}, u32[]{:S(2)}) collective-permute-start(bf16[3,2,256,128]{3,2,1,0:T(8,128)(2,1)S(1)} %collective-permute-done.18.h1_ref), channel_id=1, source_target_pairs={{0,48},{4,52},{8,56},{12,60},{16,0},{20,4},{24,8},{28,12},{32,16},... | collective-permute-start | bytes 1179656 | tf_op jit(solution)/shard_map/ppermute | solution.py:296
  140.4 33.1 %collective-permute-start.12 = (bf16[512,640]{1,0:T(8,128)(2,1)}, bf16[512,640]{1,0:T(8,128)(2,1)S(1)}, u32[]{:S(2)}, u32[]{:S(2)}) collective-permute-start(bf16[512,640]{1,0:T(8,128)(2,1)} %get-tuple-element.57), channel_id=1, source_target_pairs={{0,1},{1,0},{2,3},{3,2},{4,5},{5,4},{6,7},{7,6},{8,9},{9,8},{10,11... | collective-permute-start | bytes 1966088 | tf_op jit(solution)/shard_map/ppermute | solution.py:278
  144.6 16.5 %collective-permute-start.21 = (bf16[512,640]{1,0:T(8,128)(2,1)S(1)}, bf16[512,640]{1,0:T(8,128)(2,1)S(1)}, u32[]{:S(2)}, u32[]{:S(2)}) collective-permute-start(bf16[512,640]{1,0:T(8,128)(2,1)S(1)} %copy-done.20), channel_id=1, source_target_pairs={{0,3},{1,2},{2,1},{3,0},{4,7},{5,6},{6,5},{7,4},{8,11},{9,10},{10,... | collective-permute-start | bytes 1966088 | tf_op jit(solution)/shard_map/ppermute | solution.py:278
  158.3 16.3 %collective-permute-start.23 = (bf16[512,384]{1,0:T(8,128)(2,1)}, bf16[512,384]{1,0:T(8,128)(2,1)S(1)}, u32[]{:S(2)}, u32[]{:S(2)}) collective-permute-start(bf16[512,384]{1,0:T(8,128)(2,1)} %get-tuple-element.66), channel_id=1, source_target_pairs={{0,2},{1,3},{2,0},{3,1},{4,6},{5,7},{6,4},{7,5},{8,10},{9,11},{10,... | collective-permute-start | bytes 1179656 | tf_op jit(solution)/shard_map/ppermute | solution.py:278
  172.6 11.2 %collective-permute-start.24 = (bf16[512,384]{1,0:T(8,128)(2,1)S(1)}, bf16[512,384]{1,0:T(8,128)(2,1)S(1)}, u32[]{:S(2)}, u32[]{:S(2)}) collective-permute-start(bf16[512,384]{1,0:T(8,128)(2,1)S(1)} %copy-done.25), channel_id=1, source_target_pairs={{0,3},{1,2},{2,1},{3,0},{4,7},{5,6},{6,5},{7,4},{8,11},{9,10},{10,... | collective-permute-start | bytes 1179656 | tf_op jit(solution)/shard_map/ppermute | solution.py:278
  (28 other events, 324.6 us)

commit v3 on v2

--- a/solution.py
+++ b/solution.py
@@ -22,10 +22,9 @@
 MIDS = 19 * MIDB
 KEYS = 512 + 384 + FARS
 EXP_SCALE = math.log2(math.e) / math.sqrt(HD)
-CHUNKS = (5, 3)
+CHUNKS = (4, 4)
 VMEM_LIMIT = 56 * 1024 * 1024
 BF = jnp.bfloat16
-WORK = 4 * 4 * BLK * KEYS * HD * 8
 
 
 def seq_route(move):
@@ -193,13 +192,13 @@
         top = later
 
 
-def attend(work, first, heads, info, queries, key_rows, value_rows, far_ok, own_k, own_v, back_k, back_v, back2, *fars):
+def attend(first, heads, info, queries, key_rows, value_rows, far_ok, own_k, own_v, back_k, back_v, back2, *fars):
     def rows(count, row):
         return pl.BlockSpec((count, HD), lambda h, info: (row(info), first + h))
 
     half = rows(1024, lambda info: info[1])
     before = rows(BLK, lambda info: 3 * info[1])
-    head = lambda count: pl.BlockSpec((1, 2, count, HD), lambda h, info: (h, 0, 0, 0))
+    head = lambda count: pl.BlockSpec((1, 2, count, HD), lambda h, info: (first + h, 0, 0, 0))
     out = pl.BlockSpec((512, HD), lambda h, info: (0, h))
     return pl.pallas_call(
         attend_kernel,
@@ -208,9 +207,8 @@
             grid=(heads,),
             in_specs=[half, half, half, before, before]
             + [pl.BlockSpec((8, FARS), lambda h, info: (0, 0))]
-            + [pl.BlockSpec((1, 2 * BLK, HD), lambda h, info: (first + h, 0, 0))] * 2
-            + [pl.BlockSpec((1, 2 * BLK, HD), lambda h, info: (h, 0, 0))] * 2
-            + [pl.BlockSpec((1, 2, 128, HD), lambda h, info: (first + h, 0, 0, 0))]
+            + [pl.BlockSpec((1, 2 * BLK, HD), lambda h, info: (first + h, 0, 0))] * 4
+            + [head(128)]
             + [head(256)] * 4,
             out_specs=[out, out],
             scratch_shapes=[
@@ -225,9 +223,9 @@
         out_shape=[jax.ShapeDtypeStruct((512, heads * HD), BF)] * 2,
         compiler_params=pltpu.CompilerParams(vmem_limit_bytes=VMEM_LIMIT),
         cost_estimate=pl.CostEstimate(
-            flops=work,
-            bytes_accessed=4096,
-            transcendentals=0,
+            flops=heads * 4 * BLK * KEYS * HD * 8,
+            bytes_accessed=heads * HD * 2 * 6000,
+            transcendentals=heads * 4 * BLK * KEYS,
         ),
         name="attend",
     )(info, queries, key_rows, value_rows, key_rows, value_rows, far_ok, own_k, own_v, back_k, back_v, back2, *fars)
@@ -298,52 +296,27 @@
     own_k, own_v, last, f0 = pool(0, HEADS, key_rows, value_rows)
     g0 = jnp.concatenate([f0, over(f0, X_ROUTE)], axis=2)
     g0, own_v = lax.optimization_barrier((g0, own_v))
-    cut = lambda value, c: value[firsts[c] : firsts[c] + CHUNKS[c]]
-    above = [over(cut(own_v, c), UP_Z) for c in range(2)]
+    above = over(own_v, UP_Z)
     g1, g3 = over(g0, Y_DOWN), over(g0, Y_UP)
+    g1, g3, own_k, last = lax.optimization_barrier((g1, g3, own_k, last))
+    back2 = over(last, shift_route(2))
     gs = [g0, g1, g3, over(g1, Y_DOWN)]
-    gs, above[0], own_k, own_v, last = lax.optimization_barrier(
-        (gs, above[0], own_k, own_v, last)
-    )
-    own = (own_k, own_v)
-    far_ok = far_bias(s)
-
-    def first_stage(c, own_k, own_v, gs):
-        h0 = jnp.concatenate([cut(g, c) for g in gs], axis=2)
-        h1, h3 = over(h0, Z_DOWN), over(h0, Z_UP)
-        back_k = over(cut(own_k, c), shift_route(1))
-        along = over(cut(own_v, c), ALONG_Y)
-        return h0, h1, h3, back_k, along
-
-    def second_stage(above, h0, h1, h3, back_k, along):
-        h2 = over(h1, Z_DOWN)
-        back_v = jnp.where(s % 4 == 0, over(above, ROUND_Y), along)
-        return (far_ok, *own, back_k, back_v, back2, h0, h1, h3, h2)
-
+    own_v, gs, above, back2 = lax.optimization_barrier((own_v, gs, above, back2))
+    back_k = over(own_k, shift_route(1))
+    back_v = jnp.where(s % 4 == 0, over(above, ROUND_Y), over(own_v, ALONG_Y))
+    h0 = jnp.concatenate(gs, axis=2)
+    h1, h3 = over(h0, Z_DOWN), over(h0, Z_UP)
+    h1, back_k = lax.optimization_barrier((h1, back_k))
+    fars = [h0, h1, h3, over(h1, Z_DOWN)]
+    parts = (far_bias(s), own_k, own_v, back_k, back_v, back2, *fars)
     pieces = {}
-
-    def run(c, half, parts):
-        which, names = ((1 - pair, (2, 3)), (pair, (0, 1)))[half]
-        info = jnp.stack([s, which, flip])
-        work = WORK if c else 1
-        outs = attend(work, firsts[c], CHUNKS[c], info, queries, key_rows, value_rows, *parts)
-        for k, out in zip(names, outs):
-            pieces[c, k] = swap_heads(out, k) if k else out
-        return outs[0]
-
-    stage = first_stage(0, own_k, own_v, gs)
-    back2 = over(last, shift_route(2))
-    sent, h1 = lax.optimization_barrier(((own_k, own_v, gs), stage[1]))
-    parts = second_stage(above[0], stage[0], h1, *stage[2:])
-    stage = first_stage(1, *sent)
-    done = run(0, 0, parts)
-    parts_b = second_stage(above[1], *stage)
-    far_ok, done = lax.optimization_barrier((parts[0], done))
-    done = run(0, 1, (far_ok, *parts[1:]))
-    far_ok, done, pieces[0, 2] = lax.optimization_barrier((parts_b[0], done, pieces[0, 2]))
-    done = run(1, 0, (far_ok, *parts_b[1:]))
-    far_ok, done, pieces[0, 3] = lax.optimization_barrier((far_ok, done, pieces[0, 3]))
-    run(1, 1, (far_ok, *parts_b[1:]))
+    args = (queries, key_rows, value_rows)
+    for which, names in ((1 - pair, (2, 3)), (pair, (0, 1))):
+        for c, (first, heads) in enumerate(zip(firsts, CHUNKS)):
+            outs = attend(first, heads, jnp.stack([s, which, flip]), *args, *parts)
+            for k, out in zip(names, outs):
+                pieces[c, k] = swap_heads(out, k) if k else out
+            args = lax.optimization_barrier((*args, outs[0]))[:3]
     order = sorted(pieces, key=lambda at: (at[0], at[1]))
     return place(
         me.reshape(1), [pieces[at] for at in order], [(k, firsts[c] * HD) for c, k in order]

time: 189 us -> 174 us (0.921)
  the two profiles are of different devices: /device:TPU:29 before, /device:TPU:5 now
where the time goes in v3:
time: 174 us
  Pallas kernels  66.6 us (38%)
  waiting for transfers between devices  63.5 us (36%)
  starting transfers between devices  35.8 us (21%)
  other arithmetic  5.03 us (3%)
  local copies, waits for them, and re-layouts  2.26 us (1%)
    ppermute x12, waiting for transfers between devices, shards(): over = lambda value, route: lax.ppermute(value, 'seq', route)  59.9 us
    pallas_call x4, Pallas kernels, attend(): pl.pallas_call(attend_kernel, grid_spec=pltpu.PrefetchScalarGridSpec(num_...  56.9 us
    ppermute x12, starting transfers between devices, shards(): over = lambda value, route: lax.ppermute(value, 'seq', route)  30.6 us
    pallas_call x1, Pallas kernels, pool(): pl.pallas_call(pool_kernel, grid=(heads // step,), in_specs=[pl.BlockSpec...  6.13 us
    ppermute x6, starting transfers between devices, swap_heads(): return lax.ppermute(piece, 'head', [(i, i ^ k) for i in range(4)])  5.25 us
    ppermute x6, waiting for transfers between devices, swap_heads(): return lax.ppermute(piece, 'head', [(i, i ^ k) for i in range(4)])  3.6 us
    pallas_call x1, Pallas kernels, place(): pl.pallas_call(lambda *refs: place_kernel(columns, *refs), in_specs=[pl.B...  3.57 us
  transfers between devices with their start and end apart: 18, of which 7 were waited for; matrix products, arithmetic and copies ran while one was open for 2% of the time, Pallas kernels for 25%

profile of v3, /device:TPU:5, one launch (start us, length us, event | category | flops | bytes accessed | tf_op | source)
XLA Modules:
  0.0 173.6 jit_solution(9965202315830746608)
XLA Ops:
  0.0 6.1 %pool.1 = (bf16[8,512,128]{2,1,0:T(8,128)(2,1)}, bf16[8,512,128]{2,1,0:T(8,128)(2,1)}, bf16[8,2,128,128]{3,2,1,0:T(8,128)(2,1)}, bf16[8,2,32,128]{3,2,1,0:T(8,128)(2,1)}) custom-call(bf16[2048,1024]{1,0:T(8,128)(2,1)} %kp_ref.4, bf16[2048,1024]{1,0:T(8,128)(2,1)} %vp_ref.4), custom_call_target="tpu_custom_call" | custom-call | flops 402653184 | bytes 12582912 | tf_op jit(solution)/shard_map/pool/pallas_call | solution.py:84
  6.1 6.1 %collective-permute-done = bf16[8,2,32,128]{3,2,1,0:T(8,128)(2,1)S(1)} collective-permute-done((bf16[8,2,32,128]{3,2,1,0:T(8,128)(2,1)}, bf16[8,2,32,128]{3,2,1,0:T(8,128)(2,1)S(1)}, u32[]{:S(2)}, u32[]{:S(2)}) %collective-permute-start) | collective-permute-done | bytes 131104 | tf_op jit(solution)/shard_map/ppermute | solution.py:294
  13.1 1.6 collective-permute-start.4
  14.8 1.3 collective-permute-start.2
  16.1 3.5 %collective-permute-start.1 = (bf16[8,2,64,128]{3,2,1,0:T(8,128)(2,1)S(1)}, bf16[8,2,64,128]{3,2,1,0:T(8,128)(2,1)S(1)}, u32[]{:S(2)}, u32[]{:S(2)}) collective-permute-start(bf16[8,2,64,128]{3,2,1,0:T(8,128)(2,1)S(1)} %pad_maximum_fusion), channel_id=1, source_target_pairs={{0,12},{4,0},{8,4},{12,8},{16,28},{20,16},{24,20},{28,24},{32,44},... | collective-permute-start | bytes 786440 | tf_op jit(solution)/shard_map/ppermute | solution.py:294
  19.6 4.7 %collective-permute-done.2 = bf16[8,2,64,128]{3,2,1,0:T(8,128)(2,1)S(1)} collective-permute-done((bf16[8,2,64,128]{3,2,1,0:T(8,128)(2,1)S(1)}, bf16[8,2,64,128]{3,2,1,0:T(8,128)(2,1)S(1)}, u32[]{:S(2)}, u32[]{:S(2)}) %collective-permute-start.2) | collective-permute-done | bytes 262176 | tf_op jit(solution)/shard_map/ppermute | solution.py:294
  24.3 4.0 %collective-permute-start.5 = (bf16[8,2,128,128]{3,2,1,0:T(8,128)(2,1)}, bf16[8,2,128,128]{3,2,1,0:T(8,128)(2,1)S(1)}, u32[]{:S(2)}, u32[]{:S(2)}) collective-permute-start(bf16[8,2,128,128]{3,2,1,0:T(8,128)(2,1)} %get-tuple-element.50), channel_id=1, source_target_pairs={{0,8},{4,12},{8,16},{12,20},{16,24},{20,28},{24,32},{28,36},{32,40... | collective-permute-start | bytes 1572872 | tf_op jit(solution)/shard_map/ppermute | solution.py:294
  28.3 2.3 %collective-permute-start.3 = (bf16[8,2,64,128]{3,2,1,0:T(8,128)(2,1)S(1)}, bf16[8,2,64,128]{3,2,1,0:T(8,128)(2,1)S(1)}, u32[]{:S(2)}, u32[]{:S(2)}) collective-permute-start(bf16[8,2,64,128]{3,2,1,0:T(8,128)(2,1)S(1)} %collective-permute-done.1), channel_id=1, source_target_pairs={{0,12},{4,0},{8,4},{12,8},{16,28},{20,16},{24,20},{28,24},{32,44},... | collective-permute-start | bytes 786440 | tf_op jit(solution)/shard_map/ppermute | solution.py:294
  30.6 1.9 %collective-permute-start.7 = (bf16[8,512,128]{2,1,0:T(8,128)(2,1)}, bf16[8,512,128]{2,1,0:T(8,128)(2,1)S(1)}, u32[]{:S(2)}, u32[]{:S(2)}) collective-permute-start(bf16[8,512,128]{2,1,0:T(8,128)(2,1)} %get-tuple-element.46.own_k_ref), channel_id=1, source_target_pairs={{0,4},{4,8},{8,12},{12,16},{16,20},{20,24},{24,28},{28,32},{32,36}... | collective-permute-start | bytes 3145736 | tf_op jit(solution)/shard_map/ppermute | solution.py:294
  32.5 14.0 %collective-permute-done.3 = bf16[8,2,64,128]{3,2,1,0:T(8,128)(2,1)S(1)} collective-permute-done((bf16[8,2,64,128]{3,2,1,0:T(8,128)(2,1)S(1)}, bf16[8,2,64,128]{3,2,1,0:T(8,128)(2,1)S(1)}, u32[]{:S(2)}, u32[]{:S(2)}) %collective-permute-start.3) | collective-permute-done | bytes 262176 | tf_op jit(solution)/shard_map/ppermute | solution.py:294
  47.6 1.3 collective-permute-start.8
  48.9 13.1 %collective-permute-start.9 = (bf16[8,512,128]{2,1,0:T(8,128)(2,1)}, bf16[8,512,128]{2,1,0:T(8,128)(2,1)}, u32[]{:S(2)}, u32[]{:S(2)}) collective-permute-start(bf16[8,512,128]{2,1,0:T(8,128)(2,1)} %get-tuple-element.51.own_v_ref), channel_id=1, source_target_pairs={{0,4},{4,8},{8,12},{16,20},{20,24},{24,28},{32,36},{36,40},{40,44}... | collective-permute-start | bytes 3145736 | tf_op jit(solution)/shard_map/ppermute | solution.py:294
  62.1 1.4 collective-permute-start.10
  63.5 14.7 %collective-permute-done.7.back_k_ref = bf16[8,512,128]{2,1,0:T(8,128)(2,1)S(1)} collective-permute-done((bf16[8,512,128]{2,1,0:T(8,128)(2,1)}, bf16[8,512,128]{2,1,0:T(8,128)(2,1)S(1)}, u32[]{:S(2)}, u32[]{:S(2)}) %collective-permute-start.7) | collective-permute-done | bytes 1048608 | tf_op jit(solution)/shard_map/ppermute | solution.py:294
  80.1 7.5 %collective-permute-done.8 = bf16[8,512,128]{2,1,0:T(8,128)(2,1)} collective-permute-done((bf16[8,512,128]{2,1,0:T(8,128)(2,1)}, bf16[8,512,128]{2,1,0:T(8,128)(2,1)}, u32[]{:S(2)}, u32[]{:S(2)}) %collective-permute-start.8) | collective-permute-done | bytes 1048608 | tf_op jit(solution)/shard_map/ppermute | solution.py:294
  87.5 2.3 %broadcast_select_fusion.back_v_ref = bf16[8,512,128]{2,1,0:T(8,128)(2,1)} fusion(bf16[8,512,128]{2,1,0:T(8,128)(2,1)} %collective-permute-done.8, bf16[8,512,128]{2,1,0:T(8,128)(2,1)} %collective-permute-done.9, pred[]{:T(512)S(6)} %eq.11), kind=kLoop, calls=%fused_computation | loop fusion | flops 524288 | bytes 3145729 | tf_op jit(solution)/shard_map/jit(_where)/select_n | solution.py:306
  89.8 12.9 %collective-permute-done.10.h2_ref = bf16[8,2,256,128]{3,2,1,0:T(8,128)(2,1)} collective-permute-done((bf16[8,2,256,128]{3,2,1,0:T(8,128)(2,1)S(1)}, bf16[8,2,256,128]{3,2,1,0:T(8,128)(2,1)}, u32[]{:S(2)}, u32[]{:S(2)}) %collective-permute-start.10) | collective-permute-done | bytes 1048608 | tf_op jit(solution)/shard_map/ppermute | solution.py:294
  102.8 14.2 %attend.4 = (bf16[512,512]{1,0:T(8,128)(2,1)}, bf16[512,512]{1,0:T(8,128)(2,1)}) custom-call(s32[3]{0:T(128)} %get-tuple-element.80.info_ref, bf16[2048,1024]{1,0:T(8,128)(2,1)} %q_ref.4, bf16[2048,1024]{1,0:T(8,128)(2,1)} %kp_ref.4, bf16[2048,1024]{1,0:T(8,128)(2,1)} %vp_ref.4, bf16[2048,1024]{1,0:T(8,128)(2,1)} %kp_ref.4, bf16[2048,1024]{1,0:T(8,128)(2,1)} %vp_ref.4, ...), custom_call_target="tpu_custom_call" | custom-call | flops 8053063680 | bytes 6144000 | tf_op jit(solution)/shard_map/attend/pallas_call | solution.py:203
  118.0 14.2 %attend.5 = (bf16[512,512]{1,0:T(8,128)(2,1)}, bf16[512,512]{1,0:T(8,128)(2,1)}) custom-call(s32[3]{0:T(128)} %get-tuple-element.80.info_ref, bf16[2048,1024]{1,0:T(8,128)(2,1)} %q_ref.4, bf16[2048,1024]{1,0:T(8,128)(2,1)} %kp_ref.4, bf16[2048,1024]{1,0:T(8,128)(2,1)} %vp_ref.4, bf16[2048,1024]{1,0:T(8,128)(2,1)} %kp_ref.4, bf16[2048,1024]{1,0:T(8,128)(2,1)} %vp_ref.4, ...), custom_call_target="tpu_custom_call" | custom-call | flops 8053063680 | bytes 6144000 | tf_op jit(solution)/shard_map/attend/pallas_call | solution.py:203
  132.8 2.5 %collective-permute-start.14 = (bf16[512,512]{1,0:T(8,128)(2,1)S(1)}, bf16[512,512]{1,0:T(8,128)(2,1)S(1)}, u32[]{:S(2)}, u32[]{:S(2)}) collective-permute-start(bf16[512,512]{1,0:T(8,128)(2,1)S(1)} %copy-done.11), channel_id=1, source_target_pairs={{0,3},{1,2},{2,1},{3,0},{4,7},{5,6},{6,5},{7,4},{8,11},{9,10},{10,... | collective-permute-start | bytes 1572872 | tf_op jit(solution)/shard_map/ppermute | solution.py:276
  135.3 14.2 %attend.6 = (bf16[512,512]{1,0:T(8,128)(2,1)}, bf16[512,512]{1,0:T(8,128)(2,1)}) custom-call(s32[3]{0:T(128)} %get-tuple-element.79.info_ref, bf16[2048,1024]{1,0:T(8,128)(2,1)} %q_ref.4, bf16[2048,1024]{1,0:T(8,128)(2,1)} %kp_ref.4, bf16[2048,1024]{1,0:T(8,128)(2,1)} %vp_ref.4, bf16[2048,1024]{1,0:T(8,128)(2,1)} %kp_ref.4, bf16[2048,1024]{1,0:T(8,128)(2,1)} %vp_ref.4, ...), custom_call_target="tpu_custom_call" | custom-call | flops 8053063680 | bytes 6144000 | tf_op jit(solution)/shard_map/attend/pallas_call | solution.py:203
  149.5 14.4 %attend.7 = (bf16[512,512]{1,0:T(8,128)(2,1)}, bf16[512,512]{1,0:T(8,128)(2,1)}) custom-call(s32[3]{0:T(128)} %get-tuple-element.79.info_ref, bf16[2048,1024]{1,0:T(8,128)(2,1)} %q_ref.4, bf16[2048,1024]{1,0:T(8,128)(2,1)} %kp_ref.4, bf16[2048,1024]{1,0:T(8,128)(2,1)} %vp_ref.4, bf16[2048,1024]{1,0:T(8,128)(2,1)} %kp_ref.4, bf16[2048,1024]{1,0:T(8,128)(2,1)} %vp_ref.4, ...), custom_call_target="tpu_custom_call" | custom-call | flops 8053063680 | bytes 6144000 | tf_op jit(solution)/shard_map/attend/pallas_call | solution.py:203
  165.0 3.6 %collective-permute-done.17.refs_8_ = bf16[512,512]{1,0:T(8,128)(2,1)S(1)} collective-permute-done((bf16[512,512]{1,0:T(8,128)(2,1)}, bf16[512,512]{1,0:T(8,128)(2,1)S(1)}, u32[]{:S(2)}, u32[]{:S(2)}) %collective-permute-start.17) | collective-permute-done | bytes 524320 | tf_op jit(solution)/shard_map/ppermute | solution.py:276
  169.9 3.6 %place.1 = bf16[512,4096]{1,0:T(8,128)(2,1)} custom-call(s32[1]{0:T(128)} %bitcast.refs_0_, bf16[512,512]{1,0:T(8,128)(2,1)} %get-tuple-element.68.refs_1_, bf16[512,512]{1,0:T(8,128)(2,1)} %copy-done.9, bf16[512,512]{1,0:T(8,128)(2,1)} %copy-done.4, bf16[512,512]{1,0:T(8,128)(2,1)} %copy-done.6, bf16[512,512]{1,0:T(8,128)(2,1)} %get-tuple-element.74.refs_5_, ...), custom_call_target="tpu_custom_call" | custom-call | bytes 8388608 | tf_op jit(solution)/shard_map/place/pallas_call | solution.py:256
  (59 shorter events, 8.0 us)
Async XLA Ops:
  0.0 47.6 %copy-start.10 = (s32[4]{0:T(128)S(1)}, s32[4]{0:T(128)}, u32[]{:S(2)}) copy-start(s32[4]{0:T(128)} %constant.99.clone) | copy-start | bytes 52
  6.1 6.1 %collective-permute-start = (bf16[8,2,32,128]{3,2,1,0:T(8,128)(2,1)}, bf16[8,2,32,128]{3,2,1,0:T(8,128)(2,1)S(1)}, u32[]{:S(2)}, u32[]{:S(2)}) collective-permute-start(bf16[8,2,32,128]{3,2,1,0:T(8,128)(2,1)} %get-tuple-element.41), channel_id=1, source_target_pairs={{0,64},{4,68},{8,72},{12,76},{16,80},{20,84},{24,88},{28,92},{32,9... | collective-permute-start | bytes 393224 | tf_op jit(solution)/shard_map/ppermute | solution.py:294
  13.1 34.2 %collective-permute-start.4 = (bf16[8,512,128]{2,1,0:T(8,128)(2,1)}, bf16[8,512,128]{2,1,0:T(8,128)(2,1)}, u32[]{:S(2)}, u32[]{:S(2)}) collective-permute-start(bf16[8,512,128]{2,1,0:T(8,128)(2,1)} %get-tuple-element.51.own_v_ref), channel_id=1, source_target_pairs={{12,28},{28,44},{44,60},{60,76},{76,92},{92,108},{108,124},{13,29}... | collective-permute-start | bytes 3145736 | tf_op jit(solution)/shard_map/ppermute | solution.py:294
  14.8 9.5 %collective-permute-start.2 = (bf16[8,2,64,128]{3,2,1,0:T(8,128)(2,1)S(1)}, bf16[8,2,64,128]{3,2,1,0:T(8,128)(2,1)S(1)}, u32[]{:S(2)}, u32[]{:S(2)}) collective-permute-start(bf16[8,2,64,128]{3,2,1,0:T(8,128)(2,1)S(1)} %pad_maximum_fusion), channel_id=1, source_target_pairs={{0,4},{4,8},{8,12},{12,0},{16,20},{20,24},{24,28},{28,16},{32,36},... | collective-permute-start | bytes 786440 | tf_op jit(solution)/shard_map/ppermute | solution.py:294
  16.1 8.2 %collective-permute-start.1 = (bf16[8,2,64,128]{3,2,1,0:T(8,128)(2,1)S(1)}, bf16[8,2,64,128]{3,2,1,0:T(8,128)(2,1)S(1)}, u32[]{:S(2)}, u32[]{:S(2)}) collective-permute-start(bf16[8,2,64,128]{3,2,1,0:T(8,128)(2,1)S(1)} %pad_maximum_fusion), channel_id=1, source_target_pairs={{0,12},{4,0},{8,4},{12,8},{16,28},{20,16},{24,20},{28,24},{32,44},... | collective-permute-start | bytes 786440 | tf_op jit(solution)/shard_map/ppermute | solution.py:294
  24.3 22.2 %collective-permute-start.5 = (bf16[8,2,128,128]{3,2,1,0:T(8,128)(2,1)}, bf16[8,2,128,128]{3,2,1,0:T(8,128)(2,1)S(1)}, u32[]{:S(2)}, u32[]{:S(2)}) collective-permute-start(bf16[8,2,128,128]{3,2,1,0:T(8,128)(2,1)} %get-tuple-element.50), channel_id=1, source_target_pairs={{0,8},{4,12},{8,16},{12,20},{16,24},{20,28},{24,32},{28,36},{32,40... | collective-permute-start | bytes 1572872 | tf_op jit(solution)/shard_map/ppermute | solution.py:294
  28.3 18.2 %collective-permute-start.3 = (bf16[8,2,64,128]{3,2,1,0:T(8,128)(2,1)S(1)}, bf16[8,2,64,128]{3,2,1,0:T(8,128)(2,1)S(1)}, u32[]{:S(2)}, u32[]{:S(2)}) collective-permute-start(bf16[8,2,64,128]{3,2,1,0:T(8,128)(2,1)S(1)} %collective-permute-done.1), channel_id=1, source_target_pairs={{0,12},{4,0},{8,4},{12,8},{16,28},{20,16},{24,20},{28,24},{32,44},... | collective-permute-start | bytes 786440 | tf_op jit(solution)/shard_map/ppermute | solution.py:294
  30.6 47.6 %collective-permute-start.7 = (bf16[8,512,128]{2,1,0:T(8,128)(2,1)}, bf16[8,512,128]{2,1,0:T(8,128)(2,1)S(1)}, u32[]{:S(2)}, u32[]{:S(2)}) collective-permute-start(bf16[8,512,128]{2,1,0:T(8,128)(2,1)} %get-tuple-element.46.own_k_ref), channel_id=1, source_target_pairs={{0,4},{4,8},{8,12},{12,16},{16,20},{20,24},{24,28},{28,32},{32,36}... | collective-permute-start | bytes 3145736 | tf_op jit(solution)/shard_map/ppermute | solution.py:294
  47.5 55.3 %copy-start = (bf16[8,2,256,128]{3,2,1,0:T(8,128)(2,1)}, bf16[8,2,256,128]{3,2,1,0:T(8,128)(2,1)S(1)}, u32[]{:S(2)}) copy-start(bf16[8,2,256,128]{3,2,1,0:T(8,128)(2,1)S(1)} %constant_dynamic-update-slice_fusion.h0_ref) | copy-start | bytes 3145732
  47.5 30.7 %collective-permute-start.6 = (bf16[8,2,256,128]{3,2,1,0:T(8,128)(2,1)S(1)}, bf16[8,2,256,128]{3,2,1,0:T(8,128)(2,1)S(1)}, u32[]{:S(2)}, u32[]{:S(2)}) collective-permute-start(bf16[8,2,256,128]{3,2,1,0:T(8,128)(2,1)S(1)} %constant_dynamic-update-slice_fusion.h0_ref), channel_id=1, source_target_pairs={{0,48},{4,52},{8,56},{12,60},{16,0},{20,4},{24,8},{28,12},{32,16},... | collective-permute-start | bytes 3145736 | tf_op jit(solution)/shard_map/ppermute | solution.py:294
  47.6 39.9 %collective-permute-start.8 = (bf16[8,512,128]{2,1,0:T(8,128)(2,1)}, bf16[8,512,128]{2,1,0:T(8,128)(2,1)}, u32[]{:S(2)}, u32[]{:S(2)}) collective-permute-start(bf16[8,512,128]{2,1,0:T(8,128)(2,1)} %collective-permute-done.4), channel_id=1, source_target_pairs={{28,16},{44,32},{60,48},{76,64},{92,80},{108,96},{124,112},{29,17}... | collective-permute-start | bytes 3145736 | tf_op jit(solution)/shard_map/ppermute | solution.py:294
  48.9 38.6 %collective-permute-start.9 = (bf16[8,512,128]{2,1,0:T(8,128)(2,1)}, bf16[8,512,128]{2,1,0:T(8,128)(2,1)}, u32[]{:S(2)}, u32[]{:S(2)}) collective-permute-start(bf16[8,512,128]{2,1,0:T(8,128)(2,1)} %get-tuple-element.51.own_v_ref), channel_id=1, source_target_pairs={{0,4},{4,8},{8,12},{16,20},{20,24},{24,28},{32,36},{36,40},{40,44}... | collective-permute-start | bytes 3145736 | tf_op jit(solution)/shard_map/ppermute | solution.py:294
  62.1 40.7 %collective-permute-start.10 = (bf16[8,2,256,128]{3,2,1,0:T(8,128)(2,1)S(1)}, bf16[8,2,256,128]{3,2,1,0:T(8,128)(2,1)}, u32[]{:S(2)}, u32[]{:S(2)}) collective-permute-start(bf16[8,2,256,128]{3,2,1,0:T(8,128)(2,1)S(1)} %constant_dynamic-update-slice_fusion.h0_ref), channel_id=1, source_target_pairs={{0,16},{4,20},{8,24},{12,28},{16,32},{20,36},{24,40},{28,44},{32,4... | collective-permute-start | bytes 3145736 | tf_op jit(solution)/shard_map/ppermute | solution.py:294
  78.2 24.6 %copy-start.1 = (bf16[8,512,128]{2,1,0:T(8,128)(2,1)}, bf16[8,512,128]{2,1,0:T(8,128)(2,1)S(1)}, u32[]{:S(2)}) copy-start(bf16[8,512,128]{2,1,0:T(8,128)(2,1)S(1)} %collective-permute-done.7.back_k_ref) | copy-start | bytes 3145732
  78.2 24.6 %copy-start.2 = (bf16[8,2,256,128]{3,2,1,0:T(8,128)(2,1)}, bf16[8,2,256,128]{3,2,1,0:T(8,128)(2,1)S(1)}, u32[]{:S(2)}) copy-start(bf16[8,2,256,128]{3,2,1,0:T(8,128)(2,1)S(1)} %collective-permute-done.6.h1_ref) | copy-start | bytes 3145732
  78.2 24.6 %collective-permute-start.11 = (bf16[8,2,256,128]{3,2,1,0:T(8,128)(2,1)S(1)}, bf16[8,2,256,128]{3,2,1,0:T(8,128)(2,1)}, u32[]{:S(2)}, u32[]{:S(2)}) collective-permute-start(bf16[8,2,256,128]{3,2,1,0:T(8,128)(2,1)S(1)} %collective-permute-done.6.h1_ref), channel_id=1, source_target_pairs={{0,48},{4,52},{8,56},{12,60},{16,0},{20,4},{24,8},{28,12},{32,16},... | collective-permute-start | bytes 3145736 | tf_op jit(solution)/shard_map/ppermute | solution.py:294
  117.0 15.8 %copy-start.11 = (bf16[512,512]{1,0:T(8,128)(2,1)S(1)}, bf16[512,512]{1,0:T(8,128)(2,1)}, u32[]{:S(2)}) copy-start(bf16[512,512]{1,0:T(8,128)(2,1)} %get-tuple-element.70) | copy-start | bytes 1572868
  117.0 48.0 %collective-permute-start.13 = (bf16[512,512]{1,0:T(8,128)(2,1)}, bf16[512,512]{1,0:T(8,128)(2,1)S(1)}, u32[]{:S(2)}, u32[]{:S(2)}) collective-permute-start(bf16[512,512]{1,0:T(8,128)(2,1)} %get-tuple-element.60), channel_id=1, source_target_pairs={{0,2},{1,3},{2,0},{3,1},{4,6},{5,7},{6,4},{7,5},{8,10},{9,11},{10,... | collective-permute-start | bytes 1572872 | tf_op jit(solution)/shard_map/ppermute | solution.py:276
  132.2 36.4 %collective-permute-start.16 = (bf16[512,512]{1,0:T(8,128)(2,1)}, bf16[512,512]{1,0:T(8,128)(2,1)S(1)}, u32[]{:S(2)}, u32[]{:S(2)}) collective-permute-start(bf16[512,512]{1,0:T(8,128)(2,1)} %get-tuple-element.64), channel_id=1, source_target_pairs={{0,2},{1,3},{2,0},{3,1},{4,6},{5,7},{6,4},{7,5},{8,10},{9,11},{10,... | collective-permute-start | bytes 1572872 | tf_op jit(solution)/shard_map/ppermute | solution.py:276
  132.8 32.1 %collective-permute-start.14 = (bf16[512,512]{1,0:T(8,128)(2,1)S(1)}, bf16[512,512]{1,0:T(8,128)(2,1)S(1)}, u32[]{:S(2)}, u32[]{:S(2)}) collective-permute-start(bf16[512,512]{1,0:T(8,128)(2,1)S(1)} %copy-done.11), channel_id=1, source_target_pairs={{0,3},{1,2},{2,1},{3,0},{4,7},{5,6},{6,5},{7,4},{8,11},{9,10},{10,... | collective-permute-start | bytes 1572872 | tf_op jit(solution)/shard_map/ppermute | solution.py:276
  135.3 33.3 %collective-permute-start.17 = (bf16[512,512]{1,0:T(8,128)(2,1)}, bf16[512,512]{1,0:T(8,128)(2,1)S(1)}, u32[]{:S(2)}, u32[]{:S(2)}) collective-permute-start(bf16[512,512]{1,0:T(8,128)(2,1)} %get-tuple-element.76), channel_id=1, source_target_pairs={{0,3},{1,2},{2,1},{3,0},{4,7},{5,6},{6,5},{7,4},{8,11},{9,10},{10,... | collective-permute-start | bytes 1572872 | tf_op jit(solution)/shard_map/ppermute | solution.py:276
  149.5 15.4 %copy-start.12 = (bf16[512,512]{1,0:T(8,128)(2,1)S(1)}, bf16[512,512]{1,0:T(8,128)(2,1)}, u32[]{:S(2)}) copy-start(bf16[512,512]{1,0:T(8,128)(2,1)} %get-tuple-element.69) | copy-start | bytes 1572868
  163.9 4.7 %collective-permute-start.15 = (bf16[512,512]{1,0:T(8,128)(2,1)}, bf16[512,512]{1,0:T(8,128)(2,1)S(1)}, u32[]{:S(2)}, u32[]{:S(2)}) collective-permute-start(bf16[512,512]{1,0:T(8,128)(2,1)} %get-tuple-element.75), channel_id=1, source_target_pairs={{0,1},{1,0},{2,3},{3,2},{4,5},{5,4},{6,7},{7,6},{8,9},{9,8},{10,11... | collective-permute-start | bytes 1572872 | tf_op jit(solution)/shard_map/ppermute | solution.py:276
  164.9 3.7 %collective-permute-start.12 = (bf16[512,512]{1,0:T(8,128)(2,1)S(1)}, bf16[512,512]{1,0:T(8,128)(2,1)S(1)}, u32[]{:S(2)}, u32[]{:S(2)}) collective-permute-start(bf16[512,512]{1,0:T(8,128)(2,1)S(1)} %copy-done.12), channel_id=1, source_target_pairs={{0,1},{1,0},{2,3},{3,2},{4,5},{5,4},{6,7},{7,6},{8,9},{9,8},{10,11... | collective-permute-start | bytes 1572872 | tf_op jit(solution)/shard_map/ppermute | solution.py:276
  (7 other events, 12.4 us)

commit v4 on v3

--- a/solution.py
+++ b/solution.py
@@ -209,7 +209,8 @@
             + [pl.BlockSpec((8, FARS), lambda h, info: (0, 0))]
             + [pl.BlockSpec((1, 2 * BLK, HD), lambda h, info: (first + h, 0, 0))] * 4
             + [head(128)]
-            + [head(256)] * 4,
+            + [head(256)] * 3
+            + [pl.BlockSpec((1, 2, 256, HD), lambda h, info: (h, 0, 0, 0))],
             out_specs=[out, out],
             scratch_shapes=[
                 pltpu.VMEM((1280, HD), BF),
@@ -299,22 +300,28 @@
     above = over(own_v, UP_Z)
     g1, g3 = over(g0, Y_DOWN), over(g0, Y_UP)
     g1, g3, own_k, last = lax.optimization_barrier((g1, g3, own_k, last))
+    gs = [g0, g1, g3, over(g1, Y_DOWN)]
+    own_v, gs, above, last = lax.optimization_barrier((own_v, gs, above, last))
     back2 = over(last, shift_route(2))
-    gs = [g0, g1, g3, over(g1, Y_DOWN)]
-    own_v, gs, above, back2 = lax.optimization_barrier((own_v, gs, above, back2))
     back_k = over(own_k, shift_route(1))
     back_v = jnp.where(s % 4 == 0, over(above, ROUND_Y), over(own_v, ALONG_Y))
     h0 = jnp.concatenate(gs, axis=2)
     h1, h3 = over(h0, Z_DOWN), over(h0, Z_UP)
     h1, back_k = lax.optimization_barrier((h1, back_k))
-    fars = [h0, h1, h3, over(h1, Z_DOWN)]
-    parts = (far_bias(s), own_k, own_v, back_k, back_v, back2, *fars)
+    h3, back2 = lax.optimization_barrier((h3, back2))
+    split = CHUNKS[0]
+    h2 = (over(h1[:split], Z_DOWN), over(h3[split:], Z_UP))
+    parts = (far_bias(s), own_k, own_v, back_k, back_v, back2, h0, h1, h3)
     pieces = {}
     args = (queries, key_rows, value_rows)
     for which, names in ((1 - pair, (2, 3)), (pair, (0, 1))):
         for c, (first, heads) in enumerate(zip(firsts, CHUNKS)):
-            outs = attend(first, heads, jnp.stack([s, which, flip]), *args, *parts)
+            outs = attend(first, heads, jnp.stack([s, which, flip]), *args, *parts, h2[c])
             for k, out in zip(names, outs):
+                if (c, k) == (1, 1):
+                    out, pieces[1, 2], pieces[1, 3] = lax.optimization_barrier(
+                        (out, pieces[1, 2], pieces[1, 3])
+                    )
                 pieces[c, k] = swap_heads(out, k) if k else out
             args = lax.optimization_barrier((*args, outs[0]))[:3]
     order = sorted(pieces, key=lambda at: (at[0], at[1]))

time: 174 us -> 175 us (level)
  the two profiles are of different devices: /device:TPU:5 before, /device:TPU:101 now
where the time goes in v4:
time: 175 us; the launch traced here: 174 us
  waiting for transfers between devices  71.4 us (41%)
  Pallas kernels  66.7 us (38%)
  starting transfers between devices  25.6 us (15%)
  local copies, waits for them, and re-layouts  6.74 us (4%)
  other arithmetic  3.6 us (2%)
    ppermute x13, waiting for transfers between devices, shards(): over = lambda value, route: lax.ppermute(value, 'seq', route)  65 us
    pallas_call x4, Pallas kernels, attend(): pl.pallas_call(attend_kernel, grid_spec=pltpu.PrefetchScalarGridSpec(num_...  57 us
    ppermute x13, starting transfers between devices, shards(): over = lambda value, route: lax.ppermute(value, 'seq', route)  21 us
    ppermute x6, waiting for transfers between devices, swap_heads(): return lax.ppermute(piece, 'head', [(i, i ^ k) for i in range(4)])  6.37 us
    pallas_call x1, Pallas kernels, pool(): pl.pallas_call(pool_kernel, grid=(heads // step,), in_specs=[pl.BlockSpec...  6.12 us
    unnamed x27, local copies, waits for them, and re-layouts  4.77 us
    ppermute x6, starting transfers between devices, swap_heads(): return lax.ppermute(piece, 'head', [(i, i ^ k) for i in range(4)])  4.57 us
    pallas_call x1, Pallas kernels, place(): pl.pallas_call(lambda *refs: place_kernel(columns, *refs), in_specs=[pl.B...  3.57 us
  transfers between devices with their start and end apart: 19, of which 9 were waited for; matrix products, arithmetic and copies ran while one was open for 4% of the time, Pallas kernels for 33%

profile of v4, /device:TPU:101, one launch (start us, length us, event | category | flops | bytes accessed | tf_op | source)
XLA Modules:
  0.0 174.4 jit_solution(13903014743257337729)
XLA Ops:
  0.0 6.1 %pool.1 = (bf16[8,512,128]{2,1,0:T(8,128)(2,1)}, bf16[8,512,128]{2,1,0:T(8,128)(2,1)}, bf16[8,2,128,128]{3,2,1,0:T(8,128)(2,1)}, bf16[8,2,32,128]{3,2,1,0:T(8,128)(2,1)}) custom-call(bf16[2048,1024]{1,0:T(8,128)(2,1)} %kp_ref.4, bf16[2048,1024]{1,0:T(8,128)(2,1)} %vp_ref.4), custom_call_target="tpu_custom_call" | custom-call | flops 402653184 | bytes 12582912 | tf_op jit(solution)/shard_map/pool/pallas_call | solution.py:84
  6.4 5.9 %collective-permute-done = bf16[8,2,32,128]{3,2,1,0:T(8,128)(2,1)S(1)} collective-permute-done((bf16[8,2,32,128]{3,2,1,0:T(8,128)(2,1)}, bf16[8,2,32,128]{3,2,1,0:T(8,128)(2,1)S(1)}, u32[]{:S(2)}, u32[]{:S(2)}) %collective-permute-start) | collective-permute-done | bytes 131104 | tf_op jit(solution)/shard_map/ppermute | solution.py:295
  13.1 1.7 collective-permute-start.4
  16.1 1.4 collective-permute-start.1
  17.5 4.8 %collective-permute-done.2 = bf16[8,2,64,128]{3,2,1,0:T(8,128)(2,1)S(1)} collective-permute-done((bf16[8,2,64,128]{3,2,1,0:T(8,128)(2,1)S(1)}, bf16[8,2,64,128]{3,2,1,0:T(8,128)(2,1)S(1)}, u32[]{:S(2)}, u32[]{:S(2)}) %collective-permute-start.2) | collective-permute-done | bytes 262176 | tf_op jit(solution)/shard_map/ppermute | solution.py:295
  22.3 2.4 %collective-permute-start.3 = (bf16[8,2,64,128]{3,2,1,0:T(8,128)(2,1)S(1)}, bf16[8,2,64,128]{3,2,1,0:T(8,128)(2,1)S(1)}, u32[]{:S(2)}, u32[]{:S(2)}) collective-permute-start(bf16[8,2,64,128]{3,2,1,0:T(8,128)(2,1)S(1)} %collective-permute-done.1), channel_id=1, source_target_pairs={{0,12},{4,0},{8,4},{12,8},{16,28},{20,16},{24,20},{28,24},{32,44},... | collective-permute-start | bytes 786440 | tf_op jit(solution)/shard_map/ppermute | solution.py:295
  24.7 1.9 %collective-permute-start.6 = (bf16[8,512,128]{2,1,0:T(8,128)(2,1)}, bf16[8,512,128]{2,1,0:T(8,128)(2,1)}, u32[]{:S(2)}, u32[]{:S(2)}) collective-permute-start(bf16[8,512,128]{2,1,0:T(8,128)(2,1)} %get-tuple-element.51.own_k_ref), channel_id=1, source_target_pairs={{0,4},{4,8},{8,12},{12,16},{16,20},{20,24},{24,28},{28,32},{32,36}... | collective-permute-start | bytes 3145736 | tf_op jit(solution)/shard_map/ppermute | solution.py:295
  26.6 1.4 collective-permute-done.3
  31.1 1.9 %collective-permute-start.5 = (bf16[8,2,256,128]{3,2,1,0:T(8,128)(2,1)}, bf16[8,2,256,128]{3,2,1,0:T(8,128)(2,1)S(1)}, u32[]{:S(2)}, u32[]{:S(2)}) collective-permute-start(bf16[8,2,256,128]{3,2,1,0:T(8,128)(2,1)} %constant_dynamic-update-slice_fusion.h0_ref), channel_id=1, source_target_pairs={{0,48},{4,52},{8,56},{12,60},{16,0},{20,4},{24,8},{28,12},{32,16},... | collective-permute-start | bytes 3145736 | tf_op jit(solution)/shard_map/ppermute | solution.py:295
  35.2 2.0 %collective-permute-start.8 = (bf16[8,512,128]{2,1,0:T(8,128)(2,1)}, bf16[8,512,128]{2,1,0:T(8,128)(2,1)S(1)}, u32[]{:S(2)}, u32[]{:S(2)}) collective-permute-start(bf16[8,512,128]{2,1,0:T(8,128)(2,1)} %get-tuple-element.56.own_v_ref), channel_id=1, source_target_pairs={{0,4},{4,8},{8,12},{16,20},{20,24},{24,28},{32,36},{36,40},{40,44}... | collective-permute-start | bytes 3145736 | tf_op jit(solution)/shard_map/ppermute | solution.py:295
  37.4 13.3 %collective-permute-done.6.back_k_ref = bf16[8,512,128]{2,1,0:T(8,128)(2,1)} collective-permute-done((bf16[8,512,128]{2,1,0:T(8,128)(2,1)}, bf16[8,512,128]{2,1,0:T(8,128)(2,1)}, u32[]{:S(2)}, u32[]{:S(2)}) %collective-permute-start.6) | collective-permute-done | bytes 1048608 | tf_op jit(solution)/shard_map/ppermute | solution.py:295
  50.6 3.0 %collective-permute-start.10 = (bf16[8,2,128,128]{3,2,1,0:T(8,128)(2,1)}, bf16[8,2,128,128]{3,2,1,0:T(8,128)(2,1)}, u32[]{:S(2)}, u32[]{:S(2)}) collective-permute-start(bf16[8,2,128,128]{3,2,1,0:T(8,128)(2,1)} %get-tuple-element.63), channel_id=1, source_target_pairs={{0,8},{4,12},{8,16},{12,20},{16,24},{20,28},{24,32},{28,36},{32,40... | collective-permute-start | bytes 1572872 | tf_op jit(solution)/shard_map/ppermute | solution.py:295
  56.1 29.1 %collective-permute-done.10.back2_ref = bf16[8,2,128,128]{3,2,1,0:T(8,128)(2,1)} collective-permute-done((bf16[8,2,128,128]{3,2,1,0:T(8,128)(2,1)}, bf16[8,2,128,128]{3,2,1,0:T(8,128)(2,1)}, u32[]{:S(2)}, u32[]{:S(2)}) %collective-permute-start.10) | collective-permute-done | bytes 524320 | tf_op jit(solution)/shard_map/ppermute | solution.py:295
  85.3 2.5 %collective-permute-done.9.h2_ref = bf16[8,2,256,128]{3,2,1,0:T(8,128)(2,1)} collective-permute-done((bf16[8,2,256,128]{3,2,1,0:T(8,128)(2,1)}, bf16[8,2,256,128]{3,2,1,0:T(8,128)(2,1)}, u32[]{:S(2)}, u32[]{:S(2)}) %collective-permute-start.9) | collective-permute-done | bytes 1048608 | tf_op jit(solution)/shard_map/ppermute | solution.py:295
  88.8 2.2 %collective-permute-start.12 = (bf16[4,2,256,128]{3,2,1,0:T(8,128)(2,1)S(1)}, bf16[4,2,256,128]{3,2,1,0:T(8,128)(2,1)S(1)}, u32[]{:S(2)}, u32[]{:S(2)}) collective-permute-start(bf16[4,2,256,128]{3,2,1,0:T(8,128)(2,1)S(1)} %slice.7), channel_id=1, source_target_pairs={{0,16},{4,20},{8,24},{12,28},{16,32},{20,36},{24,40},{28,44},{32,4... | collective-permute-start | bytes 1572872 | tf_op jit(solution)/shard_map/ppermute | solution.py:295
  91.1 8.1 %collective-permute-done.7 = bf16[8,512,128]{2,1,0:T(8,128)(2,1)S(1)} collective-permute-done((bf16[8,512,128]{2,1,0:T(8,128)(2,1)}, bf16[8,512,128]{2,1,0:T(8,128)(2,1)S(1)}, u32[]{:S(2)}, u32[]{:S(2)}) %collective-permute-start.7) | collective-permute-done | bytes 1048608 | tf_op jit(solution)/shard_map/ppermute | solution.py:295
  101.1 14.2 %attend.4 = (bf16[512,512]{1,0:T(8,128)(2,1)}, bf16[512,512]{1,0:T(8,128)(2,1)}) custom-call(s32[3]{0:T(128)} %get-tuple-element.90.info_ref, bf16[2048,1024]{1,0:T(8,128)(2,1)} %q_ref.4, bf16[2048,1024]{1,0:T(8,128)(2,1)} %kp_ref.4, bf16[2048,1024]{1,0:T(8,128)(2,1)} %vp_ref.4, bf16[2048,1024]{1,0:T(8,128)(2,1)} %kp_ref.4, bf16[2048,1024]{1,0:T(8,128)(2,1)} %vp_ref.4, ...), custom_call_target="tpu_custom_call" | custom-call | flops 8053063680 | bytes 6144000 | tf_op jit(solution)/shard_map/attend/pallas_call | solution.py:203
  117.1 14.2 %attend.5 = (bf16[512,512]{1,0:T(8,128)(2,1)}, bf16[512,512]{1,0:T(8,128)(2,1)}) custom-call(s32[3]{0:T(128)} %get-tuple-element.90.info_ref, bf16[2048,1024]{1,0:T(8,128)(2,1)} %q_ref.4, bf16[2048,1024]{1,0:T(8,128)(2,1)} %kp_ref.4, bf16[2048,1024]{1,0:T(8,128)(2,1)} %vp_ref.4, bf16[2048,1024]{1,0:T(8,128)(2,1)} %kp_ref.4, bf16[2048,1024]{1,0:T(8,128)(2,1)} %vp_ref.4, ...), custom_call_target="tpu_custom_call" | custom-call | flops 8053063680 | bytes 6144000 | tf_op jit(solution)/shard_map/attend/pallas_call | solution.py:203
  131.9 1.9 %collective-permute-start.15 = (bf16[512,512]{1,0:T(8,128)(2,1)S(1)}, bf16[512,512]{1,0:T(8,128)(2,1)S(1)}, u32[]{:S(2)}, u32[]{:S(2)}) collective-permute-start(bf16[512,512]{1,0:T(8,128)(2,1)S(1)} %copy-done.9), channel_id=1, source_target_pairs={{0,3},{1,2},{2,1},{3,0},{4,7},{5,6},{6,5},{7,4},{8,11},{9,10},{10,... | collective-permute-start | bytes 1572872 | tf_op jit(solution)/shard_map/ppermute | solution.py:277
  133.8 14.3 %attend.6 = (bf16[512,512]{1,0:T(8,128)(2,1)}, bf16[512,512]{1,0:T(8,128)(2,1)}) custom-call(s32[3]{0:T(128)} %get-tuple-element.89.info_ref, bf16[2048,1024]{1,0:T(8,128)(2,1)} %q_ref.4, bf16[2048,1024]{1,0:T(8,128)(2,1)} %kp_ref.4, bf16[2048,1024]{1,0:T(8,128)(2,1)} %vp_ref.4, bf16[2048,1024]{1,0:T(8,128)(2,1)} %kp_ref.4, bf16[2048,1024]{1,0:T(8,128)(2,1)} %vp_ref.4, ...), custom_call_target="tpu_custom_call" | custom-call | flops 8053063680 | bytes 6144000 | tf_op jit(solution)/shard_map/attend/pallas_call | solution.py:203
  149.1 14.2 %attend.7 = (bf16[512,512]{1,0:T(8,128)(2,1)}, bf16[512,512]{1,0:T(8,128)(2,1)}) custom-call(s32[3]{0:T(128)} %get-tuple-element.89.info_ref, bf16[2048,1024]{1,0:T(8,128)(2,1)} %q_ref.4, bf16[2048,1024]{1,0:T(8,128)(2,1)} %kp_ref.4, bf16[2048,1024]{1,0:T(8,128)(2,1)} %vp_ref.4, bf16[2048,1024]{1,0:T(8,128)(2,1)} %kp_ref.4, bf16[2048,1024]{1,0:T(8,128)(2,1)} %vp_ref.4, ...), custom_call_target="tpu_custom_call" | custom-call | flops 8053063680 | bytes 6144000 | tf_op jit(solution)/shard_map/attend/pallas_call | solution.py:203
  163.4 4.3 %collective-permute-done.17.refs_8_ = bf16[512,512]{1,0:T(8,128)(2,1)S(1)} collective-permute-done((bf16[512,512]{1,0:T(8,128)(2,1)S(1)}, bf16[512,512]{1,0:T(8,128)(2,1)S(1)}, u32[]{:S(2)}, u32[]{:S(2)}) %collective-permute-start.17) | collective-permute-done | bytes 524320 | tf_op jit(solution)/shard_map/ppermute | solution.py:277
  167.9 2.0 %collective-permute-done.18.refs_6_ = bf16[512,512]{1,0:T(8,128)(2,1)S(1)} collective-permute-done((bf16[512,512]{1,0:T(8,128)(2,1)}, bf16[512,512]{1,0:T(8,128)(2,1)S(1)}, u32[]{:S(2)}, u32[]{:S(2)}) %collective-permute-start.18) | collective-permute-done | bytes 524320 | tf_op jit(solution)/shard_map/ppermute | solution.py:277
  170.7 3.6 %place.1 = bf16[512,4096]{1,0:T(8,128)(2,1)} custom-call(s32[1]{0:T(128)} %bitcast.refs_0_, bf16[512,512]{1,0:T(8,128)(2,1)} %get-tuple-element.75.refs_1_, bf16[512,512]{1,0:T(8,128)(2,1)} %copy-done.3, bf16[512,512]{1,0:T(8,128)(2,1)} %copy-done, bf16[512,512]{1,0:T(8,128)(2,1)} %copy-done.2, bf16[512,512]{1,0:T(8,128)(2,1)} %get-tuple-element.81.refs_5_, ...), custom_call_target="tpu_custom_call" | custom-call | bytes 8388608 | tf_op jit(solution)/shard_map/place/pallas_call | solution.py:257
  (61 shorter events, 17.6 us)
Async XLA Ops:
  0.0 33.0 %copy-start.7 = (s32[4]{0:T(128)S(1)}, s32[4]{0:T(128)}, u32[]{:S(2)}) copy-start(s32[4]{0:T(128)} %constant.99.clone) | copy-start | bytes 52
  6.1 6.1 %collective-permute-start = (bf16[8,2,32,128]{3,2,1,0:T(8,128)(2,1)}, bf16[8,2,32,128]{3,2,1,0:T(8,128)(2,1)S(1)}, u32[]{:S(2)}, u32[]{:S(2)}) collective-permute-start(bf16[8,2,32,128]{3,2,1,0:T(8,128)(2,1)} %get-tuple-element.46), channel_id=1, source_target_pairs={{0,64},{4,68},{8,72},{12,76},{16,80},{20,84},{24,88},{28,92},{32,9... | collective-permute-start | bytes 393224 | tf_op jit(solution)/shard_map/ppermute | solution.py:295
  13.1 14.8 %collective-permute-start.4 = (bf16[8,512,128]{2,1,0:T(8,128)(2,1)}, bf16[8,512,128]{2,1,0:T(8,128)(2,1)}, u32[]{:S(2)}, u32[]{:S(2)}) collective-permute-start(bf16[8,512,128]{2,1,0:T(8,128)(2,1)} %get-tuple-element.56.own_v_ref), channel_id=1, source_target_pairs={{12,28},{28,44},{44,60},{60,76},{76,92},{92,108},{108,124},{13,29}... | collective-permute-start | bytes 3145736 | tf_op jit(solution)/shard_map/ppermute | solution.py:295
  14.8 7.5 %collective-permute-start.2 = (bf16[8,2,64,128]{3,2,1,0:T(8,128)(2,1)S(1)}, bf16[8,2,64,128]{3,2,1,0:T(8,128)(2,1)S(1)}, u32[]{:S(2)}, u32[]{:S(2)}) collective-permute-start(bf16[8,2,64,128]{3,2,1,0:T(8,128)(2,1)S(1)} %pad_maximum_fusion), channel_id=1, source_target_pairs={{0,4},{4,8},{8,12},{12,0},{16,20},{20,24},{24,28},{28,16},{32,36},... | collective-permute-start | bytes 786440 | tf_op jit(solution)/shard_map/ppermute | solution.py:295
  16.1 6.2 %collective-permute-start.1 = (bf16[8,2,64,128]{3,2,1,0:T(8,128)(2,1)S(1)}, bf16[8,2,64,128]{3,2,1,0:T(8,128)(2,1)S(1)}, u32[]{:S(2)}, u32[]{:S(2)}) collective-permute-start(bf16[8,2,64,128]{3,2,1,0:T(8,128)(2,1)S(1)} %pad_maximum_fusion), channel_id=1, source_target_pairs={{0,12},{4,0},{8,4},{12,8},{16,28},{20,16},{24,20},{28,24},{32,44},... | collective-permute-start | bytes 786440 | tf_op jit(solution)/shard_map/ppermute | solution.py:295
  22.3 5.7 %collective-permute-start.3 = (bf16[8,2,64,128]{3,2,1,0:T(8,128)(2,1)S(1)}, bf16[8,2,64,128]{3,2,1,0:T(8,128)(2,1)S(1)}, u32[]{:S(2)}, u32[]{:S(2)}) collective-permute-start(bf16[8,2,64,128]{3,2,1,0:T(8,128)(2,1)S(1)} %collective-permute-done.1), channel_id=1, source_target_pairs={{0,12},{4,0},{8,4},{12,8},{16,28},{20,16},{24,20},{28,24},{32,44},... | collective-permute-start | bytes 786440 | tf_op jit(solution)/shard_map/ppermute | solution.py:295
  24.7 26.0 %collective-permute-start.6 = (bf16[8,512,128]{2,1,0:T(8,128)(2,1)}, bf16[8,512,128]{2,1,0:T(8,128)(2,1)}, u32[]{:S(2)}, u32[]{:S(2)}) collective-permute-start(bf16[8,512,128]{2,1,0:T(8,128)(2,1)} %get-tuple-element.51.own_k_ref), channel_id=1, source_target_pairs={{0,4},{4,8},{8,12},{12,16},{16,20},{20,24},{24,28},{28,32},{32,36}... | collective-permute-start | bytes 3145736 | tf_op jit(solution)/shard_map/ppermute | solution.py:295
  31.1 23.4 %collective-permute-start.5 = (bf16[8,2,256,128]{3,2,1,0:T(8,128)(2,1)}, bf16[8,2,256,128]{3,2,1,0:T(8,128)(2,1)S(1)}, u32[]{:S(2)}, u32[]{:S(2)}) collective-permute-start(bf16[8,2,256,128]{3,2,1,0:T(8,128)(2,1)} %constant_dynamic-update-slice_fusion.h0_ref), channel_id=1, source_target_pairs={{0,48},{4,52},{8,56},{12,60},{16,0},{20,4},{24,8},{28,12},{32,16},... | collective-permute-start | bytes 3145736 | tf_op jit(solution)/shard_map/ppermute | solution.py:295
  33.1 54.7 %collective-permute-start.9 = (bf16[8,2,256,128]{3,2,1,0:T(8,128)(2,1)}, bf16[8,2,256,128]{3,2,1,0:T(8,128)(2,1)}, u32[]{:S(2)}, u32[]{:S(2)}) collective-permute-start(bf16[8,2,256,128]{3,2,1,0:T(8,128)(2,1)} %constant_dynamic-update-slice_fusion.h0_ref), channel_id=1, source_target_pairs={{0,16},{4,20},{8,24},{12,28},{16,32},{20,36},{24,40},{28,44},{32,4... | collective-permute-start | bytes 3145736 | tf_op jit(solution)/shard_map/ppermute | solution.py:295
  33.9 65.2 %collective-permute-start.7 = (bf16[8,512,128]{2,1,0:T(8,128)(2,1)}, bf16[8,512,128]{2,1,0:T(8,128)(2,1)S(1)}, u32[]{:S(2)}, u32[]{:S(2)}) collective-permute-start(bf16[8,512,128]{2,1,0:T(8,128)(2,1)} %collective-permute-done.4), channel_id=1, source_target_pairs={{28,16},{44,32},{60,48},{76,64},{92,80},{108,96},{124,112},{29,17}... | collective-permute-start | bytes 3145736 | tf_op jit(solution)/shard_map/ppermute | solution.py:295
  35.2 64.0 %collective-permute-start.8 = (bf16[8,512,128]{2,1,0:T(8,128)(2,1)}, bf16[8,512,128]{2,1,0:T(8,128)(2,1)S(1)}, u32[]{:S(2)}, u32[]{:S(2)}) collective-permute-start(bf16[8,512,128]{2,1,0:T(8,128)(2,1)} %get-tuple-element.56.own_v_ref), channel_id=1, source_target_pairs={{0,4},{4,8},{8,12},{16,20},{20,24},{24,28},{32,36},{36,40},{40,44}... | collective-permute-start | bytes 3145736 | tf_op jit(solution)/shard_map/ppermute | solution.py:295
  50.6 34.6 %collective-permute-start.10 = (bf16[8,2,128,128]{3,2,1,0:T(8,128)(2,1)}, bf16[8,2,128,128]{3,2,1,0:T(8,128)(2,1)}, u32[]{:S(2)}, u32[]{:S(2)}) collective-permute-start(bf16[8,2,128,128]{3,2,1,0:T(8,128)(2,1)} %get-tuple-element.63), channel_id=1, source_target_pairs={{0,8},{4,12},{8,16},{12,20},{16,24},{20,28},{24,32},{28,36},{32,40... | collective-permute-start | bytes 1572872 | tf_op jit(solution)/shard_map/ppermute | solution.py:295
  54.5 45.8 %copy-start.6 = (bf16[8,2,256,128]{3,2,1,0:T(8,128)(2,1)}, bf16[8,2,256,128]{3,2,1,0:T(8,128)(2,1)S(1)}, u32[]{:S(2)}) copy-start(bf16[8,2,256,128]{3,2,1,0:T(8,128)(2,1)S(1)} %collective-permute-done.5.h1_ref) | copy-start | bytes 3145732
  54.5 45.7 %collective-permute-start.11 = (bf16[4,2,256,128]{3,2,1,0:T(8,128)(2,1)S(1)}, bf16[4,2,256,128]{3,2,1,0:T(8,128)(2,1)S(1)}, u32[]{:S(2)}, u32[]{:S(2)}) collective-permute-start(bf16[4,2,256,128]{3,2,1,0:T(8,128)(2,1)S(1)} %slice.6), channel_id=1, source_target_pairs={{0,48},{4,52},{8,56},{12,60},{16,0},{20,4},{24,8},{28,12},{32,16},... | collective-permute-start | bytes 1572872 | tf_op jit(solution)/shard_map/ppermute | solution.py:295
  88.8 27.4 %collective-permute-start.12 = (bf16[4,2,256,128]{3,2,1,0:T(8,128)(2,1)S(1)}, bf16[4,2,256,128]{3,2,1,0:T(8,128)(2,1)S(1)}, u32[]{:S(2)}, u32[]{:S(2)}) collective-permute-start(bf16[4,2,256,128]{3,2,1,0:T(8,128)(2,1)S(1)} %slice.7), channel_id=1, source_target_pairs={{0,16},{4,20},{8,24},{12,28},{16,32},{20,36},{24,40},{28,44},{32,4... | collective-permute-start | bytes 1572872 | tf_op jit(solution)/shard_map/ppermute | solution.py:295
  115.3 16.7 %copy-start.9 = (bf16[512,512]{1,0:T(8,128)(2,1)S(1)}, bf16[512,512]{1,0:T(8,128)(2,1)}, u32[]{:S(2)}) copy-start(bf16[512,512]{1,0:T(8,128)(2,1)} %get-tuple-element.77) | copy-start | bytes 1572868
  115.3 52.6 %collective-permute-start.14 = (bf16[512,512]{1,0:T(8,128)(2,1)}, bf16[512,512]{1,0:T(8,128)(2,1)S(1)}, u32[]{:S(2)}, u32[]{:S(2)}) collective-permute-start(bf16[512,512]{1,0:T(8,128)(2,1)} %get-tuple-element.67), channel_id=1, source_target_pairs={{0,2},{1,3},{2,0},{3,1},{4,6},{5,7},{6,4},{7,5},{8,10},{9,11},{10,... | collective-permute-start | bytes 1572872 | tf_op jit(solution)/shard_map/ppermute | solution.py:277
  131.3 36.4 %collective-permute-start.16 = (bf16[512,512]{1,0:T(8,128)(2,1)}, bf16[512,512]{1,0:T(8,128)(2,1)S(1)}, u32[]{:S(2)}, u32[]{:S(2)}) collective-permute-start(bf16[512,512]{1,0:T(8,128)(2,1)} %get-tuple-element.71), channel_id=1, source_target_pairs={{0,2},{1,3},{2,0},{3,1},{4,6},{5,7},{6,4},{7,5},{8,10},{9,11},{10,... | collective-permute-start | bytes 1572872 | tf_op jit(solution)/shard_map/ppermute | solution.py:277
  131.9 35.9 %collective-permute-start.15 = (bf16[512,512]{1,0:T(8,128)(2,1)S(1)}, bf16[512,512]{1,0:T(8,128)(2,1)S(1)}, u32[]{:S(2)}, u32[]{:S(2)}) collective-permute-start(bf16[512,512]{1,0:T(8,128)(2,1)S(1)} %copy-done.9), channel_id=1, source_target_pairs={{0,3},{1,2},{2,1},{3,0},{4,7},{5,6},{6,5},{7,4},{8,11},{9,10},{10,... | collective-permute-start | bytes 1572872 | tf_op jit(solution)/shard_map/ppermute | solution.py:277
  133.8 14.4 %copy-start.11 = (bf16[512,512]{1,0:T(8,128)(2,1)S(1)}, bf16[512,512]{1,0:T(8,128)(2,1)}, u32[]{:S(2)}) copy-start(bf16[512,512]{1,0:T(8,128)(2,1)} %get-tuple-element.83) | copy-start | bytes 1572868
  148.1 19.7 %collective-permute-start.13 = (bf16[512,512]{1,0:T(8,128)(2,1)}, bf16[512,512]{1,0:T(8,128)(2,1)S(1)}, u32[]{:S(2)}, u32[]{:S(2)}) collective-permute-start(bf16[512,512]{1,0:T(8,128)(2,1)} %get-tuple-element.76), channel_id=1, source_target_pairs={{0,1},{1,0},{2,3},{3,2},{4,5},{5,4},{6,7},{7,6},{8,9},{9,8},{10,11... | collective-permute-start | bytes 1572872 | tf_op jit(solution)/shard_map/ppermute | solution.py:277
  148.2 19.5 %collective-permute-start.17 = (bf16[512,512]{1,0:T(8,128)(2,1)S(1)}, bf16[512,512]{1,0:T(8,128)(2,1)S(1)}, u32[]{:S(2)}, u32[]{:S(2)}) collective-permute-start(bf16[512,512]{1,0:T(8,128)(2,1)S(1)} %copy-done.11), channel_id=1, source_target_pairs={{0,3},{1,2},{2,1},{3,0},{4,7},{5,6},{6,5},{7,4},{8,11},{9,10},{10,... | collective-permute-start | bytes 1572872 | tf_op jit(solution)/shard_map/ppermute | solution.py:277
  167.7 2.2 %copy-start.4 = (bf16[512,512]{1,0:T(8,128)(2,1)}, bf16[512,512]{1,0:T(8,128)(2,1)S(1)}, u32[]{:S(2)}) copy-start(bf16[512,512]{1,0:T(8,128)(2,1)S(1)} %collective-permute-done.17.refs_8_) | copy-start | bytes 1572868
  167.7 2.2 %collective-permute-start.18 = (bf16[512,512]{1,0:T(8,128)(2,1)}, bf16[512,512]{1,0:T(8,128)(2,1)S(1)}, u32[]{:S(2)}, u32[]{:S(2)}) collective-permute-start(bf16[512,512]{1,0:T(8,128)(2,1)} %get-tuple-element.84), channel_id=1, source_target_pairs={{0,1},{1,0},{2,3},{3,2},{4,5},{5,4},{6,7},{7,6},{8,9},{9,8},{10,11... | collective-permute-start | bytes 1572872 | tf_op jit(solution)/shard_map/ppermute | solution.py:277
  (7 other events, 10.9 us)

commit v5 on v4

--- a/solution.py
+++ b/solution.py
@@ -300,15 +300,14 @@
     above = over(own_v, UP_Z)
     g1, g3 = over(g0, Y_DOWN), over(g0, Y_UP)
     g1, g3, own_k, last = lax.optimization_barrier((g1, g3, own_k, last))
+    back2 = over(last, shift_route(2))
     gs = [g0, g1, g3, over(g1, Y_DOWN)]
-    own_v, gs, above, last = lax.optimization_barrier((own_v, gs, above, last))
-    back2 = over(last, shift_route(2))
+    own_v, gs, above, back2 = lax.optimization_barrier((own_v, gs, above, back2))
     back_k = over(own_k, shift_route(1))
     back_v = jnp.where(s % 4 == 0, over(above, ROUND_Y), over(own_v, ALONG_Y))
     h0 = jnp.concatenate(gs, axis=2)
     h1, h3 = over(h0, Z_DOWN), over(h0, Z_UP)
     h1, back_k = lax.optimization_barrier((h1, back_k))
-    h3, back2 = lax.optimization_barrier((h3, back2))
     split = CHUNKS[0]
     h2 = (over(h1[:split], Z_DOWN), over(h3[split:], Z_UP))
     parts = (far_bias(s), own_k, own_v, back_k, back_v, back2, h0, h1, h3)

time: 175 us -> 174 us (level)
  the two profiles are of different devices: /device:TPU:101 before, /device:TPU:5 now
where the time goes in v5:
time: 174 us
  Pallas kernels  66.7 us (38%)
  waiting for transfers between devices  60.9 us (35%)
  starting transfers between devices  35.4 us (20%)
  local copies, waits for them, and re-layouts  6.85 us (4%)
  other arithmetic  3.79 us (2%)
    pallas_call x4, Pallas kernels, attend(): pl.pallas_call(attend_kernel, grid_spec=pltpu.PrefetchScalarGridSpec(num_...  57 us
    ppermute x13, waiting for transfers between devices, shards(): over = lambda value, route: lax.ppermute(value, 'seq', route)  56.6 us
    ppermute x13, starting transfers between devices, shards(): over = lambda value, route: lax.ppermute(value, 'seq', route)  28.7 us
    ppermute x6, starting transfers between devices, swap_heads(): return lax.ppermute(piece, 'head', [(i, i ^ k) for i in range(4)])  6.67 us
    pallas_call x1, Pallas kernels, pool(): pl.pallas_call(pool_kernel, grid=(heads // step,), in_specs=[pl.BlockSpec...  6.14 us
    unnamed x29, local copies, waits for them, and re-layouts  4.85 us
    ppermute x6, waiting for transfers between devices, swap_heads(): return lax.ppermute(piece, 'head', [(i, i ^ k) for i in range(4)])  4.25 us
    pallas_call x1, Pallas kernels, place(): pl.pallas_call(lambda *refs: place_kernel(columns, *refs), in_specs=[pl.B...  3.57 us
  transfers between devices with their start and end apart: 19, of which 7 were waited for; matrix products, arithmetic and copies ran while one was open for 4% of the time, Pallas kernels for 33%

profile of v5, /device:TPU:5, one launch (start us, length us, event | category | flops | bytes accessed | tf_op | source)
XLA Modules:
  0.0 174.1 jit_solution(13031656904896763623)
XLA Ops:
  0.0 6.1 %pool.1 = (bf16[8,512,128]{2,1,0:T(8,128)(2,1)}, bf16[8,512,128]{2,1,0:T(8,128)(2,1)}, bf16[8,2,128,128]{3,2,1,0:T(8,128)(2,1)}, bf16[8,2,32,128]{3,2,1,0:T(8,128)(2,1)}) custom-call(bf16[2048,1024]{1,0:T(8,128)(2,1)} %kp_ref.4, bf16[2048,1024]{1,0:T(8,128)(2,1)} %vp_ref.4), custom_call_target="tpu_custom_call" | custom-call | flops 402653184 | bytes 12582912 | tf_op jit(solution)/shard_map/pool/pallas_call | solution.py:84
  6.2 6.1 %collective-permute-done = bf16[8,2,32,128]{3,2,1,0:T(8,128)(2,1)S(1)} collective-permute-done((bf16[8,2,32,128]{3,2,1,0:T(8,128)(2,1)}, bf16[8,2,32,128]{3,2,1,0:T(8,128)(2,1)S(1)}, u32[]{:S(2)}, u32[]{:S(2)}) %collective-permute-start) | collective-permute-done | bytes 131104 | tf_op jit(solution)/shard_map/ppermute | solution.py:295
  13.1 1.7 collective-permute-start.4
  14.8 1.3 collective-permute-start.2
  16.1 3.5 %collective-permute-start.1 = (bf16[8,2,64,128]{3,2,1,0:T(8,128)(2,1)S(1)}, bf16[8,2,64,128]{3,2,1,0:T(8,128)(2,1)S(1)}, u32[]{:S(2)}, u32[]{:S(2)}) collective-permute-start(bf16[8,2,64,128]{3,2,1,0:T(8,128)(2,1)S(1)} %pad_maximum_fusion), channel_id=1, source_target_pairs={{0,12},{4,0},{8,4},{12,8},{16,28},{20,16},{24,20},{28,24},{32,44},... | collective-permute-start | bytes 786440 | tf_op jit(solution)/shard_map/ppermute | solution.py:295
  19.6 4.7 %collective-permute-done.2 = bf16[8,2,64,128]{3,2,1,0:T(8,128)(2,1)S(1)} collective-permute-done((bf16[8,2,64,128]{3,2,1,0:T(8,128)(2,1)S(1)}, bf16[8,2,64,128]{3,2,1,0:T(8,128)(2,1)S(1)}, u32[]{:S(2)}, u32[]{:S(2)}) %collective-permute-start.2) | collective-permute-done | bytes 262176 | tf_op jit(solution)/shard_map/ppermute | solution.py:295
  24.3 4.0 %collective-permute-start.5 = (bf16[8,2,128,128]{3,2,1,0:T(8,128)(2,1)}, bf16[8,2,128,128]{3,2,1,0:T(8,128)(2,1)S(1)}, u32[]{:S(2)}, u32[]{:S(2)}) collective-permute-start(bf16[8,2,128,128]{3,2,1,0:T(8,128)(2,1)} %get-tuple-element.53), channel_id=1, source_target_pairs={{0,8},{4,12},{8,16},{12,20},{16,24},{20,28},{24,32},{28,36},{32,40... | collective-permute-start | bytes 1572872 | tf_op jit(solution)/shard_map/ppermute | solution.py:295
  28.3 2.3 %collective-permute-start.3 = (bf16[8,2,64,128]{3,2,1,0:T(8,128)(2,1)S(1)}, bf16[8,2,64,128]{3,2,1,0:T(8,128)(2,1)S(1)}, u32[]{:S(2)}, u32[]{:S(2)}) collective-permute-start(bf16[8,2,64,128]{3,2,1,0:T(8,128)(2,1)S(1)} %collective-permute-done.1), channel_id=1, source_target_pairs={{0,12},{4,0},{8,4},{12,8},{16,28},{20,16},{24,20},{28,24},{32,44},... | collective-permute-start | bytes 786440 | tf_op jit(solution)/shard_map/ppermute | solution.py:295
  30.6 1.9 %collective-permute-start.7 = (bf16[8,512,128]{2,1,0:T(8,128)(2,1)}, bf16[8,512,128]{2,1,0:T(8,128)(2,1)}, u32[]{:S(2)}, u32[]{:S(2)}) collective-permute-start(bf16[8,512,128]{2,1,0:T(8,128)(2,1)} %get-tuple-element.49.own_k_ref), channel_id=1, source_target_pairs={{0,4},{4,8},{8,12},{12,16},{16,20},{20,24},{24,28},{28,32},{32,36}... | collective-permute-start | bytes 3145736 | tf_op jit(solution)/shard_map/ppermute | solution.py:295
  32.5 14.0 %collective-permute-done.3 = bf16[8,2,64,128]{3,2,1,0:T(8,128)(2,1)S(1)} collective-permute-done((bf16[8,2,64,128]{3,2,1,0:T(8,128)(2,1)S(1)}, bf16[8,2,64,128]{3,2,1,0:T(8,128)(2,1)S(1)}, u32[]{:S(2)}, u32[]{:S(2)}) %collective-permute-start.3) | collective-permute-done | bytes 262176 | tf_op jit(solution)/shard_map/ppermute | solution.py:295
  49.8 1.6 collective-permute-start.10
  51.4 1.3 collective-permute-start.8
  52.7 11.0 %collective-permute-start.9 = (bf16[8,512,128]{2,1,0:T(8,128)(2,1)}, bf16[8,512,128]{2,1,0:T(8,128)(2,1)S(1)}, u32[]{:S(2)}, u32[]{:S(2)}) collective-permute-start(bf16[8,512,128]{2,1,0:T(8,128)(2,1)} %get-tuple-element.54.own_v_ref), channel_id=1, source_target_pairs={{0,4},{4,8},{8,12},{16,20},{20,24},{24,28},{32,36},{36,40},{40,44}... | collective-permute-start | bytes 3145736 | tf_op jit(solution)/shard_map/ppermute | solution.py:295
  64.7 13.5 %collective-permute-done.7.back_k_ref = bf16[8,512,128]{2,1,0:T(8,128)(2,1)} collective-permute-done((bf16[8,512,128]{2,1,0:T(8,128)(2,1)}, bf16[8,512,128]{2,1,0:T(8,128)(2,1)}, u32[]{:S(2)}, u32[]{:S(2)}) %collective-permute-start.7) | collective-permute-done | bytes 1048608 | tf_op jit(solution)/shard_map/ppermute | solution.py:295
  79.3 18.3 %collective-permute-done.10.h2_ref = bf16[8,2,256,128]{3,2,1,0:T(8,128)(2,1)} collective-permute-done((bf16[8,2,256,128]{3,2,1,0:T(8,128)(2,1)}, bf16[8,2,256,128]{3,2,1,0:T(8,128)(2,1)}, u32[]{:S(2)}, u32[]{:S(2)}) %collective-permute-start.10) | collective-permute-done | bytes 1048608 | tf_op jit(solution)/shard_map/ppermute | solution.py:295
  98.7 1.1 broadcast_select_fusion.back_v_ref
  100.7 14.2 %attend.4 = (bf16[512,512]{1,0:T(8,128)(2,1)}, bf16[512,512]{1,0:T(8,128)(2,1)}) custom-call(s32[3]{0:T(128)} %get-tuple-element.86.info_ref, bf16[2048,1024]{1,0:T(8,128)(2,1)} %q_ref.4, bf16[2048,1024]{1,0:T(8,128)(2,1)} %kp_ref.4, bf16[2048,1024]{1,0:T(8,128)(2,1)} %vp_ref.4, bf16[2048,1024]{1,0:T(8,128)(2,1)} %kp_ref.4, bf16[2048,1024]{1,0:T(8,128)(2,1)} %vp_ref.4, ...), custom_call_target="tpu_custom_call" | custom-call | flops 8053063680 | bytes 6144000 | tf_op jit(solution)/shard_map/attend/pallas_call | solution.py:203
  116.7 14.2 %attend.5 = (bf16[512,512]{1,0:T(8,128)(2,1)}, bf16[512,512]{1,0:T(8,128)(2,1)}) custom-call(s32[3]{0:T(128)} %get-tuple-element.86.info_ref, bf16[2048,1024]{1,0:T(8,128)(2,1)} %q_ref.4, bf16[2048,1024]{1,0:T(8,128)(2,1)} %kp_ref.4, bf16[2048,1024]{1,0:T(8,128)(2,1)} %vp_ref.4, bf16[2048,1024]{1,0:T(8,128)(2,1)} %kp_ref.4, bf16[2048,1024]{1,0:T(8,128)(2,1)} %vp_ref.4, ...), custom_call_target="tpu_custom_call" | custom-call | flops 8053063680 | bytes 6144000 | tf_op jit(solution)/shard_map/attend/pallas_call | solution.py:203
  131.6 3.9 %collective-permute-start.15 = (bf16[512,512]{1,0:T(8,128)(2,1)S(1)}, bf16[512,512]{1,0:T(8,128)(2,1)S(1)}, u32[]{:S(2)}, u32[]{:S(2)}) collective-permute-start(bf16[512,512]{1,0:T(8,128)(2,1)S(1)} %copy-done.10), channel_id=1, source_target_pairs={{0,3},{1,2},{2,1},{3,0},{4,7},{5,6},{6,5},{7,4},{8,11},{9,10},{10,... | collective-permute-start | bytes 1572872 | tf_op jit(solution)/shard_map/ppermute | solution.py:277
  135.5 14.3 %attend.6 = (bf16[512,512]{1,0:T(8,128)(2,1)}, bf16[512,512]{1,0:T(8,128)(2,1)}) custom-call(s32[3]{0:T(128)} %get-tuple-element.85.info_ref, bf16[2048,1024]{1,0:T(8,128)(2,1)} %q_ref.4, bf16[2048,1024]{1,0:T(8,128)(2,1)} %kp_ref.4, bf16[2048,1024]{1,0:T(8,128)(2,1)} %vp_ref.4, bf16[2048,1024]{1,0:T(8,128)(2,1)} %kp_ref.4, bf16[2048,1024]{1,0:T(8,128)(2,1)} %vp_ref.4, ...), custom_call_target="tpu_custom_call" | custom-call | flops 8053063680 | bytes 6144000 | tf_op jit(solution)/shard_map/attend/pallas_call | solution.py:203
  150.8 14.3 %attend.7 = (bf16[512,512]{1,0:T(8,128)(2,1)}, bf16[512,512]{1,0:T(8,128)(2,1)}) custom-call(s32[3]{0:T(128)} %get-tuple-element.85.info_ref, bf16[2048,1024]{1,0:T(8,128)(2,1)} %q_ref.4, bf16[2048,1024]{1,0:T(8,128)(2,1)} %kp_ref.4, bf16[2048,1024]{1,0:T(8,128)(2,1)} %vp_ref.4, bf16[2048,1024]{1,0:T(8,128)(2,1)} %kp_ref.4, bf16[2048,1024]{1,0:T(8,128)(2,1)} %vp_ref.4, ...), custom_call_target="tpu_custom_call" | custom-call | flops 8053063680 | bytes 6144000 | tf_op jit(solution)/shard_map/attend/pallas_call | solution.py:203
  165.1 2.2 %collective-permute-done.17.refs_8_ = bf16[512,512]{1,0:T(8,128)(2,1)S(1)} collective-permute-done((bf16[512,512]{1,0:T(8,128)(2,1)S(1)}, bf16[512,512]{1,0:T(8,128)(2,1)S(1)}, u32[]{:S(2)}, u32[]{:S(2)}) %collective-permute-start.17) | collective-permute-done | bytes 524320 | tf_op jit(solution)/shard_map/ppermute | solution.py:277
  167.5 2.0 %collective-permute-done.18.refs_6_ = bf16[512,512]{1,0:T(8,128)(2,1)S(1)} collective-permute-done((bf16[512,512]{1,0:T(8,128)(2,1)}, bf16[512,512]{1,0:T(8,128)(2,1)S(1)}, u32[]{:S(2)}, u32[]{:S(2)}) %collective-permute-start.18) | collective-permute-done | bytes 524320 | tf_op jit(solution)/shard_map/ppermute | solution.py:277
  170.3 3.6 %place.1 = bf16[512,4096]{1,0:T(8,128)(2,1)} custom-call(s32[1]{0:T(128)} %bitcast.refs_0_, bf16[512,512]{1,0:T(8,128)(2,1)} %get-tuple-element.71.refs_1_, bf16[512,512]{1,0:T(8,128)(2,1)} %copy-done.3, bf16[512,512]{1,0:T(8,128)(2,1)} %copy-done, bf16[512,512]{1,0:T(8,128)(2,1)} %copy-done.2, bf16[512,512]{1,0:T(8,128)(2,1)} %get-tuple-element.77.refs_5_, ...), custom_call_target="tpu_custom_call" | custom-call | bytes 8388608 | tf_op jit(solution)/shard_map/place/pallas_call | solution.py:257
  (63 shorter events, 12.5 us)
Async XLA Ops:
  0.0 49.8 %copy-start.7 = (s32[4]{0:T(128)S(1)}, s32[4]{0:T(128)}, u32[]{:S(2)}) copy-start(s32[4]{0:T(128)} %constant.99.clone) | copy-start | bytes 52
  6.1 6.1 %collective-permute-start = (bf16[8,2,32,128]{3,2,1,0:T(8,128)(2,1)}, bf16[8,2,32,128]{3,2,1,0:T(8,128)(2,1)S(1)}, u32[]{:S(2)}, u32[]{:S(2)}) collective-permute-start(bf16[8,2,32,128]{3,2,1,0:T(8,128)(2,1)} %get-tuple-element.44), channel_id=1, source_target_pairs={{0,64},{4,68},{8,72},{12,76},{16,80},{20,84},{24,88},{28,92},{32,9... | collective-permute-start | bytes 393224 | tf_op jit(solution)/shard_map/ppermute | solution.py:295
  13.1 33.4 %collective-permute-start.4 = (bf16[8,512,128]{2,1,0:T(8,128)(2,1)}, bf16[8,512,128]{2,1,0:T(8,128)(2,1)}, u32[]{:S(2)}, u32[]{:S(2)}) collective-permute-start(bf16[8,512,128]{2,1,0:T(8,128)(2,1)} %get-tuple-element.54.own_v_ref), channel_id=1, source_target_pairs={{12,28},{28,44},{44,60},{60,76},{76,92},{92,108},{108,124},{13,29}... | collective-permute-start | bytes 3145736 | tf_op jit(solution)/shard_map/ppermute | solution.py:295
  14.8 9.5 %collective-permute-start.2 = (bf16[8,2,64,128]{3,2,1,0:T(8,128)(2,1)S(1)}, bf16[8,2,64,128]{3,2,1,0:T(8,128)(2,1)S(1)}, u32[]{:S(2)}, u32[]{:S(2)}) collective-permute-start(bf16[8,2,64,128]{3,2,1,0:T(8,128)(2,1)S(1)} %pad_maximum_fusion), channel_id=1, source_target_pairs={{0,4},{4,8},{8,12},{12,0},{16,20},{20,24},{24,28},{28,16},{32,36},... | collective-permute-start | bytes 786440 | tf_op jit(solution)/shard_map/ppermute | solution.py:295
  16.1 8.2 %collective-permute-start.1 = (bf16[8,2,64,128]{3,2,1,0:T(8,128)(2,1)S(1)}, bf16[8,2,64,128]{3,2,1,0:T(8,128)(2,1)S(1)}, u32[]{:S(2)}, u32[]{:S(2)}) collective-permute-start(bf16[8,2,64,128]{3,2,1,0:T(8,128)(2,1)S(1)} %pad_maximum_fusion), channel_id=1, source_target_pairs={{0,12},{4,0},{8,4},{12,8},{16,28},{20,16},{24,20},{28,24},{32,44},... | collective-permute-start | bytes 786440 | tf_op jit(solution)/shard_map/ppermute | solution.py:295
  24.3 22.2 %collective-permute-start.5 = (bf16[8,2,128,128]{3,2,1,0:T(8,128)(2,1)}, bf16[8,2,128,128]{3,2,1,0:T(8,128)(2,1)S(1)}, u32[]{:S(2)}, u32[]{:S(2)}) collective-permute-start(bf16[8,2,128,128]{3,2,1,0:T(8,128)(2,1)} %get-tuple-element.53), channel_id=1, source_target_pairs={{0,8},{4,12},{8,16},{12,20},{16,24},{20,28},{24,32},{28,36},{32,40... | collective-permute-start | bytes 1572872 | tf_op jit(solution)/shard_map/ppermute | solution.py:295
  28.3 18.2 %collective-permute-start.3 = (bf16[8,2,64,128]{3,2,1,0:T(8,128)(2,1)S(1)}, bf16[8,2,64,128]{3,2,1,0:T(8,128)(2,1)S(1)}, u32[]{:S(2)}, u32[]{:S(2)}) collective-permute-start(bf16[8,2,64,128]{3,2,1,0:T(8,128)(2,1)S(1)} %collective-permute-done.1), channel_id=1, source_target_pairs={{0,12},{4,0},{8,4},{12,8},{16,28},{20,16},{24,20},{28,24},{32,44},... | collective-permute-start | bytes 786440 | tf_op jit(solution)/shard_map/ppermute | solution.py:295
  30.6 47.6 %collective-permute-start.7 = (bf16[8,512,128]{2,1,0:T(8,128)(2,1)}, bf16[8,512,128]{2,1,0:T(8,128)(2,1)}, u32[]{:S(2)}, u32[]{:S(2)}) collective-permute-start(bf16[8,512,128]{2,1,0:T(8,128)(2,1)} %get-tuple-element.49.own_k_ref), channel_id=1, source_target_pairs={{0,4},{4,8},{8,12},{12,16},{16,20},{20,24},{24,28},{28,32},{32,36}... | collective-permute-start | bytes 3145736 | tf_op jit(solution)/shard_map/ppermute | solution.py:295
  46.5 3.2 %copy-start.8 = (bf16[8,2,128,128]{3,2,1,0:T(8,128)(2,1)}, bf16[8,2,128,128]{3,2,1,0:T(8,128)(2,1)S(1)}, u32[]{:S(2)}) copy-start(bf16[8,2,128,128]{3,2,1,0:T(8,128)(2,1)S(1)} %collective-permute-done.5.back2_ref) | copy-start | bytes 1572868
  49.7 28.5 %collective-permute-start.6 = (bf16[8,2,256,128]{3,2,1,0:T(8,128)(2,1)}, bf16[8,2,256,128]{3,2,1,0:T(8,128)(2,1)S(1)}, u32[]{:S(2)}, u32[]{:S(2)}) collective-permute-start(bf16[8,2,256,128]{3,2,1,0:T(8,128)(2,1)} %constant_dynamic-update-slice_fusion.h0_ref), channel_id=1, source_target_pairs={{0,48},{4,52},{8,56},{12,60},{16,0},{20,4},{24,8},{28,12},{32,16},... | collective-permute-start | bytes 3145736 | tf_op jit(solution)/shard_map/ppermute | solution.py:295
  49.8 47.7 %collective-permute-start.10 = (bf16[8,2,256,128]{3,2,1,0:T(8,128)(2,1)}, bf16[8,2,256,128]{3,2,1,0:T(8,128)(2,1)}, u32[]{:S(2)}, u32[]{:S(2)}) collective-permute-start(bf16[8,2,256,128]{3,2,1,0:T(8,128)(2,1)} %constant_dynamic-update-slice_fusion.h0_ref), channel_id=1, source_target_pairs={{0,16},{4,20},{8,24},{12,28},{16,32},{20,36},{24,40},{28,44},{32,4... | collective-permute-start | bytes 3145736 | tf_op jit(solution)/shard_map/ppermute | solution.py:295
  51.4 47.3 %collective-permute-start.8 = (bf16[8,512,128]{2,1,0:T(8,128)(2,1)}, bf16[8,512,128]{2,1,0:T(8,128)(2,1)S(1)}, u32[]{:S(2)}, u32[]{:S(2)}) collective-permute-start(bf16[8,512,128]{2,1,0:T(8,128)(2,1)} %collective-permute-done.4), channel_id=1, source_target_pairs={{28,16},{44,32},{60,48},{76,64},{92,80},{108,96},{124,112},{29,17}... | collective-permute-start | bytes 3145736 | tf_op jit(solution)/shard_map/ppermute | solution.py:295
  52.7 46.0 %collective-permute-start.9 = (bf16[8,512,128]{2,1,0:T(8,128)(2,1)}, bf16[8,512,128]{2,1,0:T(8,128)(2,1)S(1)}, u32[]{:S(2)}, u32[]{:S(2)}) collective-permute-start(bf16[8,512,128]{2,1,0:T(8,128)(2,1)} %get-tuple-element.54.own_v_ref), channel_id=1, source_target_pairs={{0,4},{4,8},{8,12},{16,20},{20,24},{24,28},{32,36},{36,40},{40,44}... | collective-permute-start | bytes 3145736 | tf_op jit(solution)/shard_map/ppermute | solution.py:295
  78.2 21.6 %copy-start.6 = (bf16[8,2,256,128]{3,2,1,0:T(8,128)(2,1)}, bf16[8,2,256,128]{3,2,1,0:T(8,128)(2,1)S(1)}, u32[]{:S(2)}) copy-start(bf16[8,2,256,128]{3,2,1,0:T(8,128)(2,1)S(1)} %collective-permute-done.6.h1_ref) | copy-start | bytes 3145732
  78.3 21.6 %collective-permute-start.11 = (bf16[4,2,256,128]{3,2,1,0:T(8,128)(2,1)S(1)}, bf16[4,2,256,128]{3,2,1,0:T(8,128)(2,1)S(1)}, u32[]{:S(2)}, u32[]{:S(2)}) collective-permute-start(bf16[4,2,256,128]{3,2,1,0:T(8,128)(2,1)S(1)} %slice.6), channel_id=1, source_target_pairs={{0,48},{4,52},{8,56},{12,60},{16,0},{20,4},{24,8},{28,12},{32,16},... | collective-permute-start | bytes 1572872 | tf_op jit(solution)/shard_map/ppermute | solution.py:295
  98.6 17.2 %collective-permute-start.12 = (bf16[4,2,256,128]{3,2,1,0:T(8,128)(2,1)S(1)}, bf16[4,2,256,128]{3,2,1,0:T(8,128)(2,1)S(1)}, u32[]{:S(2)}, u32[]{:S(2)}) collective-permute-start(bf16[4,2,256,128]{3,2,1,0:T(8,128)(2,1)S(1)} %slice.8), channel_id=1, source_target_pairs={{0,16},{4,20},{8,24},{12,28},{16,32},{20,36},{24,40},{28,44},{32,4... | collective-permute-start | bytes 1572872 | tf_op jit(solution)/shard_map/ppermute | solution.py:295
  114.9 16.7 %copy-start.10 = (bf16[512,512]{1,0:T(8,128)(2,1)S(1)}, bf16[512,512]{1,0:T(8,128)(2,1)}, u32[]{:S(2)}) copy-start(bf16[512,512]{1,0:T(8,128)(2,1)} %get-tuple-element.73) | copy-start | bytes 1572868
  114.9 52.6 %collective-permute-start.14 = (bf16[512,512]{1,0:T(8,128)(2,1)}, bf16[512,512]{1,0:T(8,128)(2,1)S(1)}, u32[]{:S(2)}, u32[]{:S(2)}) collective-permute-start(bf16[512,512]{1,0:T(8,128)(2,1)} %get-tuple-element.63), channel_id=1, source_target_pairs={{0,2},{1,3},{2,0},{3,1},{4,6},{5,7},{6,4},{7,5},{8,10},{9,11},{10,... | collective-permute-start | bytes 1572872 | tf_op jit(solution)/shard_map/ppermute | solution.py:277
  130.9 36.4 %collective-permute-start.16 = (bf16[512,512]{1,0:T(8,128)(2,1)}, bf16[512,512]{1,0:T(8,128)(2,1)S(1)}, u32[]{:S(2)}, u32[]{:S(2)}) collective-permute-start(bf16[512,512]{1,0:T(8,128)(2,1)} %get-tuple-element.67), channel_id=1, source_target_pairs={{0,2},{1,3},{2,0},{3,1},{4,6},{5,7},{6,4},{7,5},{8,10},{9,11},{10,... | collective-permute-start | bytes 1572872 | tf_op jit(solution)/shard_map/ppermute | solution.py:277
  131.6 35.8 %collective-permute-start.15 = (bf16[512,512]{1,0:T(8,128)(2,1)S(1)}, bf16[512,512]{1,0:T(8,128)(2,1)S(1)}, u32[]{:S(2)}, u32[]{:S(2)}) collective-permute-start(bf16[512,512]{1,0:T(8,128)(2,1)S(1)} %copy-done.10), channel_id=1, source_target_pairs={{0,3},{1,2},{2,1},{3,0},{4,7},{5,6},{6,5},{7,4},{8,11},{9,10},{10,... | collective-permute-start | bytes 1572872 | tf_op jit(solution)/shard_map/ppermute | solution.py:277
  135.5 14.4 %copy-start.12 = (bf16[512,512]{1,0:T(8,128)(2,1)S(1)}, bf16[512,512]{1,0:T(8,128)(2,1)}, u32[]{:S(2)}) copy-start(bf16[512,512]{1,0:T(8,128)(2,1)} %get-tuple-element.79) | copy-start | bytes 1572868
  149.8 17.7 %collective-permute-start.13 = (bf16[512,512]{1,0:T(8,128)(2,1)}, bf16[512,512]{1,0:T(8,128)(2,1)S(1)}, u32[]{:S(2)}, u32[]{:S(2)}) collective-permute-start(bf16[512,512]{1,0:T(8,128)(2,1)} %get-tuple-element.72), channel_id=1, source_target_pairs={{0,1},{1,0},{2,3},{3,2},{4,5},{5,4},{6,7},{7,6},{8,9},{9,8},{10,11... | collective-permute-start | bytes 1572872 | tf_op jit(solution)/shard_map/ppermute | solution.py:277
  149.9 17.4 %collective-permute-start.17 = (bf16[512,512]{1,0:T(8,128)(2,1)S(1)}, bf16[512,512]{1,0:T(8,128)(2,1)S(1)}, u32[]{:S(2)}, u32[]{:S(2)}) collective-permute-start(bf16[512,512]{1,0:T(8,128)(2,1)S(1)} %copy-done.12), channel_id=1, source_target_pairs={{0,3},{1,2},{2,1},{3,0},{4,7},{5,6},{6,5},{7,4},{8,11},{9,10},{10,... | collective-permute-start | bytes 1572872 | tf_op jit(solution)/shard_map/ppermute | solution.py:277
  167.3 2.2 %collective-permute-start.18 = (bf16[512,512]{1,0:T(8,128)(2,1)}, bf16[512,512]{1,0:T(8,128)(2,1)S(1)}, u32[]{:S(2)}, u32[]{:S(2)}) collective-permute-start(bf16[512,512]{1,0:T(8,128)(2,1)} %get-tuple-element.80), channel_id=1, source_target_pairs={{0,1},{1,0},{2,3},{3,2},{4,5},{5,4},{6,7},{7,6},{8,9},{9,8},{10,11... | collective-permute-start | bytes 1572872 | tf_op jit(solution)/shard_map/ppermute | solution.py:277
  (8 other events, 13.1 us)

commit v6 on v3

--- a/solution.py
+++ b/solution.py
@@ -311,8 +311,9 @@
     parts = (far_bias(s), own_k, own_v, back_k, back_v, back2, *fars)
     pieces = {}
     args = (queries, key_rows, value_rows)
-    for which, names in ((1 - pair, (2, 3)), (pair, (0, 1))):
-        for c, (first, heads) in enumerate(zip(firsts, CHUNKS)):
+    calls = list(enumerate(zip(firsts, CHUNKS)))
+    for which, names, these in ((1 - pair, (2, 3), calls), (pair, (0, 1), [(0, (0, HEADS))])):
+        for c, (first, heads) in these:
             outs = attend(first, heads, jnp.stack([s, which, flip]), *args, *parts)
             for k, out in zip(names, outs):
                 pieces[c, k] = swap_heads(out, k) if k else out

time: 174 us -> 211 us (1.21)
  waiting for transfers between devices: 63.5 us -> 104 us
  Pallas kernels: 66.6 us -> 63.6 us
    ppermute x6 -> x5, waiting for transfers between devices: 3.6 us -> 43.9 us  [swap_heads(): return lax.ppermute(piece, 'head', [(i, i ^ k) for i in range(4)])]
    pallas_call x4 -> x3, Pallas kernels: 56.9 us -> 54.1 us  [attend(): pl.pallas_call(attend_kernel, grid_spec=pltpu.PrefetchScalarGridSpec(num_...]
    ppermute x6 -> x5, starting transfers between devices: 5.25 us -> 4.63 us  [swap_heads(): return lax.ppermute(piece, 'head', [(i, i ^ k) for i in range(4)])]
  transfers between devices with their start and end apart: 18 -> 17, of which waited for: 7 -> 9; matrix products, arithmetic and copies ran while one was open for 2% -> 2% of each run, Pallas kernels for 25% -> 0%
where the time goes in v6:
time: 211 us; the launch traced here: 210 us
  waiting for transfers between devices  104 us (49%)
  Pallas kernels  63.6 us (30%)
  starting transfers between devices  35.4 us (17%)
  other arithmetic  4.94 us (2%)
  local copies, waits for them, and re-layouts  2.17 us (1%)
    ppermute x12, waiting for transfers between devices, shards(): over = lambda value, route: lax.ppermute(value, 'seq', route)  59.8 us
    pallas_call x3, Pallas kernels, attend(): pl.pallas_call(attend_kernel, grid_spec=pltpu.PrefetchScalarGridSpec(num_...  54.1 us
    ppermute x5, waiting for transfers between devices, swap_heads(): return lax.ppermute(piece, 'head', [(i, i ^ k) for i in range(4)])  43.9 us
    ppermute x12, starting transfers between devices, shards(): over = lambda value, route: lax.ppermute(value, 'seq', route)  30.8 us
    pallas_call x1, Pallas kernels, pool(): pl.pallas_call(pool_kernel, grid=(heads // step,), in_specs=[pl.BlockSpec...  6.14 us
    ppermute x5, starting transfers between devices, swap_heads(): return lax.ppermute(piece, 'head', [(i, i ^ k) for i in range(4)])  4.63 us
  transfers between devices with their start and end apart: 17, of which 9 were waited for; matrix products, arithmetic and copies ran while one was open for 2% of the time, Pallas kernels for 0%

profile of v6, /device:TPU:5, one launch (start us, length us, event | category | flops | bytes accessed | tf_op | source)
XLA Modules:
  0.0 210.2 jit_solution(5644869858373193850)
XLA Ops:
  0.0 6.1 %pool.1 = (bf16[8,512,128]{2,1,0:T(8,128)(2,1)}, bf16[8,512,128]{2,1,0:T(8,128)(2,1)}, bf16[8,2,128,128]{3,2,1,0:T(8,128)(2,1)}, bf16[8,2,32,128]{3,2,1,0:T(8,128)(2,1)}) custom-call(bf16[2048,1024]{1,0:T(8,128)(2,1)} %kp_ref.3, bf16[2048,1024]{1,0:T(8,128)(2,1)} %vp_ref.3), custom_call_target="tpu_custom_call" | custom-call | flops 402653184 | bytes 12582912 | tf_op jit(solution)/shard_map/pool/pallas_call | solution.py:84
  6.2 6.1 %collective-permute-done = bf16[8,2,32,128]{3,2,1,0:T(8,128)(2,1)S(1)} collective-permute-done((bf16[8,2,32,128]{3,2,1,0:T(8,128)(2,1)}, bf16[8,2,32,128]{3,2,1,0:T(8,128)(2,1)S(1)}, u32[]{:S(2)}, u32[]{:S(2)}) %collective-permute-start) | collective-permute-done | bytes 131104 | tf_op jit(solution)/shard_map/ppermute | solution.py:294
  13.1 1.6 collective-permute-start.4
  14.8 1.3 collective-permute-start.2
  16.1 3.5 %collective-permute-start.1 = (bf16[8,2,64,128]{3,2,1,0:T(8,128)(2,1)S(1)}, bf16[8,2,64,128]{3,2,1,0:T(8,128)(2,1)S(1)}, u32[]{:S(2)}, u32[]{:S(2)}) collective-permute-start(bf16[8,2,64,128]{3,2,1,0:T(8,128)(2,1)S(1)} %pad_maximum_fusion), channel_id=1, source_target_pairs={{0,12},{4,0},{8,4},{12,8},{16,28},{20,16},{24,20},{28,24},{32,44},... | collective-permute-start | bytes 786440 | tf_op jit(solution)/shard_map/ppermute | solution.py:294
  19.6 4.7 %collective-permute-done.2 = bf16[8,2,64,128]{3,2,1,0:T(8,128)(2,1)S(1)} collective-permute-done((bf16[8,2,64,128]{3,2,1,0:T(8,128)(2,1)S(1)}, bf16[8,2,64,128]{3,2,1,0:T(8,128)(2,1)S(1)}, u32[]{:S(2)}, u32[]{:S(2)}) %collective-permute-start.2) | collective-permute-done | bytes 262176 | tf_op jit(solution)/shard_map/ppermute | solution.py:294
  24.3 4.0 %collective-permute-start.5 = (bf16[8,2,128,128]{3,2,1,0:T(8,128)(2,1)}, bf16[8,2,128,128]{3,2,1,0:T(8,128)(2,1)S(1)}, u32[]{:S(2)}, u32[]{:S(2)}) collective-permute-start(bf16[8,2,128,128]{3,2,1,0:T(8,128)(2,1)} %get-tuple-element.45), channel_id=1, source_target_pairs={{0,8},{4,12},{8,16},{12,20},{16,24},{20,28},{24,32},{28,36},{32,40... | collective-permute-start | bytes 1572872 | tf_op jit(solution)/shard_map/ppermute | solution.py:294
  28.3 2.3 %collective-permute-start.3 = (bf16[8,2,64,128]{3,2,1,0:T(8,128)(2,1)S(1)}, bf16[8,2,64,128]{3,2,1,0:T(8,128)(2,1)S(1)}, u32[]{:S(2)}, u32[]{:S(2)}) collective-permute-start(bf16[8,2,64,128]{3,2,1,0:T(8,128)(2,1)S(1)} %collective-permute-done.1), channel_id=1, source_target_pairs={{0,12},{4,0},{8,4},{12,8},{16,28},{20,16},{24,20},{28,24},{32,44},... | collective-permute-start | bytes 786440 | tf_op jit(solution)/shard_map/ppermute | solution.py:294
  30.6 1.9 collective-permute-start.7
  32.5 14.0 %collective-permute-done.3 = bf16[8,2,64,128]{3,2,1,0:T(8,128)(2,1)S(1)} collective-permute-done((bf16[8,2,64,128]{3,2,1,0:T(8,128)(2,1)S(1)}, bf16[8,2,64,128]{3,2,1,0:T(8,128)(2,1)S(1)}, u32[]{:S(2)}, u32[]{:S(2)}) %collective-permute-start.3) | collective-permute-done | bytes 262176 | tf_op jit(solution)/shard_map/ppermute | solution.py:294
  49.0 13.1 %collective-permute-start.9 = (bf16[8,512,128]{2,1,0:T(8,128)(2,1)}, bf16[8,512,128]{2,1,0:T(8,128)(2,1)}, u32[]{:S(2)}, u32[]{:S(2)}) collective-permute-start(bf16[8,512,128]{2,1,0:T(8,128)(2,1)} %get-tuple-element.46.own_v_ref), channel_id=1, source_target_pairs={{0,4},{4,8},{8,12},{16,20},{20,24},{24,28},{32,36},{36,40},{40,44}... | collective-permute-start | bytes 3145736 | tf_op jit(solution)/shard_map/ppermute | solution.py:294
  62.1 1.4 collective-permute-start.10
  63.5 14.7 %collective-permute-done.7.back_k_ref = bf16[8,512,128]{2,1,0:T(8,128)(2,1)S(1)} collective-permute-done((bf16[8,512,128]{2,1,0:T(8,128)(2,1)}, bf16[8,512,128]{2,1,0:T(8,128)(2,1)S(1)}, u32[]{:S(2)}, u32[]{:S(2)}) %collective-permute-start.7) | collective-permute-done | bytes 1048608 | tf_op jit(solution)/shard_map/ppermute | solution.py:294
  80.1 7.4 %collective-permute-done.8 = bf16[8,512,128]{2,1,0:T(8,128)(2,1)} collective-permute-done((bf16[8,512,128]{2,1,0:T(8,128)(2,1)}, bf16[8,512,128]{2,1,0:T(8,128)(2,1)}, u32[]{:S(2)}, u32[]{:S(2)}) %collective-permute-start.8) | collective-permute-done | bytes 1048608 | tf_op jit(solution)/shard_map/ppermute | solution.py:294
  87.6 2.3 %broadcast_select_fusion.back_v_ref = bf16[8,512,128]{2,1,0:T(8,128)(2,1)} fusion(bf16[8,512,128]{2,1,0:T(8,128)(2,1)} %collective-permute-done.8, bf16[8,512,128]{2,1,0:T(8,128)(2,1)} %collective-permute-done.9, pred[]{:T(512)S(6)} %eq.11), kind=kLoop, calls=%fused_computation | loop fusion | flops 524288 | bytes 3145729 | tf_op jit(solution)/shard_map/jit(_where)/select_n | solution.py:306
  89.9 12.9 %collective-permute-done.10.h2_ref = bf16[8,2,256,128]{3,2,1,0:T(8,128)(2,1)} collective-permute-done((bf16[8,2,256,128]{3,2,1,0:T(8,128)(2,1)S(1)}, bf16[8,2,256,128]{3,2,1,0:T(8,128)(2,1)}, u32[]{:S(2)}, u32[]{:S(2)}) %collective-permute-start.10) | collective-permute-done | bytes 1048608 | tf_op jit(solution)/shard_map/ppermute | solution.py:294
  102.8 14.2 %attend.3 = (bf16[512,512]{1,0:T(8,128)(2,1)}, bf16[512,512]{1,0:T(8,128)(2,1)}) custom-call(s32[3]{0:T(128)} %get-tuple-element.70.info_ref, bf16[2048,1024]{1,0:T(8,128)(2,1)} %q_ref.3, bf16[2048,1024]{1,0:T(8,128)(2,1)} %kp_ref.3, bf16[2048,1024]{1,0:T(8,128)(2,1)} %vp_ref.3, bf16[2048,1024]{1,0:T(8,128)(2,1)} %kp_ref.3, bf16[2048,1024]{1,0:T(8,128)(2,1)} %vp_ref.3, ...), custom_call_target="tpu_custom_call" | custom-call | flops 8053063680 | bytes 6144000 | tf_op jit(solution)/shard_map/attend/pallas_call | solution.py:203
  117.0 14.2 %attend.4 = (bf16[512,512]{1,0:T(8,128)(2,1)}, bf16[512,512]{1,0:T(8,128)(2,1)}) custom-call(s32[3]{0:T(128)} %get-tuple-element.70.info_ref, bf16[2048,1024]{1,0:T(8,128)(2,1)} %q_ref.3, bf16[2048,1024]{1,0:T(8,128)(2,1)} %kp_ref.3, bf16[2048,1024]{1,0:T(8,128)(2,1)} %vp_ref.3, bf16[2048,1024]{1,0:T(8,128)(2,1)} %kp_ref.3, bf16[2048,1024]{1,0:T(8,128)(2,1)} %vp_ref.3, ...), custom_call_target="tpu_custom_call" | custom-call | flops 8053063680 | bytes 6144000 | tf_op jit(solution)/shard_map/attend/pallas_call | solution.py:203
  131.2 25.7 %attend.5 = (bf16[512,1024]{1,0:T(8,128)(2,1)}, bf16[512,1024]{1,0:T(8,128)(2,1)}) custom-call(s32[3]{0:T(128)} %get-tuple-element.69.info_ref, bf16[2048,1024]{1,0:T(8,128)(2,1)} %q_ref.3, bf16[2048,1024]{1,0:T(8,128)(2,1)} %kp_ref.3, bf16[2048,1024]{1,0:T(8,128)(2,1)} %vp_ref.3, bf16[2048,1024]{1,0:T(8,128)(2,1)} %kp_ref.3, bf16[2048,1024]{1,0:T(8,128)(2,1)} %vp_ref.3, ...), custom_call_target="tpu_custom_call" | custom-call | flops 16106127360 | bytes 12288000 | tf_op jit(solution)/shard_map/attend/pallas_call | solution.py:203
  157.0 1.4 collective-permute-start.12
  161.6 22.4 %collective-permute-done.14.refs_4_ = bf16[512,512]{1,0:T(8,128)(2,1)S(1)} collective-permute-done((bf16[512,512]{1,0:T(8,128)(2,1)S(1)}, bf16[512,512]{1,0:T(8,128)(2,1)S(1)}, u32[]{:S(2)}, u32[]{:S(2)}) %collective-permute-start.14) | collective-permute-done | bytes 524320 | tf_op jit(solution)/shard_map/ppermute | solution.py:276
  184.0 10.9 %collective-permute-done.16.refs_6_ = bf16[512,512]{1,0:T(8,128)(2,1)S(1)} collective-permute-done((bf16[512,512]{1,0:T(8,128)(2,1)S(1)}, bf16[512,512]{1,0:T(8,128)(2,1)S(1)}, u32[]{:S(2)}, u32[]{:S(2)}) %collective-permute-start.16) | collective-permute-done | bytes 524320 | tf_op jit(solution)/shard_map/ppermute | solution.py:276
  195.0 10.6 %collective-permute-done.15.refs_5_ = bf16[512,512]{1,0:T(8,128)(2,1)S(1)} collective-permute-done((bf16[512,512]{1,0:T(8,128)(2,1)S(1)}, bf16[512,512]{1,0:T(8,128)(2,1)S(1)}, u32[]{:S(2)}, u32[]{:S(2)}) %collective-permute-start.15) | collective-permute-done | bytes 524320 | tf_op jit(solution)/shard_map/ppermute | solution.py:276
  206.7 3.3 %place.1 = bf16[512,4096]{1,0:T(8,128)(2,1)} custom-call(s32[1]{0:T(128)} %bitcast.refs_0_, bf16[512,1024]{1,0:T(8,128)(2,1)} %get-tuple-element.63.refs_1_, bf16[512,1024]{1,0:T(8,128)(2,1)} %copy-done.4, bf16[512,512]{1,0:T(8,128)(2,1)} %copy-done.5, bf16[512,512]{1,0:T(8,128)(2,1)} %copy-done.6, bf16[512,512]{1,0:T(8,128)(2,1)} %copy-done.8, ...), custom_call_target="tpu_custom_call" | custom-call | bytes 6291456 | tf_op jit(solution)/shard_map/place/pallas_call | solution.py:256
  (58 shorter events, 9.7 us)
Async XLA Ops:
  0.0 47.6 %copy-start.9 = (s32[4]{0:T(128)S(1)}, s32[4]{0:T(128)}, u32[]{:S(2)}) copy-start(s32[4]{0:T(128)} %constant.99.clone) | copy-start | bytes 52
  6.1 6.1 %collective-permute-start = (bf16[8,2,32,128]{3,2,1,0:T(8,128)(2,1)}, bf16[8,2,32,128]{3,2,1,0:T(8,128)(2,1)S(1)}, u32[]{:S(2)}, u32[]{:S(2)}) collective-permute-start(bf16[8,2,32,128]{3,2,1,0:T(8,128)(2,1)} %get-tuple-element.36), channel_id=1, source_target_pairs={{0,64},{4,68},{8,72},{12,76},{16,80},{20,84},{24,88},{28,92},{32,9... | collective-permute-start | bytes 393224 | tf_op jit(solution)/shard_map/ppermute | solution.py:294
  13.1 34.2 %collective-permute-start.4 = (bf16[8,512,128]{2,1,0:T(8,128)(2,1)}, bf16[8,512,128]{2,1,0:T(8,128)(2,1)}, u32[]{:S(2)}, u32[]{:S(2)}) collective-permute-start(bf16[8,512,128]{2,1,0:T(8,128)(2,1)} %get-tuple-element.46.own_v_ref), channel_id=1, source_target_pairs={{12,28},{28,44},{44,60},{60,76},{76,92},{92,108},{108,124},{13,29}... | collective-permute-start | bytes 3145736 | tf_op jit(solution)/shard_map/ppermute | solution.py:294
  14.8 9.5 %collective-permute-start.2 = (bf16[8,2,64,128]{3,2,1,0:T(8,128)(2,1)S(1)}, bf16[8,2,64,128]{3,2,1,0:T(8,128)(2,1)S(1)}, u32[]{:S(2)}, u32[]{:S(2)}) collective-permute-start(bf16[8,2,64,128]{3,2,1,0:T(8,128)(2,1)S(1)} %pad_maximum_fusion), channel_id=1, source_target_pairs={{0,4},{4,8},{8,12},{12,0},{16,20},{20,24},{24,28},{28,16},{32,36},... | collective-permute-start | bytes 786440 | tf_op jit(solution)/shard_map/ppermute | solution.py:294
  16.1 8.2 %collective-permute-start.1 = (bf16[8,2,64,128]{3,2,1,0:T(8,128)(2,1)S(1)}, bf16[8,2,64,128]{3,2,1,0:T(8,128)(2,1)S(1)}, u32[]{:S(2)}, u32[]{:S(2)}) collective-permute-start(bf16[8,2,64,128]{3,2,1,0:T(8,128)(2,1)S(1)} %pad_maximum_fusion), channel_id=1, source_target_pairs={{0,12},{4,0},{8,4},{12,8},{16,28},{20,16},{24,20},{28,24},{32,44},... | collective-permute-start | bytes 786440 | tf_op jit(solution)/shard_map/ppermute | solution.py:294
  24.3 22.2 %collective-permute-start.5 = (bf16[8,2,128,128]{3,2,1,0:T(8,128)(2,1)}, bf16[8,2,128,128]{3,2,1,0:T(8,128)(2,1)S(1)}, u32[]{:S(2)}, u32[]{:S(2)}) collective-permute-start(bf16[8,2,128,128]{3,2,1,0:T(8,128)(2,1)} %get-tuple-element.45), channel_id=1, source_target_pairs={{0,8},{4,12},{8,16},{12,20},{16,24},{20,28},{24,32},{28,36},{32,40... | collective-permute-start | bytes 1572872 | tf_op jit(solution)/shard_map/ppermute | solution.py:294
  28.3 18.2 %collective-permute-start.3 = (bf16[8,2,64,128]{3,2,1,0:T(8,128)(2,1)S(1)}, bf16[8,2,64,128]{3,2,1,0:T(8,128)(2,1)S(1)}, u32[]{:S(2)}, u32[]{:S(2)}) collective-permute-start(bf16[8,2,64,128]{3,2,1,0:T(8,128)(2,1)S(1)} %collective-permute-done.1), channel_id=1, source_target_pairs={{0,12},{4,0},{8,4},{12,8},{16,28},{20,16},{24,20},{28,24},{32,44},... | collective-permute-start | bytes 786440 | tf_op jit(solution)/shard_map/ppermute | solution.py:294
  30.6 47.6 %collective-permute-start.7 = (bf16[8,512,128]{2,1,0:T(8,128)(2,1)}, bf16[8,512,128]{2,1,0:T(8,128)(2,1)S(1)}, u32[]{:S(2)}, u32[]{:S(2)}) collective-permute-start(bf16[8,512,128]{2,1,0:T(8,128)(2,1)} %get-tuple-element.41.own_k_ref), channel_id=1, source_target_pairs={{0,4},{4,8},{8,12},{12,16},{16,20},{20,24},{24,28},{28,32},{32,36}... | collective-permute-start | bytes 3145736 | tf_op jit(solution)/shard_map/ppermute | solution.py:294
  47.5 55.3 %copy-start = (bf16[8,2,256,128]{3,2,1,0:T(8,128)(2,1)}, bf16[8,2,256,128]{3,2,1,0:T(8,128)(2,1)S(1)}, u32[]{:S(2)}) copy-start(bf16[8,2,256,128]{3,2,1,0:T(8,128)(2,1)S(1)} %constant_dynamic-update-slice_fusion.h0_ref) | copy-start | bytes 3145732
  47.5 30.7 %collective-permute-start.6 = (bf16[8,2,256,128]{3,2,1,0:T(8,128)(2,1)S(1)}, bf16[8,2,256,128]{3,2,1,0:T(8,128)(2,1)S(1)}, u32[]{:S(2)}, u32[]{:S(2)}) collective-permute-start(bf16[8,2,256,128]{3,2,1,0:T(8,128)(2,1)S(1)} %constant_dynamic-update-slice_fusion.h0_ref), channel_id=1, source_target_pairs={{0,48},{4,52},{8,56},{12,60},{16,0},{20,4},{24,8},{28,12},{32,16},... | collective-permute-start | bytes 3145736 | tf_op jit(solution)/shard_map/ppermute | solution.py:294
  47.7 39.9 %collective-permute-start.8 = (bf16[8,512,128]{2,1,0:T(8,128)(2,1)}, bf16[8,512,128]{2,1,0:T(8,128)(2,1)}, u32[]{:S(2)}, u32[]{:S(2)}) collective-permute-start(bf16[8,512,128]{2,1,0:T(8,128)(2,1)} %collective-permute-done.4), channel_id=1, source_target_pairs={{28,16},{44,32},{60,48},{76,64},{92,80},{108,96},{124,112},{29,17}... | collective-permute-start | bytes 3145736 | tf_op jit(solution)/shard_map/ppermute | solution.py:294
  49.0 38.6 %collective-permute-start.9 = (bf16[8,512,128]{2,1,0:T(8,128)(2,1)}, bf16[8,512,128]{2,1,0:T(8,128)(2,1)}, u32[]{:S(2)}, u32[]{:S(2)}) collective-permute-start(bf16[8,512,128]{2,1,0:T(8,128)(2,1)} %get-tuple-element.46.own_v_ref), channel_id=1, source_target_pairs={{0,4},{4,8},{8,12},{16,20},{20,24},{24,28},{32,36},{36,40},{40,44}... | collective-permute-start | bytes 3145736 | tf_op jit(solution)/shard_map/ppermute | solution.py:294
  62.1 40.7 %collective-permute-start.10 = (bf16[8,2,256,128]{3,2,1,0:T(8,128)(2,1)S(1)}, bf16[8,2,256,128]{3,2,1,0:T(8,128)(2,1)}, u32[]{:S(2)}, u32[]{:S(2)}) collective-permute-start(bf16[8,2,256,128]{3,2,1,0:T(8,128)(2,1)S(1)} %constant_dynamic-update-slice_fusion.h0_ref), channel_id=1, source_target_pairs={{0,16},{4,20},{8,24},{12,28},{16,32},{20,36},{24,40},{28,44},{32,4... | collective-permute-start | bytes 3145736 | tf_op jit(solution)/shard_map/ppermute | solution.py:294
  78.2 24.6 %copy-start.1 = (bf16[8,512,128]{2,1,0:T(8,128)(2,1)}, bf16[8,512,128]{2,1,0:T(8,128)(2,1)S(1)}, u32[]{:S(2)}) copy-start(bf16[8,512,128]{2,1,0:T(8,128)(2,1)S(1)} %collective-permute-done.7.back_k_ref) | copy-start | bytes 3145732
  78.2 24.6 %collective-permute-start.11 = (bf16[8,2,256,128]{3,2,1,0:T(8,128)(2,1)S(1)}, bf16[8,2,256,128]{3,2,1,0:T(8,128)(2,1)}, u32[]{:S(2)}, u32[]{:S(2)}) collective-permute-start(bf16[8,2,256,128]{3,2,1,0:T(8,128)(2,1)S(1)} %collective-permute-done.6.h1_ref), channel_id=1, source_target_pairs={{0,48},{4,52},{8,56},{12,60},{16,0},{20,4},{24,8},{28,12},{32,16},... | collective-permute-start | bytes 3145736 | tf_op jit(solution)/shard_map/ppermute | solution.py:294
  131.2 27.1 %copy-start.12 = (bf16[512,512]{1,0:T(8,128)(2,1)S(1)}, bf16[512,512]{1,0:T(8,128)(2,1)}, u32[]{:S(2)}) copy-start(bf16[512,512]{1,0:T(8,128)(2,1)} %get-tuple-element.55) | copy-start | bytes 1572868
  131.2 28.1 %copy-start.13 = (bf16[512,512]{1,0:T(8,128)(2,1)S(1)}, bf16[512,512]{1,0:T(8,128)(2,1)}, u32[]{:S(2)}) copy-start(bf16[512,512]{1,0:T(8,128)(2,1)} %get-tuple-element.65) | copy-start | bytes 1572868
  131.2 28.9 %copy-start.11 = (bf16[512,512]{1,0:T(8,128)(2,1)S(1)}, bf16[512,512]{1,0:T(8,128)(2,1)}, u32[]{:S(2)}) copy-start(bf16[512,512]{1,0:T(8,128)(2,1)} %get-tuple-element.66) | copy-start | bytes 1572868
  131.2 29.8 %copy-start.10 = (bf16[512,512]{1,0:T(8,128)(2,1)S(1)}, bf16[512,512]{1,0:T(8,128)(2,1)}, u32[]{:S(2)}) copy-start(bf16[512,512]{1,0:T(8,128)(2,1)} %get-tuple-element.59) | copy-start | bytes 1572868
  157.0 48.6 %collective-permute-start.12 = (bf16[512,1024]{1,0:T(8,128)(2,1)}, bf16[512,1024]{1,0:T(8,128)(2,1)S(1)}, u32[]{:S(2)}, u32[]{:S(2)}) collective-permute-start(bf16[512,1024]{1,0:T(8,128)(2,1)} %get-tuple-element.64), channel_id=1, source_target_pairs={{0,1},{1,0},{2,3},{3,2},{4,5},{5,4},{6,7},{7,6},{8,9},{9,8},{10,11... | collective-permute-start | bytes 3145736 | tf_op jit(solution)/shard_map/ppermute | solution.py:276
  158.4 25.7 %collective-permute-start.13 = (bf16[512,512]{1,0:T(8,128)(2,1)S(1)}, bf16[512,512]{1,0:T(8,128)(2,1)S(1)}, u32[]{:S(2)}, u32[]{:S(2)}) collective-permute-start(bf16[512,512]{1,0:T(8,128)(2,1)S(1)} %copy-done.12), channel_id=1, source_target_pairs={{0,2},{1,3},{2,0},{3,1},{4,6},{5,7},{6,4},{7,5},{8,10},{9,11},{10,... | collective-permute-start | bytes 1572872 | tf_op jit(solution)/shard_map/ppermute | solution.py:276
  159.3 24.7 %collective-permute-start.14 = (bf16[512,512]{1,0:T(8,128)(2,1)S(1)}, bf16[512,512]{1,0:T(8,128)(2,1)S(1)}, u32[]{:S(2)}, u32[]{:S(2)}) collective-permute-start(bf16[512,512]{1,0:T(8,128)(2,1)S(1)} %copy-done.13), channel_id=1, source_target_pairs={{0,3},{1,2},{2,1},{3,0},{4,7},{5,6},{6,5},{7,4},{8,11},{9,10},{10,... | collective-permute-start | bytes 1572872 | tf_op jit(solution)/shard_map/ppermute | solution.py:276
  160.1 34.9 %collective-permute-start.16 = (bf16[512,512]{1,0:T(8,128)(2,1)S(1)}, bf16[512,512]{1,0:T(8,128)(2,1)S(1)}, u32[]{:S(2)}, u32[]{:S(2)}) collective-permute-start(bf16[512,512]{1,0:T(8,128)(2,1)S(1)} %copy-done.11), channel_id=1, source_target_pairs={{0,3},{1,2},{2,1},{3,0},{4,7},{5,6},{6,5},{7,4},{8,11},{9,10},{10,... | collective-permute-start | bytes 1572872 | tf_op jit(solution)/shard_map/ppermute | solution.py:276
  161.0 44.5 %collective-permute-start.15 = (bf16[512,512]{1,0:T(8,128)(2,1)S(1)}, bf16[512,512]{1,0:T(8,128)(2,1)S(1)}, u32[]{:S(2)}, u32[]{:S(2)}) collective-permute-start(bf16[512,512]{1,0:T(8,128)(2,1)S(1)} %copy-done.10), channel_id=1, source_target_pairs={{0,2},{1,3},{2,0},{3,1},{4,6},{5,7},{6,4},{7,5},{8,10},{9,11},{10,... | collective-permute-start | bytes 1572872 | tf_op jit(solution)/shard_map/ppermute | solution.py:276
  (7 other events, 81.0 us)
